TPU v7x, 32 devices: a whole 2x2x4 slice. The times are simulated.
32 devices in a mesh: fgrp: 8 (over z, x), tile: 2 (over core), pol: 2 (over y).
Axes of the slice: x: 2, y: 2, z: 4, core: 2. Of those that a mesh axis runs over, the one named last changes fastest.
Arguments:
- voltages: bfloat16 [2, 2048, 131072], P(None, ('tile', 'pol'), 'fgrp'), may hold values from -4 to 4
- gains: float32 [2, 2048, 64], P(None, ('tile', 'pol')), may hold values from -4 to 4
Outputs:
- visibilities: float32 [64, 2, 2048, 2048], P('fgrp', None, ('tile', 'pol'))
All inputs are finite; a program needn't handle non-finite values.
Results may differ from a plain program's by a relative error of at most 0.0039.
Values may be sent and summed in bfloat16 or wider, within the bound.
No kernel may reach another device: no remote copies, remote signals or barrier semaphores. Data moves between devices by JAX's collectives and lax.ppermute only.
A program may use at most 256 MiB of HBM per device.

v0:
```python
import functools
import math

import jax
import jax.numpy as jnp
import ml_dtypes
import numpy as np
from jax import lax
from jax.experimental import pallas as pl
from jax.experimental.pallas import tpu as pltpu
from jax.sharding import PartitionSpec as P

NFFT = 4096
TAPS = 4
VMEM = 56 * 2**20


def filter_taps():
    span = TAPS * NFFT
    position = np.arange(span, dtype=np.float64)
    centred = (position - span / 2 + 0.5) / NFFT
    window = 0.5 - 0.5 * np.cos(2.0 * np.pi * (position + 0.5) / span)
    return (np.sinc(centred) * window).reshape(TAPS, NFFT)


def low_taps():
    energy = (filter_taps() ** 2).sum(axis=1)
    return [t for t in range(TAPS) if energy[t] > 0.01 * energy.sum()]


def filter_table(channels):
    phases = np.arange(NFFT)[:, None] * np.arange(channels)[None, :] % NFFT
    angles = phases * (2.0 * np.pi / NFFT)
    transform = np.concatenate([np.cos(angles), np.sin(angles)], axis=1) / math.sqrt(NFFT)
    blocks = [tap[:, None] * transform for tap in filter_taps()]
    high = [b.astype(np.float32).astype(ml_dtypes.bfloat16) for b in blocks]
    low = [
        (blocks[t] - high[t].astype(np.float64)).astype(np.float32).astype(ml_dtypes.bfloat16)
        for t in low_taps()
    ]
    return np.ascontiguousarray(np.concatenate(high + low, axis=1).T)


def filter_kernel(volt_ref, table_ref, gain_ref, out_ref, sums):
    frame, part = pl.program_id(0), pl.program_id(1)
    width, rows = sums.shape[2], sums.shape[3]
    half = width // 2
    slots = sums.shape[0]

    @pl.when((frame == 0) & (part == 0))
    def _():
        sums[...] = jnp.zeros_like(sums)

    product = lax.dot_general(
        table_ref[...],
        volt_ref[0],
        (((1,), (1,)), ((), ())),
        preferred_element_type=jnp.float32,
    )
    low = low_taps()
    for tap in range(TAPS):
        term = product[tap * width : (tap + 1) * width]
        if tap in low:
            at = (TAPS + low.index(tap)) * width
            term = term + product[at : at + width]
        sums[frame + TAPS - 1 - tap, part] += term

    @pl.when((frame == pl.num_programs(0) - 1) & (part == 1))
    def _():
        owners = out_ref.shape[0]
        share = half // owners
        for slot in range(slots):
            real = sums[slot, 0, :half] + sums[slot, 1, half:]
            imag = sums[slot, 1, :half] - sums[slot, 0, half:]
            out_real = gain_ref[0] * real - gain_ref[1] * imag
            out_imag = gain_ref[0] * imag + gain_ref[1] * real
            for owner in range(owners):
                at = owner * share
                both = jnp.concatenate(
                    [out_real[at : at + share], out_imag[at : at + share]], axis=0
                )
                out_ref[owner, 2 * share * slot : 2 * share * (slot + 1), :] = both.astype(
                    jnp.bfloat16
                )


def filter_all(voltages, table, gains, owners):
    rows = voltages.shape[1]
    frames = voltages.shape[2] // NFFT
    half = gains.shape[1]
    slots = frames + TAPS - 1
    out_rows = slots * 2 * half // owners
    columns = table.shape[0]
    return pl.pallas_call(
        filter_kernel,
        grid=(frames, 2),
        in_specs=[
            pl.BlockSpec((1, rows, NFFT), lambda f, c: (c, 0, f)),
            pl.BlockSpec((columns, NFFT), lambda f, c: (0, 0)),
            pl.BlockSpec((2, half, rows), lambda f, c: (0, 0, 0)),
        ],
        out_specs=pl.BlockSpec((owners, out_rows, rows), lambda f, c: (0, 0, 0)),
        out_shape=jax.ShapeDtypeStruct((owners, out_rows, rows), jnp.bfloat16),
        scratch_shapes=[pltpu.VMEM((slots, 2, 2 * half, rows), jnp.float32)],
        compiler_params=pltpu.CompilerParams(vmem_limit_bytes=VMEM),
        cost_estimate=pl.CostEstimate(
            flops=2 * 2 * rows * frames * NFFT * columns,
            bytes_accessed=2 * (2 * rows * frames * NFFT + NFFT * columns),
            transcendentals=0,
        ),
        name="filter_all",
    )(voltages, table, gains)


def merge_kernel(frames, share, in_ref, out_ref, scratch):
    owners = in_ref.shape[0]
    depth = 2 * owners * frames
    blocks = scratch.shape[0]
    for group in range(owners):
        for frame in range(frames):
            at = 2 * share * frame
            value = in_ref[group, at : at + 2 * share, :].astype(jnp.float32)
            if group > 0 and frame < TAPS - 1:
                at = 2 * share * (frame + frames)
                value = value + in_ref[group - 1, at : at + 2 * share, :].astype(jnp.float32)
            if value.shape[1] < 128 * blocks:
                spare = jnp.zeros((2 * share, 128 * blocks - value.shape[1]), jnp.float32)
                value = jnp.concatenate([value, spare], axis=1)
            for part in range(2):
                row = (part * owners + group) * frames + frame
                for block in range(blocks):
                    scratch[block, pl.ds(row, share, stride=depth), :] = value[
                        part * share : (part + 1) * share, block * 128 : (block + 1) * 128
                    ]
    for block in range(blocks):
        lanes = min(128, out_ref.shape[1] - block * 128)
        out_ref[:, block * 128 : block * 128 + lanes] = scratch[block, :, :lanes].astype(
            jnp.bfloat16
        )


def merge(turned, frames, share):
    owners, _, rows = turned.shape
    out_rows = share * 2 * owners * frames
    return pl.pallas_call(
        functools.partial(merge_kernel, frames, share),
        out_shape=jax.ShapeDtypeStruct((out_rows, rows), jnp.bfloat16),
        scratch_shapes=[pltpu.VMEM((pl.cdiv(rows, 128), out_rows, 128), jnp.float32)],
        compiler_params=pltpu.CompilerParams(vmem_limit_bytes=VMEM),
        name="merge",
    )(turned)


def visibility(left, right, norm):
    half = left.shape[0] // 2
    swapped = jnp.concatenate([left[half:], -left[:half]], axis=0)
    return norm * lax.dot_general(
        jnp.concatenate([left, swapped], axis=1),
        right,
        (((0,), (0,)), ((), ())),
        preferred_element_type=jnp.float32,
    )


def correlate_kernel(norm, own_ref, all_ref, out_ref):
    rows = own_ref.shape[1]
    for group in range(all_ref.shape[0]):
        product = visibility(own_ref[...], all_ref[group], norm)
        out_ref[0, 0, :, group * rows : (group + 1) * rows] = product[:rows]
        out_ref[0, 1, :, group * rows : (group + 1) * rows] = product[rows:]


def correlate(own, gathered, share, norm):
    out_rows, rows = own.shape
    depth = out_rows // share
    groups = gathered.shape[0]
    return pl.pallas_call(
        functools.partial(correlate_kernel, norm),
        grid=(share,),
        in_specs=[
            pl.BlockSpec((depth, rows), lambda c: (c, 0)),
            pl.BlockSpec((groups, depth, rows), lambda c: (0, c, 0)),
        ],
        out_specs=pl.BlockSpec((1, 2, rows, groups * rows), lambda c: (c, 0, 0, 0)),
        out_shape=jax.ShapeDtypeStruct((share, 2, rows, groups * rows), jnp.float32),
        compiler_params=pltpu.CompilerParams(vmem_limit_bytes=VMEM),
        name="correlate",
    )(own, gathered)


def block_kernel(norm, place_ref, own_ref, other_ref, *refs):
    out_ref = refs[-1]
    rows = own_ref.shape[1]
    product = visibility(own_ref[...], other_ref[...], norm)
    out_ref[0, 0] = product[:rows]
    out_ref[0, 1] = product[rows:]


def correlate_block(own, other, place, total, result, share, norm):
    out_rows, rows = own.shape
    depth = out_rows // share
    specs = [pl.BlockSpec((depth, rows), lambda c, place: (c, 0))] * 2
    operands = [place, own, other]
    aliases = {}
    if result is not None:
        aliases = {len(operands): 0}
        operands.append(result)
        specs.append(pl.BlockSpec(memory_space=pl.ANY))
    return pl.pallas_call(
        functools.partial(block_kernel, norm),
        grid_spec=pltpu.PrefetchScalarGridSpec(
            num_scalar_prefetch=1,
            grid=(share,),
            in_specs=specs,
            out_specs=pl.BlockSpec((1, 2, rows, rows), lambda c, place: (c, 0, 0, place[0])),
        ),
        out_shape=jax.ShapeDtypeStruct((share, 2, rows, total), jnp.float32),
        input_output_aliases=aliases,
        compiler_params=pltpu.CompilerParams(vmem_limit_bytes=VMEM),
        cost_estimate=pl.CostEstimate(
            flops=4 * share * rows * rows * depth,
            bytes_accessed=4 * share * 2 * rows * rows,
            transcendentals=0,
        ),
        name="correlate_block",
    )(*operands)


def cycled(shard, axis, by):
    length = lax.axis_size(axis)
    if by == 0:
        return shard
    return lax.ppermute(shard, axis, [(i, (i + by) % length) for i in range(length)])


def body(voltages, gains):
    inputs_here = voltages.shape[1]
    frames_here = voltages.shape[2] // NFFT
    channels = gains.shape[2]
    owners = lax.axis_size("fgrp")
    share = channels // owners
    norm = 1.0 / math.sqrt(frames_here * owners)
    table = jnp.asarray(filter_table(channels))
    partial = filter_all(voltages, table, jnp.swapaxes(gains, 1, 2), owners)
    turned = lax.all_to_all(partial, "fgrp", split_axis=0, concat_axis=0, tiled=True)
    own = merge(turned, frames_here, share)
    tiles, pols = lax.axis_size("tile"), lax.axis_size("pol")
    if inputs_here % 128:
        wide = lax.all_gather(lax.all_gather(own, "pol", axis=0), "tile", axis=0)
        return correlate(own, wide.reshape((-1,) + own.shape), share, norm)
    tile, pol = lax.axis_index("tile"), lax.axis_index("pol")
    result = None
    for by_pol in range(pols):
        near = cycled(own, "pol", by_pol)
        if by_pol:
            near, result = lax.optimization_barrier((near, result))
        for by_tile in range(tiles):
            other = cycled(near, "tile", by_tile)
            place = (tile - by_tile) % tiles * pols + (pol - by_pol) % pols
            result = correlate_block(
                own,
                other,
                place.astype(jnp.int32).reshape(1),
                tiles * pols * inputs_here,
                result,
                share,
                norm,
            )
    return result


def solution(mesh):
    placed = (P(None, ("tile", "pol"), "fgrp"), P(None, ("tile", "pol"), None))
    return jax.shard_map(
        body,
        mesh=mesh,
        in_specs=placed,
        out_specs=P("fgrp", None, ("tile", "pol"), None),
        check_vma=False,
    )
```

profile of v0, /device:TPU:0, one launch (start us, length us, event | category | flops | bytes accessed | tf_op | source)
XLA Modules:
  0.0 107.1 jit_solution(14039625919315992060)
XLA Ops:
  0.0 33.3 %filter_all.1 = bf16[8,112,512]{2,1,0:T(8,128)(2,1)} custom-call(bf16[2,512,16384]{2,1,0:T(8,128)(2,1)} %volt_ref.1, bf16[768,4096]{1,0:T(8,128)(2,1)} %constant.45.clone.table_ref, f32[2,64,512]{2,1,0:T(8,128)} %bitcast.5), custom_call_target="tpu_custom_call" | custom-call | flops 25769803776 | bytes 39845888 | tf_op jit(solution)/shard_map/filter_all/pallas_call | solution.py:94
  33.3 30.7 %all_to_all.5.in_ref = bf16[8,112,512]{2,1,0:T(8,128)(2,1)} all-to-all(bf16[8,112,512]{2,1,0:T(8,128)(2,1)} %filter_all.1), channel_id=1, replica_groups=mesh['fgrp'=8,'tile'=2,'pol'=2] {'fgrp'}, dimensions={0} | all-to-all | bytes 1835008 | tf_op jit(solution)/shard_map/all_to_all | solution.py:245
  64.0 3.1 %merge.1.own_ref.other_ref = bf16[512,512]{1,0:T(8,128)(2,1)} custom-call(bf16[8,112,512]{2,1,0:T(8,128)(2,1)} %all_to_all.5.in_ref), custom_call_target="tpu_custom_call" | custom-call | tf_op jit(solution)/shard_map/merge/pallas_call | solution.py:145
  67.1 0.0 collective-permute-start.1
  67.1 1.5 %collective-permute-start = (bf16[512,512]{1,0:T(8,128)(2,1)}, bf16[512,512]{1,0:T(8,128)(2,1)S(1)}, u32[]{:S(2)}, u32[]{:S(2)}) collective-permute-start(bf16[512,512]{1,0:T(8,128)(2,1)} %merge.1.own_ref.other_ref), channel_id=1, source_target_pairs={{0,1},{1,0},{2,3},{3,2},{4,5},{5,4},{6,7},{7,6},{8,9},{9,8},{10,11... | collective-permute-start | bytes 1572872 | tf_op jit(solution)/shard_map/ppermute | solution.py:233
  68.6 9.0 %correlate_block.4.refs_0_ = f32[8,2,512,2048]{3,2,1,0:T(8,128)} custom-call(s32[1]{0:T(128)} %bitcast.3.place_ref, bf16[512,512]{1,0:T(8,128)(2,1)} %merge.1.own_ref.other_ref, bf16[512,512]{1,0:T(8,128)(2,1)} %merge.1.own_ref.other_ref), custom_call_target="tpu_custom_call" | custom-call | flops 536870912 | bytes 16777216 | tf_op jit(solution)/shard_map/correlate_block/pallas_call | solution.py:209
  77.7 0.0 collective-permute-done.1.other_ref
  77.7 0.0 copy-start.1
  77.7 0.8 copy-done.1
  78.5 9.0 %correlate_block.5.refs_0_ = f32[8,2,512,2048]{3,2,1,0:T(8,128)} custom-call(s32[1]{0:T(128)} %bitcast.2.place_ref, bf16[512,512]{1,0:T(8,128)(2,1)} %merge.1.own_ref.other_ref, bf16[512,512]{1,0:T(8,128)(2,1)} %copy-done.1, f32[8,2,512,2048]{3,2,1,0:T(8,128)} %correlate_block.4.refs_0_), custom_call_target="tpu_custom_call", output_to_operand_aliasing={{}: (3, {})} | custom-call | flops 536870912 | bytes 16777216 | tf_op jit(solution)/shard_map/correlate_block/pallas_call | solution.py:209
  87.5 0.0 collective-permute-done.other_ref
  87.5 0.0 copy-start
  87.5 0.3 collective-permute-start.2
  87.8 0.5 copy-done
  88.3 9.0 %correlate_block.6.refs_0_ = f32[8,2,512,2048]{3,2,1,0:T(8,128)} custom-call(s32[1]{0:T(128)} %bitcast.4.place_ref, bf16[512,512]{1,0:T(8,128)(2,1)} %merge.1.own_ref.other_ref, bf16[512,512]{1,0:T(8,128)(2,1)} %copy-done, f32[8,2,512,2048]{3,2,1,0:T(8,128)} %correlate_block.5.refs_0_), custom_call_target="tpu_custom_call", output_to_operand_aliasing={{}: (3, {})} | custom-call | flops 536870912 | bytes 16777216 | tf_op jit(solution)/shard_map/correlate_block/pallas_call | solution.py:209
  97.3 0.0 collective-permute-done.2.other_ref
  97.3 0.0 copy-start.2
  97.3 0.8 copy-done.2
  98.1 9.0 %correlate_block.7 = f32[8,2,512,2048]{3,2,1,0:T(8,128)} custom-call(s32[1]{0:T(128)} %bitcast.place_ref, bf16[512,512]{1,0:T(8,128)(2,1)} %merge.1.own_ref.other_ref, bf16[512,512]{1,0:T(8,128)(2,1)} %copy-done.2, f32[8,2,512,2048]{3,2,1,0:T(8,128)} %correlate_block.6.refs_0_), custom_call_target="tpu_custom_call", output_to_operand_aliasing={{}: (3, {})} | custom-call | flops 536870912 | bytes 16777216 | tf_op jit(solution)/shard_map/correlate_block/pallas_call | solution.py:209
Async XLA Ops:
  67.1 10.6 %collective-permute-start.1 = (bf16[512,512]{1,0:T(8,128)(2,1)}, bf16[512,512]{1,0:T(8,128)(2,1)S(1)}, u32[]{:S(2)}, u32[]{:S(2)}) collective-permute-start(bf16[512,512]{1,0:T(8,128)(2,1)} %merge.1.own_ref.other_ref), channel_id=1, source_target_pairs={{0,2},{2,0},{1,3},{3,1},{4,6},{6,4},{5,7},{7,5},{8,10},{10,8},{9,1... | collective-permute-start | bytes 1572872 | tf_op jit(solution)/shard_map/ppermute | solution.py:233
  67.1 20.4 %collective-permute-start = (bf16[512,512]{1,0:T(8,128)(2,1)}, bf16[512,512]{1,0:T(8,128)(2,1)S(1)}, u32[]{:S(2)}, u32[]{:S(2)}) collective-permute-start(bf16[512,512]{1,0:T(8,128)(2,1)} %merge.1.own_ref.other_ref), channel_id=1, source_target_pairs={{0,1},{1,0},{2,3},{3,2},{4,5},{5,4},{6,7},{7,6},{8,9},{9,8},{10,11... | collective-permute-start | bytes 1572872 | tf_op jit(solution)/shard_map/ppermute | solution.py:233
  77.7 0.8 copy-start.1
  87.5 0.8 copy-start
  87.5 9.8 %collective-permute-start.2 = (bf16[512,512]{1,0:T(8,128)(2,1)S(1)}, bf16[512,512]{1,0:T(8,128)(2,1)S(1)}, u32[]{:S(2)}, u32[]{:S(2)}) collective-permute-start(bf16[512,512]{1,0:T(8,128)(2,1)S(1)} %collective-permute-done.other_ref), channel_id=1, source_target_pairs={{0,2},{2,0},{1,3},{3,1},{4,6},{6,4},{5,7},{7,5},{8,10},{10,8},{9,1... | collective-permute-start | bytes 1572872 | tf_op jit(solution)/shard_map/ppermute | solution.py:233
  97.3 0.8 copy-start.2
where the time goes:
time: 109 us; the launch traced here: 107 us
  Pallas kernels  72.5 us (67%)
  blocking collectives  30.7 us (28%)
  local copies, waits for them, and re-layouts  2.07 us (2%)
  starting transfers between devices  1.81 us (2%)
    pallas_call x4, Pallas kernels, correlate_block(): pl.pallas_call(functools.partial(block_kernel, norm), grid_spec=pltpu.Pre...  36.1 us
    pallas_call x1, Pallas kernels, filter_all(): pl.pallas_call(filter_kernel, grid=(frames, 2), in_specs=[pl.BlockSpec((1...  33.3 us
    all_to_all x1, blocking collectives, body(): lax.all_to_all(partial, 'fgrp', split_axis=0, concat_axis=0, tiled=True)  30.7 us
    pallas_call x1, Pallas kernels, merge(): pl.pallas_call(functools.partial(merge_kernel, frames, share), out_shape=...  3.11 us
  transfers between devices with their start and end apart: 3, of which 0 were waited for; matrix products, arithmetic and copies ran while one was open for 0% of the time, Pallas kernels for 25%

commit v1 on v0

v1 whole, which is shorter than its diff:
```python
import functools
import math

import jax
import jax.numpy as jnp
import ml_dtypes
import numpy as np
from jax import lax
from jax.experimental import pallas as pl
from jax.experimental.pallas import tpu as pltpu
from jax.sharding import PartitionSpec as P

NFFT = 4096
TAPS = 4
VMEM = 56 * 2**20


def filter_taps():
    span = TAPS * NFFT
    position = np.arange(span, dtype=np.float64)
    centred = (position - span / 2 + 0.5) / NFFT
    window = 0.5 - 0.5 * np.cos(2.0 * np.pi * (position + 0.5) / span)
    return (np.sinc(centred) * window).reshape(TAPS, NFFT)


def low_taps():
    energy = (filter_taps() ** 2).sum(axis=1)
    return [t for t in range(TAPS) if energy[t] > 0.01 * energy.sum()]


def filter_table(channels):
    phases = np.arange(NFFT)[:, None] * np.arange(channels)[None, :] % NFFT
    angles = phases * (2.0 * np.pi / NFFT)
    transform = np.concatenate([np.cos(angles), np.sin(angles)], axis=1) / math.sqrt(NFFT)
    blocks = [tap[:, None] * transform for tap in filter_taps()]
    high = [b.astype(np.float32).astype(ml_dtypes.bfloat16) for b in blocks]
    low = [
        (blocks[t] - high[t].astype(np.float64)).astype(np.float32).astype(ml_dtypes.bfloat16)
        for t in low_taps()
    ]
    return np.ascontiguousarray(np.concatenate(high + low, axis=1).T)


def peer(me, step, length, way):
    if length & (length - 1):
        return (me + way * step) % length
    return me ^ step


def filter_kernel(me_ref, volt_ref, table_hbm, gain_ref, *refs):
    out_refs, (sums, table, arrived) = refs[:-3], refs[-3:]
    frame, part = pl.program_id(0), pl.program_id(1)
    slots, _, width, rows = sums.shape
    half = width // 2
    pieces = arrived.shape[0]
    depth = table.shape[1] // pieces

    def fetch(piece):
        columns = pl.ds(piece * depth, depth)
        return pltpu.make_async_copy(
            table_hbm.at[:, columns], table.at[:, columns], arrived.at[piece]
        )

    def product(start, size):
        return lax.dot_general(
            table[:, start : start + size],
            volt_ref[0, :, start : start + size],
            (((1,), (1,)), ((), ())),
            preferred_element_type=jnp.float32,
        )

    def add(term):
        low = low_taps()
        for tap in range(TAPS):
            value = term[tap * width : (tap + 1) * width]
            if tap in low:
                at = (TAPS + low.index(tap)) * width
                value = value + term[at : at + width]
            sums[frame + TAPS - 1 - tap, part] += value

    first = (frame == 0) & (part == 0)

    @pl.when(first)
    def _():
        for piece in range(pieces):
            fetch(piece).start()
        sums[...] = jnp.zeros_like(sums)
        for piece in range(pieces):
            fetch(piece).wait()
            add(product(piece * depth, depth))

    @pl.when(jnp.logical_not(first))
    def _():
        add(product(0, table.shape[1]))

    @pl.when((frame == pl.num_programs(0) - 1) & (part == 1))
    def _():
        owners = len(out_refs)
        share = half // owners
        for slot in range(slots):
            real = sums[slot, 0, :half] + sums[slot, 1, half:]
            imag = sums[slot, 1, :half] - sums[slot, 0, half:]
            sums[slot, 0, :half] = gain_ref[0] * real - gain_ref[1] * imag
            sums[slot, 1, :half] = gain_ref[0] * imag + gain_ref[1] * real
        for step in range(owners):
            owner = peer(me_ref[0], step, owners, 1)
            mine = pl.ds(pl.multiple_of(owner * share, share), share)
            for slot in range(slots):
                both = jnp.concatenate([sums[slot, 0, mine, :], sums[slot, 1, mine, :]], axis=0)
                at = 2 * share * slot
                out_refs[step][at : at + 2 * share, :] = both.astype(jnp.bfloat16)


def filter_part(me, voltages, table, gains, part, rows, owners):
    frames = voltages.shape[2] // NFFT
    half = gains.shape[1]
    slots = frames + TAPS - 1
    out_rows = slots * 2 * half // owners
    columns = table.shape[0]
    pieces = 4
    return pl.pallas_call(
        filter_kernel,
        grid=(frames, 2),
        in_specs=[
            pl.BlockSpec(memory_space=pltpu.SMEM),
            pl.BlockSpec((1, rows, NFFT), lambda f, c: (c, part, f)),
            pl.BlockSpec(memory_space=pl.ANY),
            pl.BlockSpec((2, half, rows), lambda f, c: (0, 0, part)),
        ],
        out_specs=[pl.BlockSpec((out_rows, rows), lambda f, c: (0, 0))] * owners,
        out_shape=[jax.ShapeDtypeStruct((out_rows, rows), jnp.bfloat16)] * owners,
        scratch_shapes=[
            pltpu.VMEM((slots, 2, 2 * half, rows), jnp.float32),
            pltpu.VMEM((columns, NFFT), jnp.bfloat16),
            pltpu.SemaphoreType.DMA((pieces,)),
        ],
        compiler_params=pltpu.CompilerParams(vmem_limit_bytes=VMEM),
        cost_estimate=pl.CostEstimate(
            flops=2 * 2 * rows * frames * NFFT * columns,
            bytes_accessed=2 * (2 * rows * frames * NFFT + NFFT * columns),
            transcendentals=0,
        ),
        name="filter_part",
    )(me, voltages, table, gains)


def merge_kernel(frames, share, me_ref, *refs):
    in_refs, (out_ref, turned_ref, stacked, scratch) = refs[:-4], refs[-4:]
    owners = len(in_refs)
    depth = 2 * owners * frames
    blocks = scratch.shape[0]
    for step in range(owners):
        stacked[peer(me_ref[0], step, owners, -1)] = in_refs[step][...].astype(jnp.float32)
    for group in range(owners):
        for frame in range(frames):
            at = 2 * share * frame
            value = stacked[group, at : at + 2 * share, :]
            if group > 0 and frame < TAPS - 1:
                at = 2 * share * (frame + frames)
                value = value + stacked[group - 1, at : at + 2 * share, :]
            if value.shape[1] < 128 * blocks:
                spare = jnp.zeros((2 * share, 128 * blocks - value.shape[1]), jnp.float32)
                value = jnp.concatenate([value, spare], axis=1)
            for part in range(2):
                row = (part * owners + group) * frames + frame
                for block in range(blocks):
                    scratch[block, pl.ds(row, share, stride=depth), :] = value[
                        part * share : (part + 1) * share, block * 128 : (block + 1) * 128
                    ]
    for block in range(blocks):
        lanes = min(128, out_ref.shape[1] - block * 128)
        at = block * 128
        out_ref[:, at : at + lanes] = scratch[block, :, :lanes].astype(jnp.bfloat16)
        turned_ref[at : at + lanes, :] = scratch[block].T[:lanes].astype(jnp.bfloat16)


def merge(me, received, frames, share):
    owners = len(received)
    in_rows, rows = received[0].shape
    out_rows = share * 2 * owners * frames
    return pl.pallas_call(
        functools.partial(merge_kernel, frames, share),
        in_specs=[pl.BlockSpec(memory_space=pltpu.SMEM)]
        + [pl.BlockSpec(memory_space=pltpu.VMEM)] * owners,
        out_shape=[
            jax.ShapeDtypeStruct((out_rows, rows), jnp.bfloat16),
            jax.ShapeDtypeStruct((rows, out_rows), jnp.bfloat16),
        ],
        scratch_shapes=[
            pltpu.VMEM((owners, in_rows, rows), jnp.float32),
            pltpu.VMEM((pl.cdiv(rows, 128), out_rows, 128), jnp.float32),
        ],
        compiler_params=pltpu.CompilerParams(vmem_limit_bytes=16 * 2**20),
        name="merge",
    )(me, *received)


def block_kernel(norm, parts, blocks, place_ref, *refs):
    left_refs, right_refs, out_ref = refs[:parts], refs[parts : parts * (1 + blocks)], refs[-1]
    rows = left_refs[0].shape[0]
    depth = right_refs[0].shape[0]
    odd = lax.rem(pl.program_id(0), 2) == 1
    for block in range(blocks):

        @pl.when(pl.program_id(1) == block)
        def _():
            for other in range(parts):
                right = right_refs[block * parts + other][...]
                crossed = jnp.concatenate([-right[depth // 2 :], right[: depth // 2]], axis=0)
                for kind, value in enumerate((right, crossed)):
                    none = jnp.zeros_like(value)
                    wide = jnp.concatenate(
                        [jnp.where(odd, none, value), jnp.where(odd, value, none)], axis=0
                    )
                    for part in range(parts):
                        out_ref[
                            0,
                            kind,
                            part * rows : (part + 1) * rows,
                            other * rows : (other + 1) * rows,
                        ] = norm * jnp.dot(
                            left_refs[part][...], wide, preferred_element_type=jnp.float32
                        )


def correlate(left, rights, places, total, result, share, norm):
    parts, blocks = len(left), len(rights)
    rows, out_rows = left[0].shape
    depth = out_rows // share
    width = parts * rows
    operands = [places, *left, *(shard for right in rights for shard in right)]
    specs = [pl.BlockSpec((rows, 2 * depth), lambda c, b, places: (0, c // 2))] * parts
    specs += [pl.BlockSpec((depth, rows), lambda c, b, places: (c, 0))] * (blocks * parts)
    aliases = {}
    if result is not None:
        aliases = {len(operands): 0}
        operands.append(result)
        specs.append(pl.BlockSpec(memory_space=pl.ANY))
    return pl.pallas_call(
        functools.partial(block_kernel, norm, parts, blocks),
        grid_spec=pltpu.PrefetchScalarGridSpec(
            num_scalar_prefetch=1,
            grid=(share, blocks),
            in_specs=specs,
            out_specs=pl.BlockSpec((1, 2, width, width), lambda c, b, places: (c, 0, 0, places[b])),
        ),
        out_shape=jax.ShapeDtypeStruct((share, 2, width, total), jnp.float32),
        input_output_aliases=aliases,
        compiler_params=pltpu.CompilerParams(vmem_limit_bytes=24 * 2**20),
        cost_estimate=pl.CostEstimate(
            flops=4 * share * blocks * width * width * depth,
            bytes_accessed=4 * share * 2 * blocks * width * width,
            transcendentals=0,
        ),
        name="correlate",
    )(*operands)


def whole_kernel(norm, left_ref, all_ref, out_ref):
    rows = left_ref.shape[0]
    depth = all_ref.shape[1]
    odd = lax.rem(pl.program_id(0), 2) == 1
    for group in range(all_ref.shape[0]):
        right = all_ref[group]
        crossed = jnp.concatenate([-right[depth // 2 :], right[: depth // 2]], axis=0)
        for kind, value in enumerate((right, crossed)):
            none = jnp.zeros_like(value)
            wide = jnp.concatenate(
                [jnp.where(odd, none, value), jnp.where(odd, value, none)], axis=0
            )
            out_ref[0, kind, :, group * rows : (group + 1) * rows] = norm * jnp.dot(
                left_ref[...], wide, preferred_element_type=jnp.float32
            )


def correlate_whole(left, gathered, share, norm):
    rows, out_rows = left.shape
    depth = out_rows // share
    groups = gathered.shape[0]
    return pl.pallas_call(
        functools.partial(whole_kernel, norm),
        grid=(share,),
        in_specs=[
            pl.BlockSpec((rows, 2 * depth), lambda c: (0, c // 2)),
            pl.BlockSpec((groups, depth, rows), lambda c: (0, c, 0)),
        ],
        out_specs=pl.BlockSpec((1, 2, rows, groups * rows), lambda c: (c, 0, 0, 0)),
        out_shape=jax.ShapeDtypeStruct((share, 2, rows, groups * rows), jnp.float32),
        compiler_params=pltpu.CompilerParams(vmem_limit_bytes=24 * 2**20),
        name="correlate_whole",
    )(left, gathered)


def swapped(shard, axis, step):
    if step == 0:
        return shard
    length = lax.axis_size(axis)
    return lax.ppermute(shard, axis, [(i, peer(i, step, length, 1)) for i in range(length)])


def body(voltages, gains):
    inputs_here = voltages.shape[1]
    frames_here = voltages.shape[2] // NFFT
    channels = gains.shape[2]
    owners = lax.axis_size("fgrp")
    share = channels // owners
    rows = 256 if inputs_here % 256 == 0 else inputs_here
    parts = inputs_here // rows
    norm = 1.0 / math.sqrt(frames_here * owners)
    table = jnp.asarray(filter_table(channels))
    by_channel = jnp.swapaxes(gains, 1, 2)
    me = lax.axis_index("fgrp").astype(jnp.int32).reshape(1)
    own, left = [], []
    blocks = filter_part(me, voltages, table, by_channel, 0, rows, owners)
    for part in range(parts):
        received = [swapped(block, "fgrp", step) for step, block in enumerate(blocks)]
        if part + 1 < parts:
            blocks = filter_part(me, voltages, table, by_channel, part + 1, rows, owners)
            received, blocks = lax.optimization_barrier((received, blocks))
        merged, turned = merge(me, received, frames_here, share)
        own.append(merged)
        left.append(turned)
    tiles, pols = lax.axis_size("tile"), lax.axis_size("pol")
    if inputs_here % 128:
        wide = lax.all_gather(lax.all_gather(own[0], "pol", axis=0), "tile", axis=0)
        return correlate_whole(left[0], wide.reshape((-1,) + own[0].shape), share, norm)
    tile, pol = lax.axis_index("tile"), lax.axis_index("pol")

    def place(by_tile, by_pol):
        return (peer(tile, by_tile, tiles, -1) * pols + peer(pol, by_pol, pols, -1)).astype(jnp.int32)

    total = tiles * pols * inputs_here
    far = [[swapped(shard, "pol", by_pol) for shard in own] for by_pol in range(1, pols)]
    result = correlate(left, [own], place(0, 0).reshape(1), total, None, share, norm)
    far, result = lax.optimization_barrier((far, result))
    for by_pol in range(pols):
        near = own if by_pol == 0 else far[by_pol - 1]
        rights = [
            [swapped(shard, "tile", by_tile) for shard in near] for by_tile in range(tiles)
        ]
        steps = range(1 if by_pol == 0 else 0, tiles)
        result = correlate(
            left,
            [rights[step] for step in steps],
            jnp.stack([place(step, by_pol) for step in steps]),
            total,
            result,
            share,
            norm,
        )
    return result


def solution(mesh):
    placed = (P(None, ("tile", "pol"), "fgrp"), P(None, ("tile", "pol"), None))
    return jax.shard_map(
        body,
        mesh=mesh,
        in_specs=placed,
        out_specs=P("fgrp", None, ("tile", "pol"), None),
        check_vma=False,
    )
```

time: 109 us -> 108 us (level); the launches traced: 107 us -> 108 us
  blocking collectives: 30.7 us -> 0 us
  starting transfers between devices: 1.81 us -> 28 us
  waiting for transfers between devices: 0.01 us -> 4 us
  Pallas kernels: 72.5 us -> 74.1 us
    all_to_all x1 -> x0, blocking collectives: 30.7 us -> none  [body(): lax.all_to_all(partial, 'fgrp', split_axis=0, concat_axis=0, tiled=True)]
    ppermute x3 -> x20, starting transfers between devices: 1.81 us -> 28 us  [swapped(): lax.ppermute(shard, axis, [(i, peer(i, step, length, 1)) for i in range(l...]
    ppermute x3 -> x20, waiting for transfers between devices: 0.01 us -> 4 us  [swapped(): lax.ppermute(shard, axis, [(i, peer(i, step, length, 1)) for i in range(l...]
    pallas_call x6 -> x7, Pallas kernels: 72.5 us -> 74.1 us  [the longest x2 42.2 us: filter_part(): pl.pallas_call(filter_kernel, grid=(frames, 2), in_specs=[pl.BlockSpec(me...]
  transfers between devices with their start and end apart: 3 -> 20, of which waited for: 0 -> 1; matrix products, arithmetic and copies ran while one was open for 0% -> 0% of each run, Pallas kernels for 25% -> 35%
where the time goes in v1:
time: 108 us
  Pallas kernels  74.1 us (69%)
  starting transfers between devices  28 us (26%)
  waiting for transfers between devices  4 us (4%)
  local copies, waits for them, and re-layouts  1.64 us (2%)
    pallas_call x2, Pallas kernels, filter_part(): pl.pallas_call(filter_kernel, grid=(frames, 2), in_specs=[pl.BlockSpec(me...  42.2 us
    pallas_call x3, Pallas kernels, correlate(): pl.pallas_call(functools.partial(block_kernel, norm, parts, blocks), grid...  30.9 us
    ppermute x20, starting transfers between devices, swapped(): lax.ppermute(shard, axis, [(i, peer(i, step, length, 1)) for i in range(l...  28 us
    ppermute x20, waiting for transfers between devices, swapped(): lax.ppermute(shard, axis, [(i, peer(i, step, length, 1)) for i in range(l...  4 us
  transfers between devices with their start and end apart: 20, of which 1 were waited for; matrix products, arithmetic and copies ran while one was open for 0% of the time, Pallas kernels for 35%

profile of v1, /device:TPU:0, one launch (start us, length us, event | category | flops | bytes accessed | tf_op | source)
XLA Modules:
  0.0 108.0 jit_solution(7529637654417918329)
XLA Ops:
  0.0 21.1 %filter_part.2 = (bf16[112,256]{1,0:T(8,128)(2,1)}, bf16[112,256]{1,0:T(8,128)(2,1)}, bf16[112,256]{1,0:T(8,128)(2,1)}, bf16[112,256]{1,0:T(8,128)(2,1)}, bf16[1...) custom-call(s32[1]{0:T(128)} %bitcast.2.me_ref, ...), custom_call_target="tpu_custom_call" | custom-call | flops 12884901888 | bytes 23068672 | tf_op jit(solution)/shard_map/filter_part/pallas_call | solution.py:121
  21.1 3.0 %collective-permute-start = (bf16[112,256]{1,0:T(8,128)(2,1)}, bf16[112,256]{1,0:T(8,128)(2,1)S(1)}, u32[]{:S(2)}, u32[]{:S(2)}) collective-permute-start(bf16[112,256]{1,0:T(8,128)(2,1)} %get-tuple-element.45), channel_id=1, source_target_pairs={{0,4},{4,0},{8,12},{12,8},{16,20},{20,16},{24,28},{28,24},{1,5},{5... | collective-permute-start | bytes 172040 | tf_op jit(solution)/shard_map/ppermute | solution.py:298
  24.1 1.6 %collective-permute-start.1 = (bf16[112,256]{1,0:T(8,128)(2,1)}, bf16[112,256]{1,0:T(8,128)(2,1)S(1)}, u32[]{:S(2)}, u32[]{:S(2)}) collective-permute-start(bf16[112,256]{1,0:T(8,128)(2,1)} %get-tuple-element.46), channel_id=1, source_target_pairs={{0,8},{4,12},{8,0},{12,4},{16,24},{20,28},{24,16},{28,20},{1,9},{5... | collective-permute-start | bytes 172040 | tf_op jit(solution)/shard_map/ppermute | solution.py:298
  25.7 3.0 %collective-permute-start.3 = (bf16[112,256]{1,0:T(8,128)(2,1)}, bf16[112,256]{1,0:T(8,128)(2,1)S(1)}, u32[]{:S(2)}, u32[]{:S(2)}) collective-permute-start(bf16[112,256]{1,0:T(8,128)(2,1)} %get-tuple-element.48), channel_id=1, source_target_pairs={{0,16},{4,20},{8,24},{12,28},{16,0},{20,4},{24,8},{28,12},{1,17},{... | collective-permute-start | bytes 172040 | tf_op jit(solution)/shard_map/ppermute | solution.py:298
  28.7 1.3 %collective-permute-start.4 = (bf16[112,256]{1,0:T(8,128)(2,1)}, bf16[112,256]{1,0:T(8,128)(2,1)S(1)}, u32[]{:S(2)}, u32[]{:S(2)}) collective-permute-start(bf16[112,256]{1,0:T(8,128)(2,1)} %get-tuple-element.49), channel_id=1, source_target_pairs={{0,20},{4,16},{8,28},{12,24},{16,4},{20,0},{24,12},{28,8},{1,21},{... | collective-permute-start | bytes 172040 | tf_op jit(solution)/shard_map/ppermute | solution.py:298
  29.9 3.6 %collective-permute-start.5 = (bf16[112,256]{1,0:T(8,128)(2,1)}, bf16[112,256]{1,0:T(8,128)(2,1)S(1)}, u32[]{:S(2)}, u32[]{:S(2)}) collective-permute-start(bf16[112,256]{1,0:T(8,128)(2,1)} %get-tuple-element.50), channel_id=1, source_target_pairs={{0,24},{4,28},{8,16},{12,20},{16,8},{20,12},{24,0},{28,4},{1,25},{... | collective-permute-start | bytes 172040 | tf_op jit(solution)/shard_map/ppermute | solution.py:298
  33.6 21.1 %filter_part.3 = (bf16[112,256]{1,0:T(8,128)(2,1)}, bf16[112,256]{1,0:T(8,128)(2,1)}, bf16[112,256]{1,0:T(8,128)(2,1)}, bf16[112,256]{1,0:T(8,128)(2,1)}, bf16[1...) custom-call(s32[1]{0:T(128)} %bitcast.2.me_ref, ...), custom_call_target="tpu_custom_call" | custom-call | flops 12884901888 | bytes 23068672 | tf_op jit(solution)/shard_map/filter_part/pallas_call | solution.py:121
  54.7 1.7 %collective-permute-start.7 = (bf16[112,256]{1,0:T(8,128)(2,1)}, bf16[112,256]{1,0:T(8,128)(2,1)S(1)}, u32[]{:S(2)}, u32[]{:S(2)}) collective-permute-start(bf16[112,256]{1,0:T(8,128)(2,1)} %get-tuple-element.70), channel_id=1, source_target_pairs={{0,4},{4,0},{8,12},{12,8},{16,20},{20,16},{24,28},{28,24},{1,5},{5... | collective-permute-start | bytes 172040 | tf_op jit(solution)/shard_map/ppermute | solution.py:298
  56.5 1.8 %collective-permute-start.9 = (bf16[112,256]{1,0:T(8,128)(2,1)}, bf16[112,256]{1,0:T(8,128)(2,1)S(1)}, u32[]{:S(2)}, u32[]{:S(2)}) collective-permute-start(bf16[112,256]{1,0:T(8,128)(2,1)} %get-tuple-element.72), channel_id=1, source_target_pairs={{0,12},{4,8},{8,4},{12,0},{16,28},{20,24},{24,20},{28,16},{1,13},{... | collective-permute-start | bytes 172040 | tf_op jit(solution)/shard_map/ppermute | solution.py:298
  58.3 2.3 %collective-permute-start.10 = (bf16[112,256]{1,0:T(8,128)(2,1)}, bf16[112,256]{1,0:T(8,128)(2,1)S(1)}, u32[]{:S(2)}, u32[]{:S(2)}) collective-permute-start(bf16[112,256]{1,0:T(8,128)(2,1)} %get-tuple-element.73), channel_id=1, source_target_pairs={{0,16},{4,20},{8,24},{12,28},{16,0},{20,4},{24,8},{28,12},{1,17},{... | collective-permute-start | bytes 172040 | tf_op jit(solution)/shard_map/ppermute | solution.py:298
  60.6 1.7 %collective-permute-start.11 = (bf16[112,256]{1,0:T(8,128)(2,1)}, bf16[112,256]{1,0:T(8,128)(2,1)S(1)}, u32[]{:S(2)}, u32[]{:S(2)}) collective-permute-start(bf16[112,256]{1,0:T(8,128)(2,1)} %get-tuple-element.74), channel_id=1, source_target_pairs={{0,20},{4,16},{8,28},{12,24},{16,4},{20,0},{24,12},{28,8},{1,21},{... | collective-permute-start | bytes 172040 | tf_op jit(solution)/shard_map/ppermute | solution.py:298
  62.3 3.6 %collective-permute-start.12 = (bf16[112,256]{1,0:T(8,128)(2,1)}, bf16[112,256]{1,0:T(8,128)(2,1)S(1)}, u32[]{:S(2)}, u32[]{:S(2)}) collective-permute-start(bf16[112,256]{1,0:T(8,128)(2,1)} %get-tuple-element.75), channel_id=1, source_target_pairs={{0,24},{4,28},{8,16},{12,20},{16,8},{20,12},{24,0},{28,4},{1,25},{... | collective-permute-start | bytes 172040 | tf_op jit(solution)/shard_map/ppermute | solution.py:298
  66.0 0.8 copy-done
  66.8 0.5 merge.2
  67.3 1.7 %collective-permute-start.14 = (bf16[512,256]{1,0:T(8,128)(2,1)S(1)}, bf16[512,256]{1,0:T(8,128)(2,1)S(1)}, u32[]{:S(2)}, u32[]{:S(2)}) collective-permute-start(bf16[512,256]{1,0:T(8,128)(2,1)S(1)} %get-tuple-element.78.refs_2_), channel_id=1, source_target_pairs={{0,1},{1,0},{2,3},{3,2},{4,5},{5,4},{6,7},{7,6},{8,9},{9,8},{10,11... | collective-permute-start | bytes 786440 | tf_op jit(solution)/shard_map/ppermute | solution.py:298
  69.1 3.9 %collective-permute-done.13.refs_7_ = bf16[112,256]{1,0:T(8,128)(2,1)S(1)} collective-permute-done((bf16[112,256]{1,0:T(8,128)(2,1)}, bf16[112,256]{1,0:T(8,128)(2,1)S(1)}, u32[]{:S(2)}, u32[]{:S(2)}) %collective-permute-start.13) | collective-permute-done | bytes 57376 | tf_op jit(solution)/shard_map/ppermute | solution.py:298
  73.0 0.8 copy-done.1
  73.8 0.5 merge.3
  74.4 1.6 %collective-permute-start.15 = (bf16[512,256]{1,0:T(8,128)(2,1)S(1)}, bf16[512,256]{1,0:T(8,128)(2,1)S(1)}, u32[]{:S(2)}, u32[]{:S(2)}) collective-permute-start(bf16[512,256]{1,0:T(8,128)(2,1)S(1)} %get-tuple-element.79.refs_3_), channel_id=1, source_target_pairs={{0,1},{1,0},{2,3},{3,2},{4,5},{5,4},{6,7},{7,6},{8,9},{9,8},{10,11... | collective-permute-start | bytes 786440 | tf_op jit(solution)/shard_map/ppermute | solution.py:298
  75.9 0.5 collective-permute-start.19
  76.4 7.8 %correlate.3.refs_4_ = f32[8,2,512,2048]{3,2,1,0:T(8,128)} custom-call(s32[1]{0:T(128)} %bitcast.4.place_ref, bf16[256,512]{1,0:T(8,128)(2,1)S(1)} %get-tuple-element.68.refs_0_, bf16[256,512]{1,0:T(8,128)(2,1)S(1)} %get-tuple-element.77.refs_1_, bf16[512,256]{1,0:T(8,128)(2,1)S(1)} %get-tuple-element.78.refs_2_, bf16[512,256]{1,0:T(8,128)(2,1)S(1)} %get-tuple-element.79.refs_3_), custom_call_target="tpu_custom_call" | custom-call | flops 536870912 | bytes 16777216 | tf_op jit(solution)/shard_map/correlate/pallas_call | solution.py:239
  84.2 0.5 collective-permute-start.17
  84.8 7.8 %correlate.4.refs_6_ = f32[8,2,512,2048]{3,2,1,0:T(8,128)} custom-call(s32[1]{0:T(128)} %bitcast.5.place_ref, bf16[256,512]{1,0:T(8,128)(2,1)S(1)} %get-tuple-element.68.refs_0_, bf16[256,512]{1,0:T(8,128)(2,1)S(1)} %get-tuple-element.77.refs_1_, bf16[512,256]{1,0:T(8,128)(2,1)S(1)} %collective-permute-done.18.refs_2_, ...), custom_call_target="tpu_custom_call", output_to_operand_aliasing={{}: (5, {})} | custom-call | flops 536870912 | bytes 16777216 | tf_op jit(solution)/shard_map/correlate/pallas_call | solution.py:239
  92.6 15.4 %correlate.5 = f32[8,2,512,2048]{3,2,1,0:T(8,128)} custom-call(s32[2]{0:T(128)S(1)} %pad_add_fusion.place_ref, bf16[256,512]{1,0:T(8,128)(2,1)S(1)} %get-tuple-element.68.refs_0_, bf16[256,512]{1,0:T(8,128)(2,1)S(1)} %get-tuple-element.77.refs_1_, bf16[512,256]{1,0:T(8,128)(2,1)S(1)} %collective-permute-done.14.refs_2_, ...), custom_call_target="tpu_custom_call", output_to_operand_aliasing={{}: (7, {})} | custom-call | flops 1073741824 | bytes 33554432 | tf_op jit(solution)/shard_map/correlate/pallas_call | solution.py:239
  (28 shorter events, 0.2 us)
Async XLA Ops:
  21.1 8.9 %collective-permute-start = (bf16[112,256]{1,0:T(8,128)(2,1)}, bf16[112,256]{1,0:T(8,128)(2,1)S(1)}, u32[]{:S(2)}, u32[]{:S(2)}) collective-permute-start(bf16[112,256]{1,0:T(8,128)(2,1)} %get-tuple-element.45), channel_id=1, source_target_pairs={{0,4},{4,0},{8,12},{12,8},{16,20},{20,16},{24,28},{28,24},{1,5},{5... | collective-permute-start | bytes 172040 | tf_op jit(solution)/shard_map/ppermute | solution.py:298
  24.1 9.5 %collective-permute-start.1 = (bf16[112,256]{1,0:T(8,128)(2,1)}, bf16[112,256]{1,0:T(8,128)(2,1)S(1)}, u32[]{:S(2)}, u32[]{:S(2)}) collective-permute-start(bf16[112,256]{1,0:T(8,128)(2,1)} %get-tuple-element.46), channel_id=1, source_target_pairs={{0,8},{4,12},{8,0},{12,4},{16,24},{20,28},{24,16},{28,20},{1,9},{5... | collective-permute-start | bytes 172040 | tf_op jit(solution)/shard_map/ppermute | solution.py:298
  25.7 29.0 %collective-permute-start.2 = (bf16[112,256]{1,0:T(8,128)(2,1)}, bf16[112,256]{1,0:T(8,128)(2,1)S(1)}, u32[]{:S(2)}, u32[]{:S(2)}) collective-permute-start(bf16[112,256]{1,0:T(8,128)(2,1)} %get-tuple-element.47), channel_id=1, source_target_pairs={{0,12},{4,8},{8,4},{12,0},{16,28},{20,24},{24,20},{28,16},{1,13},{... | collective-permute-start | bytes 172040 | tf_op jit(solution)/shard_map/ppermute | solution.py:298
  25.7 29.0 %collective-permute-start.3 = (bf16[112,256]{1,0:T(8,128)(2,1)}, bf16[112,256]{1,0:T(8,128)(2,1)S(1)}, u32[]{:S(2)}, u32[]{:S(2)}) collective-permute-start(bf16[112,256]{1,0:T(8,128)(2,1)} %get-tuple-element.48), channel_id=1, source_target_pairs={{0,16},{4,20},{8,24},{12,28},{16,0},{20,4},{24,8},{28,12},{1,17},{... | collective-permute-start | bytes 172040 | tf_op jit(solution)/shard_map/ppermute | solution.py:298
  28.7 26.0 %collective-permute-start.4 = (bf16[112,256]{1,0:T(8,128)(2,1)}, bf16[112,256]{1,0:T(8,128)(2,1)S(1)}, u32[]{:S(2)}, u32[]{:S(2)}) collective-permute-start(bf16[112,256]{1,0:T(8,128)(2,1)} %get-tuple-element.49), channel_id=1, source_target_pairs={{0,20},{4,16},{8,28},{12,24},{16,4},{20,0},{24,12},{28,8},{1,21},{... | collective-permute-start | bytes 172040 | tf_op jit(solution)/shard_map/ppermute | solution.py:298
  29.9 24.8 %collective-permute-start.5 = (bf16[112,256]{1,0:T(8,128)(2,1)}, bf16[112,256]{1,0:T(8,128)(2,1)S(1)}, u32[]{:S(2)}, u32[]{:S(2)}) collective-permute-start(bf16[112,256]{1,0:T(8,128)(2,1)} %get-tuple-element.50), channel_id=1, source_target_pairs={{0,24},{4,28},{8,16},{12,20},{16,8},{20,12},{24,0},{28,4},{1,25},{... | collective-permute-start | bytes 172040 | tf_op jit(solution)/shard_map/ppermute | solution.py:298
  33.5 21.2 %collective-permute-start.6 = (bf16[112,256]{1,0:T(8,128)(2,1)}, bf16[112,256]{1,0:T(8,128)(2,1)S(1)}, u32[]{:S(2)}, u32[]{:S(2)}) collective-permute-start(bf16[112,256]{1,0:T(8,128)(2,1)} %get-tuple-element.51), channel_id=1, source_target_pairs={{0,28},{4,24},{8,20},{12,16},{16,12},{20,8},{24,4},{28,0},{1,29},{... | collective-permute-start | bytes 172040 | tf_op jit(solution)/shard_map/ppermute | solution.py:298
  54.7 7.6 %collective-permute-start.7 = (bf16[112,256]{1,0:T(8,128)(2,1)}, bf16[112,256]{1,0:T(8,128)(2,1)S(1)}, u32[]{:S(2)}, u32[]{:S(2)}) collective-permute-start(bf16[112,256]{1,0:T(8,128)(2,1)} %get-tuple-element.70), channel_id=1, source_target_pairs={{0,4},{4,0},{8,12},{12,8},{16,20},{20,16},{24,28},{28,24},{1,5},{5... | collective-permute-start | bytes 172040 | tf_op jit(solution)/shard_map/ppermute | solution.py:298
  56.5 9.5 %collective-permute-start.8 = (bf16[112,256]{1,0:T(8,128)(2,1)}, bf16[112,256]{1,0:T(8,128)(2,1)S(1)}, u32[]{:S(2)}, u32[]{:S(2)}) collective-permute-start(bf16[112,256]{1,0:T(8,128)(2,1)} %get-tuple-element.71), channel_id=1, source_target_pairs={{0,8},{4,12},{8,0},{12,4},{16,24},{20,28},{24,16},{28,20},{1,9},{5... | collective-permute-start | bytes 172040 | tf_op jit(solution)/shard_map/ppermute | solution.py:298
  56.5 10.8 %collective-permute-start.9 = (bf16[112,256]{1,0:T(8,128)(2,1)}, bf16[112,256]{1,0:T(8,128)(2,1)S(1)}, u32[]{:S(2)}, u32[]{:S(2)}) collective-permute-start(bf16[112,256]{1,0:T(8,128)(2,1)} %get-tuple-element.72), channel_id=1, source_target_pairs={{0,12},{4,8},{8,4},{12,0},{16,28},{20,24},{24,20},{28,16},{1,13},{... | collective-permute-start | bytes 172040 | tf_op jit(solution)/shard_map/ppermute | solution.py:298
  58.3 10.7 %collective-permute-start.10 = (bf16[112,256]{1,0:T(8,128)(2,1)}, bf16[112,256]{1,0:T(8,128)(2,1)S(1)}, u32[]{:S(2)}, u32[]{:S(2)}) collective-permute-start(bf16[112,256]{1,0:T(8,128)(2,1)} %get-tuple-element.73), channel_id=1, source_target_pairs={{0,16},{4,20},{8,24},{12,28},{16,0},{20,4},{24,8},{28,12},{1,17},{... | collective-permute-start | bytes 172040 | tf_op jit(solution)/shard_map/ppermute | solution.py:298
  60.6 8.4 %collective-permute-start.11 = (bf16[112,256]{1,0:T(8,128)(2,1)}, bf16[112,256]{1,0:T(8,128)(2,1)S(1)}, u32[]{:S(2)}, u32[]{:S(2)}) collective-permute-start(bf16[112,256]{1,0:T(8,128)(2,1)} %get-tuple-element.74), channel_id=1, source_target_pairs={{0,20},{4,16},{8,28},{12,24},{16,4},{20,0},{24,12},{28,8},{1,21},{... | collective-permute-start | bytes 172040 | tf_op jit(solution)/shard_map/ppermute | solution.py:298
  62.3 6.7 %collective-permute-start.12 = (bf16[112,256]{1,0:T(8,128)(2,1)}, bf16[112,256]{1,0:T(8,128)(2,1)S(1)}, u32[]{:S(2)}, u32[]{:S(2)}) collective-permute-start(bf16[112,256]{1,0:T(8,128)(2,1)} %get-tuple-element.75), channel_id=1, source_target_pairs={{0,24},{4,28},{8,16},{12,20},{16,8},{20,12},{24,0},{28,4},{1,25},{... | collective-permute-start | bytes 172040 | tf_op jit(solution)/shard_map/ppermute | solution.py:298
  65.9 7.1 %collective-permute-start.13 = (bf16[112,256]{1,0:T(8,128)(2,1)}, bf16[112,256]{1,0:T(8,128)(2,1)S(1)}, u32[]{:S(2)}, u32[]{:S(2)}) collective-permute-start(bf16[112,256]{1,0:T(8,128)(2,1)} %get-tuple-element.76), channel_id=1, source_target_pairs={{0,28},{4,24},{8,20},{12,16},{16,12},{20,8},{24,4},{28,0},{1,29},{... | collective-permute-start | bytes 172040 | tf_op jit(solution)/shard_map/ppermute | solution.py:298
  66.0 0.8 copy-start
  67.3 16.9 %collective-permute-start.14 = (bf16[512,256]{1,0:T(8,128)(2,1)S(1)}, bf16[512,256]{1,0:T(8,128)(2,1)S(1)}, u32[]{:S(2)}, u32[]{:S(2)}) collective-permute-start(bf16[512,256]{1,0:T(8,128)(2,1)S(1)} %get-tuple-element.78.refs_2_), channel_id=1, source_target_pairs={{0,1},{1,0},{2,3},{3,2},{4,5},{5,4},{6,7},{7,6},{8,9},{9,8},{10,11... | collective-permute-start | bytes 786440 | tf_op jit(solution)/shard_map/ppermute | solution.py:298
  73.0 0.8 copy-start.1
  74.4 9.9 %collective-permute-start.15 = (bf16[512,256]{1,0:T(8,128)(2,1)S(1)}, bf16[512,256]{1,0:T(8,128)(2,1)S(1)}, u32[]{:S(2)}, u32[]{:S(2)}) collective-permute-start(bf16[512,256]{1,0:T(8,128)(2,1)S(1)} %get-tuple-element.79.refs_3_), channel_id=1, source_target_pairs={{0,1},{1,0},{2,3},{3,2},{4,5},{5,4},{6,7},{7,6},{8,9},{9,8},{10,11... | collective-permute-start | bytes 786440 | tf_op jit(solution)/shard_map/ppermute | solution.py:298
  75.9 8.9 %collective-permute-start.18 = (bf16[512,256]{1,0:T(8,128)(2,1)S(1)}, bf16[512,256]{1,0:T(8,128)(2,1)S(1)}, u32[]{:S(2)}, u32[]{:S(2)}) collective-permute-start(bf16[512,256]{1,0:T(8,128)(2,1)S(1)} %get-tuple-element.78.refs_2_), channel_id=1, source_target_pairs={{0,2},{2,0},{1,3},{3,1},{4,6},{6,4},{5,7},{7,5},{8,10},{10,8},{9,1... | collective-permute-start | bytes 786440 | tf_op jit(solution)/shard_map/ppermute | solution.py:298
  75.9 8.9 %collective-permute-start.19 = (bf16[512,256]{1,0:T(8,128)(2,1)S(1)}, bf16[512,256]{1,0:T(8,128)(2,1)S(1)}, u32[]{:S(2)}, u32[]{:S(2)}) collective-permute-start(bf16[512,256]{1,0:T(8,128)(2,1)S(1)} %get-tuple-element.79.refs_3_), channel_id=1, source_target_pairs={{0,2},{2,0},{1,3},{3,1},{4,6},{6,4},{5,7},{7,5},{8,10},{10,8},{9,1... | collective-permute-start | bytes 786440 | tf_op jit(solution)/shard_map/ppermute | solution.py:298
  84.2 8.4 %collective-permute-start.16 = (bf16[512,256]{1,0:T(8,128)(2,1)S(1)}, bf16[512,256]{1,0:T(8,128)(2,1)S(1)}, u32[]{:S(2)}, u32[]{:S(2)}) collective-permute-start(bf16[512,256]{1,0:T(8,128)(2,1)S(1)} %collective-permute-done.14.refs_2_), channel_id=1, source_target_pairs={{0,2},{2,0},{1,3},{3,1},{4,6},{6,4},{5,7},{7,5},{8,10},{10,8},{9,1... | collective-permute-start | bytes 786440 | tf_op jit(solution)/shard_map/ppermute | solution.py:298
  84.2 8.4 %collective-permute-start.17 = (bf16[512,256]{1,0:T(8,128)(2,1)S(1)}, bf16[512,256]{1,0:T(8,128)(2,1)S(1)}, u32[]{:S(2)}, u32[]{:S(2)}) collective-permute-start(bf16[512,256]{1,0:T(8,128)(2,1)S(1)} %collective-permute-done.15.refs_3_), channel_id=1, source_target_pairs={{0,2},{2,0},{1,3},{3,1},{4,6},{6,4},{5,7},{7,5},{8,10},{10,8},{9,1... | collective-permute-start | bytes 786440 | tf_op jit(solution)/shard_map/ppermute | solution.py:298

commit v2 on v1

v2 whole, which is shorter than its diff:
```python
import functools
import math

import jax
import jax.numpy as jnp
import ml_dtypes
import numpy as np
from jax import lax
from jax.experimental import pallas as pl
from jax.experimental.pallas import tpu as pltpu
from jax.sharding import PartitionSpec as P

NFFT = 4096
TAPS = 4
VMEM = 56 * 2**20


def filter_taps():
    span = TAPS * NFFT
    position = np.arange(span, dtype=np.float64)
    centred = (position - span / 2 + 0.5) / NFFT
    window = 0.5 - 0.5 * np.cos(2.0 * np.pi * (position + 0.5) / span)
    return (np.sinc(centred) * window).reshape(TAPS, NFFT)


def low_taps():
    energy = (filter_taps() ** 2).sum(axis=1)
    return [t for t in range(TAPS) if energy[t] > 0.01 * energy.sum()]


def filter_table(channels):
    phases = np.arange(NFFT)[:, None] * np.arange(channels)[None, :] % NFFT
    angles = phases * (2.0 * np.pi / NFFT)
    transform = np.concatenate([np.cos(angles), np.sin(angles)], axis=1) / math.sqrt(NFFT)
    blocks = [tap[:, None] * transform for tap in filter_taps()]
    high = [b.astype(np.float32).astype(ml_dtypes.bfloat16) for b in blocks]
    low = [
        (blocks[t] - high[t].astype(np.float64)).astype(np.float32).astype(ml_dtypes.bfloat16)
        for t in low_taps()
    ]
    return np.ascontiguousarray(np.concatenate(high + low, axis=1).T)


def peer(me, step, length, way):
    if length & (length - 1):
        return (me + way * step) % length
    return me ^ step


def filter_kernel(volt_ref, table_hbm, gain_ref, out_ref, sums, table, arrived):
    frame = pl.program_id(0)
    slots, _, width, rows = sums.shape
    half = width // 2
    pieces = arrived.shape[0]
    depth = table.shape[1] // pieces

    def fetch(piece):
        columns = pl.ds(piece * depth, depth)
        return pltpu.make_async_copy(
            table_hbm.at[:, columns], table.at[:, columns], arrived.at[piece]
        )

    def product(start, size):
        return lax.dot_general(
            table[:, start : start + size],
            volt_ref[:, :, start : start + size].reshape(2 * rows, size),
            (((1,), (1,)), ((), ())),
            preferred_element_type=jnp.float32,
        )

    def add(term):
        low = low_taps()
        for tap in range(TAPS):
            value = term[tap * width : (tap + 1) * width]
            if tap in low:
                at = (TAPS + low.index(tap)) * width
                value = value + term[at : at + width]
            for part in range(2):
                sums[frame + TAPS - 1 - tap, part] += value[:, part * rows : (part + 1) * rows]

    @pl.when(frame == 0)
    def _():
        for piece in range(pieces):
            fetch(piece).start()
        sums[...] = jnp.zeros_like(sums)
        for piece in range(pieces):
            fetch(piece).wait()
            add(product(piece * depth, depth))

    @pl.when(frame > 0)
    def _():
        add(product(0, table.shape[1]))

    @pl.when(frame == pl.num_programs(0) - 1)
    def _():
        owners = out_ref.shape[0]
        share = half // owners
        for slot in range(slots):
            real = sums[slot, 0, :half] + sums[slot, 1, half:]
            imag = sums[slot, 1, :half] - sums[slot, 0, half:]
            out_real = gain_ref[0] * real - gain_ref[1] * imag
            out_imag = gain_ref[0] * imag + gain_ref[1] * real
            for owner in range(owners):
                at = owner * share
                both = jnp.concatenate(
                    [out_real[at : at + share], out_imag[at : at + share]], axis=0
                )
                at = 2 * share * slot
                out_ref[owner, at : at + 2 * share, :] = both.astype(jnp.bfloat16)


def filter_all(voltages, table, gains, owners):
    rows = voltages.shape[1]
    frames = voltages.shape[2] // NFFT
    half = gains.shape[1]
    slots = frames + TAPS - 1
    out_rows = slots * 2 * half // owners
    columns = table.shape[0]
    pieces = 2
    return pl.pallas_call(
        filter_kernel,
        grid=(frames,),
        in_specs=[
            pl.BlockSpec((2, rows, NFFT), lambda f: (0, 0, f)),
            pl.BlockSpec(memory_space=pl.ANY),
            pl.BlockSpec((2, half, rows), lambda f: (0, 0, 0)),
        ],
        out_specs=pl.BlockSpec((owners, out_rows, rows), lambda f: (0, 0, 0)),
        out_shape=jax.ShapeDtypeStruct((owners, out_rows, rows), jnp.bfloat16),
        scratch_shapes=[
            pltpu.VMEM((slots, 2, 2 * half, rows), jnp.float32),
            pltpu.VMEM((columns, NFFT), jnp.bfloat16),
            pltpu.SemaphoreType.DMA((pieces,)),
        ],
        compiler_params=pltpu.CompilerParams(vmem_limit_bytes=VMEM),
        cost_estimate=pl.CostEstimate(
            flops=2 * 2 * rows * frames * NFFT * columns,
            bytes_accessed=2 * (2 * rows * frames * NFFT + NFFT * columns),
            transcendentals=0,
        ),
        name="filter_all",
    )(voltages, table, gains)


def merge_kernel(frames, share, norm, in_ref, out_ref, left_ref, scratch):
    owners = in_ref.shape[0]
    depth = 2 * owners * frames
    blocks = scratch.shape[0]
    for group in range(owners):
        for frame in range(frames):
            at = 2 * share * frame
            value = in_ref[group, at : at + 2 * share, :].astype(jnp.float32)
            if group > 0 and frame < TAPS - 1:
                at = 2 * share * (frame + frames)
                value = value + in_ref[group - 1, at : at + 2 * share, :].astype(jnp.float32)
            if value.shape[1] < 128 * blocks:
                spare = jnp.zeros((2 * share, 128 * blocks - value.shape[1]), jnp.float32)
                value = jnp.concatenate([value, spare], axis=1)
            for part in range(2):
                row = (part * owners + group) * frames + frame
                for block in range(blocks):
                    scratch[block, pl.ds(row, share, stride=depth), :] = value[
                        part * share : (part + 1) * share, block * 128 : (block + 1) * 128
                    ]
    for block in range(blocks):
        lanes = min(128, out_ref.shape[1] - block * 128)
        at = block * 128
        for channel in range(share):
            rounded = scratch[block, channel * depth : (channel + 1) * depth, :].astype(jnp.bfloat16)
            out_ref[channel * depth : (channel + 1) * depth, at : at + lanes] = rounded[:, :lanes]
            scaled = norm * rounded.astype(jnp.float32)
            high = scaled.astype(jnp.bfloat16).astype(jnp.float32)
            both = jnp.concatenate([high, scaled - high], axis=0).T
            left_ref[at : at + lanes, 2 * channel * depth : 2 * (channel + 1) * depth] = both[
                :lanes
            ].astype(jnp.bfloat16)


def merge(turned, frames, share, norm):
    owners, in_rows, rows = turned.shape
    out_rows = share * 2 * owners * frames
    return pl.pallas_call(
        functools.partial(merge_kernel, frames, share, norm),
        in_specs=[pl.BlockSpec(memory_space=pltpu.VMEM)],
        out_shape=[
            jax.ShapeDtypeStruct((out_rows, rows), jnp.bfloat16),
            jax.ShapeDtypeStruct((rows, 2 * out_rows), jnp.bfloat16),
        ],
        scratch_shapes=[pltpu.VMEM((pl.cdiv(rows, 128), out_rows, 128), jnp.float32)],
        compiler_params=pltpu.CompilerParams(vmem_limit_bytes=16 * 2**20),
        name="merge",
    )(turned)


def visibility(left, right):
    half = right.shape[0] // 2
    crossed = jnp.concatenate([-right[half:], right[:half]], axis=0)
    return [
        jnp.dot(
            left, jnp.concatenate([value, value], axis=0), preferred_element_type=jnp.float32
        )
        for value in (right, crossed)
    ]


def block_kernel(blocks, place_ref, left_ref, *refs):
    right_refs, out_ref = refs[:blocks], refs[-1]
    count = out_ref.shape[0]
    depth = right_refs[0].shape[0] // count
    for block in range(blocks):

        @pl.when(pl.program_id(1) == block)
        def _():
            for channel in range(count):
                out_ref[channel, 0], out_ref[channel, 1] = visibility(
                    left_ref[:, 2 * depth * channel : 2 * depth * (channel + 1)],
                    right_refs[block][depth * channel : depth * (channel + 1), :],
                )


def correlate(left, rights, places, total, result, share):
    blocks = len(rights)
    out_rows, rows = rights[0].shape
    depth = out_rows // share
    count = 2
    operands = [places, left, *rights]
    specs = [pl.BlockSpec((rows, 2 * depth * count), lambda c, b, places: (0, c))]
    specs += [pl.BlockSpec((depth * count, rows), lambda c, b, places: (c, 0))] * blocks
    aliases = {}
    if result is not None:
        aliases = {len(operands): 0}
        operands.append(result)
        specs.append(pl.BlockSpec(memory_space=pl.ANY))
    return pl.pallas_call(
        functools.partial(block_kernel, blocks),
        grid_spec=pltpu.PrefetchScalarGridSpec(
            num_scalar_prefetch=1,
            grid=(share // count, blocks),
            in_specs=specs,
            out_specs=pl.BlockSpec(
                (count, 2, rows, rows), lambda c, b, places: (c, 0, 0, places[b])
            ),
        ),
        out_shape=jax.ShapeDtypeStruct((share, 2, rows, total), jnp.float32),
        input_output_aliases=aliases,
        compiler_params=pltpu.CompilerParams(vmem_limit_bytes=24 * 2**20),
        cost_estimate=pl.CostEstimate(
            flops=8 * share * blocks * rows * rows * depth,
            bytes_accessed=4 * share * 2 * blocks * rows * rows,
            transcendentals=0,
        ),
        name="correlate",
    )(*operands)


def whole_kernel(left_ref, all_ref, out_ref):
    rows = left_ref.shape[0]
    for group in range(all_ref.shape[0]):
        values = visibility(left_ref[...], all_ref[group])
        for kind in range(2):
            out_ref[0, kind, :, group * rows : (group + 1) * rows] = values[kind]


def correlate_whole(left, gathered, share):
    groups, out_rows, rows = gathered.shape
    depth = out_rows // share
    return pl.pallas_call(
        whole_kernel,
        grid=(share,),
        in_specs=[
            pl.BlockSpec((rows, 2 * depth), lambda c: (0, c)),
            pl.BlockSpec((groups, depth, rows), lambda c: (0, c, 0)),
        ],
        out_specs=pl.BlockSpec((1, 2, rows, groups * rows), lambda c: (c, 0, 0, 0)),
        out_shape=jax.ShapeDtypeStruct((share, 2, rows, groups * rows), jnp.float32),
        compiler_params=pltpu.CompilerParams(vmem_limit_bytes=24 * 2**20),
        name="correlate_whole",
    )(left, gathered)


def swapped(shard, axis, step):
    if step == 0:
        return shard
    length = lax.axis_size(axis)
    return lax.ppermute(shard, axis, [(i, peer(i, step, length, 1)) for i in range(length)])


def body(voltages, gains):
    inputs_here = voltages.shape[1]
    frames_here = voltages.shape[2] // NFFT
    channels = gains.shape[2]
    owners = lax.axis_size("fgrp")
    share = channels // owners
    norm = 1.0 / math.sqrt(frames_here * owners)
    table = jnp.asarray(filter_table(channels))
    partial = filter_all(voltages, table, jnp.swapaxes(gains, 1, 2), owners)
    turned = lax.all_to_all(partial, "fgrp", split_axis=0, concat_axis=0, tiled=True)
    own, left = merge(turned, frames_here, share, norm)
    tiles, pols = lax.axis_size("tile"), lax.axis_size("pol")
    if inputs_here % 128:
        wide = lax.all_gather(lax.all_gather(own, "pol", axis=0), "tile", axis=0)
        return correlate_whole(left, wide.reshape((-1,) + own.shape), share)
    tile, pol = lax.axis_index("tile"), lax.axis_index("pol")

    def place(by_tile, by_pol):
        return (peer(tile, by_tile, tiles, -1) * pols + peer(pol, by_pol, pols, -1)).astype(jnp.int32)

    total = tiles * pols * inputs_here
    far = [swapped(own, "pol", by_pol) for by_pol in range(1, pols)]
    result = correlate(left, [own], place(0, 0).reshape(1), total, None, share)
    far, result = lax.optimization_barrier((far, result))
    for by_pol in range(pols):
        near = own if by_pol == 0 else far[by_pol - 1]
        rights = [swapped(near, "tile", by_tile) for by_tile in range(tiles)]
        steps = range(1 if by_pol == 0 else 0, tiles)
        result = correlate(
            left,
            [rights[step] for step in steps],
            jnp.stack([place(step, by_pol) for step in steps]),
            total,
            result,
            share,
        )
    return result


def solution(mesh):
    placed = (P(None, ("tile", "pol"), "fgrp"), P(None, ("tile", "pol"), None))
    return jax.shard_map(
        body,
        mesh=mesh,
        in_specs=placed,
        out_specs=P("fgrp", None, ("tile", "pol"), None),
        check_vma=False,
    )
```

time: 108 us -> 99 us (0.917)
  blocking collectives: 0 us -> 30.6 us
  starting transfers between devices: 28 us -> 1.59 us
  Pallas kernels: 74.1 us -> 62.8 us
  local copies, waits for them, and re-layouts: 1.64 us -> 0 us
    all_to_all x0 -> x1, blocking collectives: none -> 30.6 us  [body(): lax.all_to_all(partial, 'fgrp', split_axis=0, concat_axis=0, tiled=True)]
    ppermute x20 -> x3, starting transfers between devices: 28 us -> 1.59 us  [swapped(): lax.ppermute(shard, axis, [(i, peer(i, step, length, 1)) for i in range(l...]
    pallas_call x7 -> x5, Pallas kernels: 74.1 us -> 62.8 us  [the longest x1 35.1 us: filter_all(): pl.pallas_call(filter_kernel, grid=(frames,), in_specs=[pl.BlockSpec((2,...]
    unnamed x4 -> x0, local copies, waits for them, and re-layouts: 1.64 us -> none
    ppermute x20 -> x3, waiting for transfers between devices: 4 us -> 3.67 us  [swapped(): lax.ppermute(shard, axis, [(i, peer(i, step, length, 1)) for i in range(l...]
  transfers between devices with their start and end apart: 20 -> 3, of which waited for: 1 -> 1; matrix products, arithmetic and copies ran while one was open for 0% -> 0% of each run, Pallas kernels for 35% -> 14%
where the time goes in v2:
time: 99 us; the launch traced here: 98.8 us
  Pallas kernels  62.8 us (63%)
  blocking collectives  30.6 us (31%)
  waiting for transfers between devices  3.67 us (4%)
  starting transfers between devices  1.59 us (2%)
    pallas_call x1, Pallas kernels, filter_all(): pl.pallas_call(filter_kernel, grid=(frames,), in_specs=[pl.BlockSpec((2,...  35.1 us
    all_to_all x1, blocking collectives, body(): lax.all_to_all(partial, 'fgrp', split_axis=0, concat_axis=0, tiled=True)  30.6 us
    pallas_call x3, Pallas kernels, correlate(): pl.pallas_call(functools.partial(block_kernel, blocks), grid_spec=pltpu.P...  26.7 us
    ppermute x3, waiting for transfers between devices, swapped(): lax.ppermute(shard, axis, [(i, peer(i, step, length, 1)) for i in range(l...  3.67 us
  transfers between devices with their start and end apart: 3, of which 1 were waited for; matrix products, arithmetic and copies ran while one was open for 0% of the time, Pallas kernels for 14%

profile of v2, /device:TPU:0, one launch (start us, length us, event | category | flops | bytes accessed | tf_op | source)
XLA Modules:
  0.0 98.8 jit_solution(1133876781782417959)
XLA Ops:
  0.0 35.1 %filter_all.1 = bf16[8,112,512]{2,1,0:T(8,128)(2,1)} custom-call(bf16[2,512,16384]{2,1,0:T(8,128)(2,1)} %volt_ref.1, bf16[768,4096]{1,0:T(8,128)(2,1)} %constant.12.clone.table_hbm, f32[2,64,512]{2,1,0:T(8,128)} %bitcast.5), custom_call_target="tpu_custom_call" | custom-call | flops 25769803776 | bytes 39845888 | tf_op jit(solution)/shard_map/filter_all/pallas_call | solution.py:120
  35.1 30.6 %all_to_all.5.in_ref = bf16[8,112,512]{2,1,0:T(8,128)(2,1)S(1)} all-to-all(bf16[8,112,512]{2,1,0:T(8,128)(2,1)} %filter_all.1), channel_id=1, replica_groups=mesh['fgrp'=8,'tile'=2,'pol'=2] {'fgrp'}, dimensions={0} | all-to-all | bytes 1835008 | tf_op jit(solution)/shard_map/all_to_all | solution.py:297
  65.7 1.1 %merge.1 = (bf16[512,512]{1,0:T(8,128)(2,1)S(1)}, bf16[512,1024]{1,0:T(8,128)(2,1)S(1)}) custom-call(bf16[8,112,512]{2,1,0:T(8,128)(2,1)S(1)} %all_to_all.5.in_ref), custom_call_target="tpu_custom_call" | custom-call | tf_op jit(solution)/shard_map/merge/pallas_call | solution.py:182
  66.8 1.6 %collective-permute-start = (bf16[512,512]{1,0:T(8,128)(2,1)S(1)}, bf16[512,512]{1,0:T(8,128)(2,1)S(1)}, u32[]{:S(2)}, u32[]{:S(2)}) collective-permute-start(bf16[512,512]{1,0:T(8,128)(2,1)S(1)} %get-tuple-element.10.refs_0_), channel_id=1, source_target_pairs={{0,1},{1,0},{2,3},{3,2},{4,5},{5,4},{6,7},{7,6},{8,9},{9,8},{10,11... | collective-permute-start | bytes 1572872 | tf_op jit(solution)/shard_map/ppermute | solution.py:285
  68.4 0.0 collective-permute-start.2
  68.4 6.9 %correlate.3.refs_1_ = f32[8,2,512,2048]{3,2,1,0:T(8,128)} custom-call(s32[1]{0:T(128)} %bitcast.3.place_ref, bf16[512,1024]{1,0:T(8,128)(2,1)S(1)} %get-tuple-element.9.left_ref, bf16[512,512]{1,0:T(8,128)(2,1)S(1)} %get-tuple-element.10.refs_0_), custom_call_target="tpu_custom_call" | custom-call | flops 1073741824 | bytes 16777216 | tf_op jit(solution)/shard_map/correlate/pallas_call | solution.py:234
  75.3 3.7 %collective-permute-done.refs_0_ = bf16[512,512]{1,0:T(8,128)(2,1)S(1)} collective-permute-done((bf16[512,512]{1,0:T(8,128)(2,1)S(1)}, bf16[512,512]{1,0:T(8,128)(2,1)S(1)}, u32[]{:S(2)}, u32[]{:S(2)}) %collective-permute-start) | collective-permute-done | bytes 524320 | tf_op jit(solution)/shard_map/ppermute | solution.py:285
  78.9 0.0 collective-permute-start.1
  78.9 0.1 pad_add_fusion.place_ref
  79.0 0.0 collective-permute-done.2.refs_0_
  79.0 6.9 %correlate.4.refs_2_ = f32[8,2,512,2048]{3,2,1,0:T(8,128)} custom-call(s32[1]{0:T(128)} %bitcast.4.place_ref, bf16[512,1024]{1,0:T(8,128)(2,1)S(1)} %get-tuple-element.9.left_ref, bf16[512,512]{1,0:T(8,128)(2,1)S(1)} %collective-permute-done.2.refs_0_, f32[8,2,512,2048]{3,2,1,0:T(8,128)} %correlate.3.refs_1_), custom_call_target="tpu_custom_call", output_to_operand_aliasing={{}: (3, {})} | custom-call | flops 1073741824 | bytes 16777216 | tf_op jit(solution)/shard_map/correlate/pallas_call | solution.py:234
  85.9 0.0 collective-permute-done.1.refs_1_
  85.9 12.9 %correlate.5 = f32[8,2,512,2048]{3,2,1,0:T(8,128)} custom-call(s32[2]{0:T(128)S(1)} %pad_add_fusion.place_ref, bf16[512,1024]{1,0:T(8,128)(2,1)S(1)} %get-tuple-element.9.left_ref, bf16[512,512]{1,0:T(8,128)(2,1)S(1)} %collective-permute-done.refs_0_, bf16[512,512]{1,0:T(8,128)(2,1)S(1)} %collective-permute-done.1.refs_1_, ...), custom_call_target="tpu_custom_call", output_to_operand_aliasing={{}: (4, {})} | custom-call | flops 2147483648 | bytes 33554432 | tf_op jit(solution)/shard_map/correlate/pallas_call | solution.py:234
Async XLA Ops:
  66.8 12.1 %collective-permute-start = (bf16[512,512]{1,0:T(8,128)(2,1)S(1)}, bf16[512,512]{1,0:T(8,128)(2,1)S(1)}, u32[]{:S(2)}, u32[]{:S(2)}) collective-permute-start(bf16[512,512]{1,0:T(8,128)(2,1)S(1)} %get-tuple-element.10.refs_0_), channel_id=1, source_target_pairs={{0,1},{1,0},{2,3},{3,2},{4,5},{5,4},{6,7},{7,6},{8,9},{9,8},{10,11... | collective-permute-start | bytes 1572872 | tf_op jit(solution)/shard_map/ppermute | solution.py:285
  68.4 10.6 %collective-permute-start.2 = (bf16[512,512]{1,0:T(8,128)(2,1)S(1)}, bf16[512,512]{1,0:T(8,128)(2,1)S(1)}, u32[]{:S(2)}, u32[]{:S(2)}) collective-permute-start(bf16[512,512]{1,0:T(8,128)(2,1)S(1)} %get-tuple-element.10.refs_0_), channel_id=1, source_target_pairs={{0,2},{2,0},{1,3},{3,1},{4,6},{6,4},{5,7},{7,5},{8,10},{10,8},{9,1... | collective-permute-start | bytes 1572872 | tf_op jit(solution)/shard_map/ppermute | solution.py:285
  78.9 7.0 %collective-permute-start.1 = (bf16[512,512]{1,0:T(8,128)(2,1)S(1)}, bf16[512,512]{1,0:T(8,128)(2,1)S(1)}, u32[]{:S(2)}, u32[]{:S(2)}) collective-permute-start(bf16[512,512]{1,0:T(8,128)(2,1)S(1)} %collective-permute-done.refs_0_), channel_id=1, source_target_pairs={{0,2},{2,0},{1,3},{3,1},{4,6},{6,4},{5,7},{7,5},{8,10},{10,8},{9,1... | collective-permute-start | bytes 1572872 | tf_op jit(solution)/shard_map/ppermute | solution.py:285

commit v3 on v2

--- a/solution.py
+++ b/solution.py
@@ -23,22 +23,24 @@
     return (np.sinc(centred) * window).reshape(TAPS, NFFT)
 
 
-def low_taps():
+def tap_order():
     energy = (filter_taps() ** 2).sum(axis=1)
-    return [t for t in range(TAPS) if energy[t] > 0.01 * energy.sum()]
+    order = list(range(TAPS))[::-1]
+    return order, [t for t in order if energy[t] > 0.01 * energy.sum()]
 
 
 def filter_table(channels):
+    order, low_order = tap_order()
     phases = np.arange(NFFT)[:, None] * np.arange(channels)[None, :] % NFFT
     angles = phases * (2.0 * np.pi / NFFT)
     transform = np.concatenate([np.cos(angles), np.sin(angles)], axis=1) / math.sqrt(NFFT)
-    blocks = [tap[:, None] * transform for tap in filter_taps()]
-    high = [b.astype(np.float32).astype(ml_dtypes.bfloat16) for b in blocks]
+    blocks = {t: filter_taps()[t][:, None] * transform for t in order}
+    high = {t: b.astype(np.float32).astype(ml_dtypes.bfloat16) for t, b in blocks.items()}
     low = [
         (blocks[t] - high[t].astype(np.float64)).astype(np.float32).astype(ml_dtypes.bfloat16)
-        for t in low_taps()
+        for t in low_order
     ]
-    return np.ascontiguousarray(np.concatenate(high + low, axis=1).T)
+    return np.ascontiguousarray(np.concatenate([high[t] for t in order] + low, axis=1).T)
 
 
 def peer(me, step, length, way):
@@ -47,12 +49,16 @@
     return me ^ step
 
 
-def filter_kernel(volt_ref, table_hbm, gain_ref, out_ref, sums, table, arrived):
-    frame = pl.program_id(0)
-    slots, _, width, rows = sums.shape
-    half = width // 2
+def filter_kernel(volt_ref, table_hbm, gain_ref, out_ref, sums, low_sums, table, arrived):
+    frame, part = pl.program_id(0), pl.program_id(1)
+    rows = sums.shape[2]
+    half = gain_ref.shape[1]
+    width = 2 * half
     pieces = arrived.shape[0]
     depth = table.shape[1] // pieces
+    order, low_order = tap_order()
+    here = pl.ds(pl.multiple_of(frame * width, width), len(order) * width)
+    low_here = pl.ds(pl.multiple_of(frame * width, width), len(low_order) * width)
 
     def fetch(piece):
         columns = pl.ds(piece * depth, depth)
@@ -60,53 +66,53 @@
             table_hbm.at[:, columns], table.at[:, columns], arrived.at[piece]
         )
 
-    def product(start, size):
-        return lax.dot_general(
+    def add(start, size):
+        before = jnp.concatenate([sums[part, here, :], low_sums[part, low_here, :]], axis=0)
+        after = before + lax.dot_general(
             table[:, start : start + size],
-            volt_ref[:, :, start : start + size].reshape(2 * rows, size),
+            volt_ref[0, :, start : start + size],
             (((1,), (1,)), ((), ())),
             preferred_element_type=jnp.float32,
         )
-
-    def add(term):
-        low = low_taps()
-        for tap in range(TAPS):
-            value = term[tap * width : (tap + 1) * width]
-            if tap in low:
-                at = (TAPS + low.index(tap)) * width
-                value = value + term[at : at + width]
-            for part in range(2):
-                sums[frame + TAPS - 1 - tap, part] += value[:, part * rows : (part + 1) * rows]
-
-    @pl.when(frame == 0)
+        sums[part, here, :] = after[: len(order) * width]
+        low_sums[part, low_here, :] = after[len(order) * width :]
+
+    first = (frame == 0) & (part == 0)
+
+    @pl.when(first)
     def _():
         for piece in range(pieces):
             fetch(piece).start()
         sums[...] = jnp.zeros_like(sums)
+        low_sums[...] = jnp.zeros_like(low_sums)
         for piece in range(pieces):
             fetch(piece).wait()
-            add(product(piece * depth, depth))
-
-    @pl.when(frame > 0)
+            add(piece * depth, depth)
+
+    @pl.when(jnp.logical_not(first))
     def _():
-        add(product(0, table.shape[1]))
-
-    @pl.when(frame == pl.num_programs(0) - 1)
+        add(0, table.shape[1])
+
+    @pl.when((frame == pl.num_programs(0) - 1) & (part == 1))
     def _():
         owners = out_ref.shape[0]
         share = half // owners
-        for slot in range(slots):
-            real = sums[slot, 0, :half] + sums[slot, 1, half:]
-            imag = sums[slot, 1, :half] - sums[slot, 0, half:]
+        for slot in range(sums.shape[1] // width):
+            both = [sums[c, slot * width : (slot + 1) * width, :] for c in range(2)]
+            at = (slot - order.index(low_order[0])) * width
+            if 0 <= at < low_sums.shape[1]:
+                both = [both[c] + low_sums[c, at : at + width, :] for c in range(2)]
+            real = both[0][:half] + both[1][half:]
+            imag = both[1][:half] - both[0][half:]
             out_real = gain_ref[0] * real - gain_ref[1] * imag
             out_imag = gain_ref[0] * imag + gain_ref[1] * real
             for owner in range(owners):
                 at = owner * share
-                both = jnp.concatenate(
+                pair = jnp.concatenate(
                     [out_real[at : at + share], out_imag[at : at + share]], axis=0
                 )
                 at = 2 * share * slot
-                out_ref[owner, at : at + 2 * share, :] = both.astype(jnp.bfloat16)
+                out_ref[owner, at : at + 2 * share, :] = pair.astype(jnp.bfloat16)
 
 
 def filter_all(voltages, table, gains, owners):
@@ -114,21 +120,23 @@
     frames = voltages.shape[2] // NFFT
     half = gains.shape[1]
     slots = frames + TAPS - 1
+    low_slots = frames + len(tap_order()[1]) - 1
     out_rows = slots * 2 * half // owners
     columns = table.shape[0]
-    pieces = 2
+    pieces = 4
     return pl.pallas_call(
         filter_kernel,
-        grid=(frames,),
+        grid=(frames, 2),
         in_specs=[
-            pl.BlockSpec((2, rows, NFFT), lambda f: (0, 0, f)),
+            pl.BlockSpec((1, rows, NFFT), lambda f, c: (c, 0, f)),
             pl.BlockSpec(memory_space=pl.ANY),
-            pl.BlockSpec((2, half, rows), lambda f: (0, 0, 0)),
+            pl.BlockSpec((2, half, rows), lambda f, c: (0, 0, 0)),
         ],
-        out_specs=pl.BlockSpec((owners, out_rows, rows), lambda f: (0, 0, 0)),
+        out_specs=pl.BlockSpec((owners, out_rows, rows), lambda f, c: (0, 0, 0)),
         out_shape=jax.ShapeDtypeStruct((owners, out_rows, rows), jnp.bfloat16),
         scratch_shapes=[
-            pltpu.VMEM((slots, 2, 2 * half, rows), jnp.float32),
+            pltpu.VMEM((2, slots * 2 * half, rows), jnp.float32),
+            pltpu.VMEM((2, low_slots * 2 * half, rows), jnp.float32),
             pltpu.VMEM((columns, NFFT), jnp.bfloat16),
             pltpu.SemaphoreType.DMA((pieces,)),
         ],
@@ -306,21 +314,15 @@
         return (peer(tile, by_tile, tiles, -1) * pols + peer(pol, by_pol, pols, -1)).astype(jnp.int32)
 
     total = tiles * pols * inputs_here
-    far = [swapped(own, "pol", by_pol) for by_pol in range(1, pols)]
-    result = correlate(left, [own], place(0, 0).reshape(1), total, None, share)
-    far, result = lax.optimization_barrier((far, result))
+    result = None
     for by_pol in range(pols):
-        near = own if by_pol == 0 else far[by_pol - 1]
-        rights = [swapped(near, "tile", by_tile) for by_tile in range(tiles)]
-        steps = range(1 if by_pol == 0 else 0, tiles)
-        result = correlate(
-            left,
-            [rights[step] for step in steps],
-            jnp.stack([place(step, by_pol) for step in steps]),
-            total,
-            result,
-            share,
-        )
+        near = swapped(own, "pol", by_pol)
+        if by_pol:
+            near, result = lax.optimization_barrier((near, result))
+        for by_tile in range(tiles):
+            right = swapped(near, "tile", by_tile)
+            where = place(by_tile, by_pol).reshape(1)
+            result = correlate(left, [right], where, total, result, share)
     return result
 
 

time: 99 us -> 94.8 us (0.958)
  waiting for transfers between devices: 3.67 us -> 0.01 us
    ppermute x3, waiting for transfers between devices: 3.67 us -> 0.01 us  [swapped(): lax.ppermute(shard, axis, [(i, peer(i, step, length, 1)) for i in range(l...]
    pallas_call x1, Pallas kernels: 35.1 us -> 33.5 us  [filter_all(): pl.pallas_call(filter_kernel, grid=(frames, 2), in_specs=[pl.BlockSpec((1...]
    pallas_call x3 -> x4, Pallas kernels: 26.7 us -> 27.5 us  [correlate(): pl.pallas_call(functools.partial(block_kernel, blocks), grid_spec=pltpu.P...]
  transfers between devices with their start and end apart: 3 -> 3, of which waited for: 1 -> 0; matrix products, arithmetic and copies ran while one was open for 0% -> 0% of each run, Pallas kernels for 14% -> 22%
where the time goes in v3:
time: 94.8 us; the launch traced here: 94.6 us
  Pallas kernels  62.2 us (66%)
  blocking collectives  30.6 us (32%)
  starting transfers between devices  1.81 us (2%)
    pallas_call x1, Pallas kernels, filter_all(): pl.pallas_call(filter_kernel, grid=(frames, 2), in_specs=[pl.BlockSpec((1...  33.5 us
    all_to_all x1, blocking collectives, body(): lax.all_to_all(partial, 'fgrp', split_axis=0, concat_axis=0, tiled=True)  30.6 us
    pallas_call x4, Pallas kernels, correlate(): pl.pallas_call(functools.partial(block_kernel, blocks), grid_spec=pltpu.P...  27.5 us
  transfers between devices with their start and end apart: 3, of which 0 were waited for; matrix products, arithmetic and copies ran while one was open for 0% of the time, Pallas kernels for 22%

profile of v3, /device:TPU:0, one launch (start us, length us, event | category | flops | bytes accessed | tf_op | source)
XLA Modules:
  0.0 94.6 jit_solution(9919400366192331795)
XLA Ops:
  0.0 33.5 %filter_all.1 = bf16[8,112,512]{2,1,0:T(8,128)(2,1)} custom-call(bf16[2,512,16384]{2,1,0:T(8,128)(2,1)} %volt_ref.1, bf16[768,4096]{1,0:T(8,128)(2,1)} %constant.12.clone.table_hbm, f32[2,64,512]{2,1,0:T(8,128)} %bitcast.5), custom_call_target="tpu_custom_call" | custom-call | flops 25769803776 | bytes 39845888 | tf_op jit(solution)/shard_map/filter_all/pallas_call | solution.py:127
  33.5 30.6 %all_to_all.5.in_ref = bf16[8,112,512]{2,1,0:T(8,128)(2,1)S(1)} all-to-all(bf16[8,112,512]{2,1,0:T(8,128)(2,1)} %filter_all.1), channel_id=1, replica_groups=mesh['fgrp'=8,'tile'=2,'pol'=2] {'fgrp'}, dimensions={0} | all-to-all | bytes 1835008 | tf_op jit(solution)/shard_map/all_to_all | solution.py:305
  64.1 1.1 %merge.1 = (bf16[512,512]{1,0:T(8,128)(2,1)S(1)}, bf16[512,1024]{1,0:T(8,128)(2,1)S(1)}) custom-call(bf16[8,112,512]{2,1,0:T(8,128)(2,1)S(1)} %all_to_all.5.in_ref), custom_call_target="tpu_custom_call" | custom-call | tf_op jit(solution)/shard_map/merge/pallas_call | solution.py:190
  65.2 0.1 collective-permute-start.1
  65.3 1.6 %collective-permute-start = (bf16[512,512]{1,0:T(8,128)(2,1)S(1)}, bf16[512,512]{1,0:T(8,128)(2,1)S(1)}, u32[]{:S(2)}, u32[]{:S(2)}) collective-permute-start(bf16[512,512]{1,0:T(8,128)(2,1)S(1)} %get-tuple-element.10.refs_0_), channel_id=1, source_target_pairs={{0,1},{1,0},{2,3},{3,2},{4,5},{5,4},{6,7},{7,6},{8,9},{9,8},{10,11... | collective-permute-start | bytes 1572872 | tf_op jit(solution)/shard_map/ppermute | solution.py:293
  66.9 6.9 %correlate.4.refs_1_ = f32[8,2,512,2048]{3,2,1,0:T(8,128)} custom-call(s32[1]{0:T(128)} %bitcast.3.place_ref, bf16[512,1024]{1,0:T(8,128)(2,1)S(1)} %get-tuple-element.9.left_ref, bf16[512,512]{1,0:T(8,128)(2,1)S(1)} %get-tuple-element.10.refs_0_), custom_call_target="tpu_custom_call" | custom-call | flops 1073741824 | bytes 16777216 | tf_op jit(solution)/shard_map/correlate/pallas_call | solution.py:242
  73.8 0.0 collective-permute-done.1.refs_0_
  73.8 6.9 %correlate.5.refs_1_ = f32[8,2,512,2048]{3,2,1,0:T(8,128)} custom-call(s32[1]{0:T(128)} %bitcast.2.place_ref, bf16[512,1024]{1,0:T(8,128)(2,1)S(1)} %get-tuple-element.9.left_ref, bf16[512,512]{1,0:T(8,128)(2,1)S(1)} %collective-permute-done.1.refs_0_, f32[8,2,512,2048]{3,2,1,0:T(8,128)} %correlate.4.refs_1_), custom_call_target="tpu_custom_call", output_to_operand_aliasing={{}: (3, {})} | custom-call | flops 1073741824 | bytes 16777216 | tf_op jit(solution)/shard_map/correlate/pallas_call | solution.py:242
  80.7 0.0 collective-permute-done.refs_0_
  80.7 0.2 collective-permute-start.2
  80.8 6.9 %correlate.6.refs_1_ = f32[8,2,512,2048]{3,2,1,0:T(8,128)} custom-call(s32[1]{0:T(128)} %bitcast.4.place_ref, bf16[512,1024]{1,0:T(8,128)(2,1)S(1)} %get-tuple-element.9.left_ref, bf16[512,512]{1,0:T(8,128)(2,1)S(1)} %collective-permute-done.refs_0_, f32[8,2,512,2048]{3,2,1,0:T(8,128)} %correlate.5.refs_1_), custom_call_target="tpu_custom_call", output_to_operand_aliasing={{}: (3, {})} | custom-call | flops 1073741824 | bytes 16777216 | tf_op jit(solution)/shard_map/correlate/pallas_call | solution.py:242
  87.7 0.0 collective-permute-done.2.refs_0_
  87.7 6.9 %correlate.7 = f32[8,2,512,2048]{3,2,1,0:T(8,128)} custom-call(s32[1]{0:T(128)} %bitcast.place_ref, bf16[512,1024]{1,0:T(8,128)(2,1)S(1)} %get-tuple-element.9.left_ref, bf16[512,512]{1,0:T(8,128)(2,1)S(1)} %collective-permute-done.2.refs_0_, f32[8,2,512,2048]{3,2,1,0:T(8,128)} %correlate.6.refs_1_), custom_call_target="tpu_custom_call", output_to_operand_aliasing={{}: (3, {})} | custom-call | flops 1073741824 | bytes 16777216 | tf_op jit(solution)/shard_map/correlate/pallas_call | solution.py:242
Async XLA Ops:
  65.2 8.5 %collective-permute-start.1 = (bf16[512,512]{1,0:T(8,128)(2,1)S(1)}, bf16[512,512]{1,0:T(8,128)(2,1)S(1)}, u32[]{:S(2)}, u32[]{:S(2)}) collective-permute-start(bf16[512,512]{1,0:T(8,128)(2,1)S(1)} %get-tuple-element.10.refs_0_), channel_id=1, source_target_pairs={{0,2},{2,0},{1,3},{3,1},{4,6},{6,4},{5,7},{7,5},{8,10},{10,8},{9,1... | collective-permute-start | bytes 1572872 | tf_op jit(solution)/shard_map/ppermute | solution.py:293
  65.3 15.3 %collective-permute-start = (bf16[512,512]{1,0:T(8,128)(2,1)S(1)}, bf16[512,512]{1,0:T(8,128)(2,1)S(1)}, u32[]{:S(2)}, u32[]{:S(2)}) collective-permute-start(bf16[512,512]{1,0:T(8,128)(2,1)S(1)} %get-tuple-element.10.refs_0_), channel_id=1, source_target_pairs={{0,1},{1,0},{2,3},{3,2},{4,5},{5,4},{6,7},{7,6},{8,9},{9,8},{10,11... | collective-permute-start | bytes 1572872 | tf_op jit(solution)/shard_map/ppermute | solution.py:293
  80.7 7.0 %collective-permute-start.2 = (bf16[512,512]{1,0:T(8,128)(2,1)S(1)}, bf16[512,512]{1,0:T(8,128)(2,1)S(1)}, u32[]{:S(2)}, u32[]{:S(2)}) collective-permute-start(bf16[512,512]{1,0:T(8,128)(2,1)S(1)} %collective-permute-done.refs_0_), channel_id=1, source_target_pairs={{0,2},{2,0},{1,3},{3,1},{4,6},{6,4},{5,7},{7,5},{8,10},{10,8},{9,1... | collective-permute-start | bytes 1572872 | tf_op jit(solution)/shard_map/ppermute | solution.py:293

commit v4 on v3

--- a/solution.py
+++ b/solution.py
@@ -40,7 +40,7 @@
         (blocks[t] - high[t].astype(np.float64)).astype(np.float32).astype(ml_dtypes.bfloat16)
         for t in low_order
     ]
-    return np.ascontiguousarray(np.concatenate([high[t] for t in order] + low, axis=1).T)
+    return np.concatenate([high[t] for t in order] + low, axis=1)
 
 
 def peer(me, step, length, way):
@@ -49,33 +49,30 @@
     return me ^ step
 
 
-def filter_kernel(volt_ref, table_hbm, gain_ref, out_ref, sums, low_sums, table, arrived):
+def filter_kernel(volt_ref, table_hbm, gain_ref, out_ref, sums, table, arrived):
     frame, part = pl.program_id(0), pl.program_id(1)
-    rows = sums.shape[2]
-    half = gain_ref.shape[1]
-    width = 2 * half
+    width = sums.shape[3]
+    half = width // 2
     pieces = arrived.shape[0]
-    depth = table.shape[1] // pieces
+    depth = table.shape[0] // pieces
     order, low_order = tap_order()
-    here = pl.ds(pl.multiple_of(frame * width, width), len(order) * width)
-    low_here = pl.ds(pl.multiple_of(frame * width, width), len(low_order) * width)
 
     def fetch(piece):
-        columns = pl.ds(piece * depth, depth)
-        return pltpu.make_async_copy(
-            table_hbm.at[:, columns], table.at[:, columns], arrived.at[piece]
-        )
+        rows = pl.ds(piece * depth, depth)
+        return pltpu.make_async_copy(table_hbm.at[rows, :], table.at[rows, :], arrived.at[piece])
 
     def add(start, size):
-        before = jnp.concatenate([sums[part, here, :], low_sums[part, low_here, :]], axis=0)
-        after = before + lax.dot_general(
-            table[:, start : start + size],
+        product = jnp.dot(
             volt_ref[0, :, start : start + size],
-            (((1,), (1,)), ((), ())),
+            table[start : start + size, :],
             preferred_element_type=jnp.float32,
         )
-        sums[part, here, :] = after[: len(order) * width]
-        low_sums[part, low_here, :] = after[len(order) * width :]
+        for at, tap in enumerate(order):
+            value = product[:, at * width : (at + 1) * width]
+            if tap in low_order:
+                low = (len(order) + low_order.index(tap)) * width
+                value = value + product[:, low : low + width]
+            sums[frame + at, part] += value
 
     first = (frame == 0) & (part == 0)
 
@@ -84,26 +81,23 @@
         for piece in range(pieces):
             fetch(piece).start()
         sums[...] = jnp.zeros_like(sums)
-        low_sums[...] = jnp.zeros_like(low_sums)
         for piece in range(pieces):
             fetch(piece).wait()
             add(piece * depth, depth)
 
     @pl.when(jnp.logical_not(first))
     def _():
-        add(0, table.shape[1])
+        add(0, table.shape[0])
 
     @pl.when((frame == pl.num_programs(0) - 1) & (part == 1))
     def _():
         owners = out_ref.shape[0]
         share = half // owners
-        for slot in range(sums.shape[1] // width):
-            both = [sums[c, slot * width : (slot + 1) * width, :] for c in range(2)]
-            at = (slot - order.index(low_order[0])) * width
-            if 0 <= at < low_sums.shape[1]:
-                both = [both[c] + low_sums[c, at : at + width, :] for c in range(2)]
-            real = both[0][:half] + both[1][half:]
-            imag = both[1][:half] - both[0][half:]
+        lane = lax.broadcasted_iota(jnp.int32, sums.shape[2:], 1)
+        for slot in range(sums.shape[0]):
+            first_part, second = sums[slot, 0], pltpu.roll(sums[slot, 1], half, 1)
+            raw = jnp.where(lane < half, second + first_part, second - first_part).T
+            real, imag = raw[:half], raw[half:]
             out_real = gain_ref[0] * real - gain_ref[1] * imag
             out_imag = gain_ref[0] * imag + gain_ref[1] * real
             for owner in range(owners):
@@ -120,9 +114,8 @@
     frames = voltages.shape[2] // NFFT
     half = gains.shape[1]
     slots = frames + TAPS - 1
-    low_slots = frames + len(tap_order()[1]) - 1
     out_rows = slots * 2 * half // owners
-    columns = table.shape[0]
+    columns = table.shape[1]
     pieces = 4
     return pl.pallas_call(
         filter_kernel,
@@ -135,9 +128,8 @@
         out_specs=pl.BlockSpec((owners, out_rows, rows), lambda f, c: (0, 0, 0)),
         out_shape=jax.ShapeDtypeStruct((owners, out_rows, rows), jnp.bfloat16),
         scratch_shapes=[
-            pltpu.VMEM((2, slots * 2 * half, rows), jnp.float32),
-            pltpu.VMEM((2, low_slots * 2 * half, rows), jnp.float32),
-            pltpu.VMEM((columns, NFFT), jnp.bfloat16),
+            pltpu.VMEM((slots, 2, rows, 2 * half), jnp.float32),
+            pltpu.VMEM((NFFT, columns), jnp.bfloat16),
             pltpu.SemaphoreType.DMA((pieces,)),
         ],
         compiler_params=pltpu.CompilerParams(vmem_limit_bytes=VMEM),

time: 94.8 us -> 96.5 us (1.018)
  Pallas kernels: 62.2 us -> 63.9 us
    pallas_call x1, Pallas kernels: 33.5 us -> 35.2 us  [filter_all(): pl.pallas_call(filter_kernel, grid=(frames, 2), in_specs=[pl.BlockSpec((1...]
  transfers between devices with their start and end apart: 3 -> 3, of which waited for: 0 -> 0; matrix products, arithmetic and copies ran while one was open for 0% -> 0% of each run, Pallas kernels for 22% -> 21%
where the time goes in v4:
time: 96.5 us; the launch traced here: 96.3 us
  Pallas kernels  63.9 us (66%)
  blocking collectives  30.6 us (32%)
  starting transfers between devices  1.82 us (2%)
    pallas_call x1, Pallas kernels, filter_all(): pl.pallas_call(filter_kernel, grid=(frames, 2), in_specs=[pl.BlockSpec((1...  35.2 us
    all_to_all x1, blocking collectives, body(): lax.all_to_all(partial, 'fgrp', split_axis=0, concat_axis=0, tiled=True)  30.6 us
    pallas_call x4, Pallas kernels, correlate(): pl.pallas_call(functools.partial(block_kernel, blocks), grid_spec=pltpu.P...  27.5 us
  transfers between devices with their start and end apart: 3, of which 0 were waited for; matrix products, arithmetic and copies ran while one was open for 0% of the time, Pallas kernels for 21%

profile of v4, /device:TPU:0, one launch (start us, length us, event | category | flops | bytes accessed | tf_op | source)
XLA Modules:
  0.0 96.3 jit_solution(17750190900059670646)
XLA Ops:
  0.0 35.2 %filter_all.1 = bf16[8,112,512]{2,1,0:T(8,128)(2,1)} custom-call(bf16[2,512,16384]{2,1,0:T(8,128)(2,1)} %volt_ref.1, bf16[4096,768]{1,0:T(8,128)(2,1)} %constant.12.clone.table_hbm, f32[2,64,512]{2,1,0:T(8,128)} %bitcast.5), custom_call_target="tpu_custom_call" | custom-call | flops 25769803776 | bytes 39845888 | tf_op jit(solution)/shard_map/filter_all/pallas_call | solution.py:120
  35.2 30.6 %all_to_all.5.in_ref = bf16[8,112,512]{2,1,0:T(8,128)(2,1)S(1)} all-to-all(bf16[8,112,512]{2,1,0:T(8,128)(2,1)} %filter_all.1), channel_id=1, replica_groups=mesh['fgrp'=8,'tile'=2,'pol'=2] {'fgrp'}, dimensions={0} | all-to-all | bytes 1835008 | tf_op jit(solution)/shard_map/all_to_all | solution.py:297
  65.8 1.1 %merge.1 = (bf16[512,512]{1,0:T(8,128)(2,1)S(1)}, bf16[512,1024]{1,0:T(8,128)(2,1)S(1)}) custom-call(bf16[8,112,512]{2,1,0:T(8,128)(2,1)S(1)} %all_to_all.5.in_ref), custom_call_target="tpu_custom_call" | custom-call | tf_op jit(solution)/shard_map/merge/pallas_call | solution.py:182
  66.9 0.1 collective-permute-start.1
  67.0 1.6 %collective-permute-start = (bf16[512,512]{1,0:T(8,128)(2,1)S(1)}, bf16[512,512]{1,0:T(8,128)(2,1)S(1)}, u32[]{:S(2)}, u32[]{:S(2)}) collective-permute-start(bf16[512,512]{1,0:T(8,128)(2,1)S(1)} %get-tuple-element.10.refs_0_), channel_id=1, source_target_pairs={{0,1},{1,0},{2,3},{3,2},{4,5},{5,4},{6,7},{7,6},{8,9},{9,8},{10,11... | collective-permute-start | bytes 1572872 | tf_op jit(solution)/shard_map/ppermute | solution.py:285
  68.6 6.9 %correlate.4.refs_1_ = f32[8,2,512,2048]{3,2,1,0:T(8,128)} custom-call(s32[1]{0:T(128)} %bitcast.3.place_ref, bf16[512,1024]{1,0:T(8,128)(2,1)S(1)} %get-tuple-element.9.left_ref, bf16[512,512]{1,0:T(8,128)(2,1)S(1)} %get-tuple-element.10.refs_0_), custom_call_target="tpu_custom_call" | custom-call | flops 1073741824 | bytes 16777216 | tf_op jit(solution)/shard_map/correlate/pallas_call | solution.py:234
  75.5 0.0 collective-permute-done.1.refs_0_
  75.5 6.9 %correlate.5.refs_1_ = f32[8,2,512,2048]{3,2,1,0:T(8,128)} custom-call(s32[1]{0:T(128)} %bitcast.2.place_ref, bf16[512,1024]{1,0:T(8,128)(2,1)S(1)} %get-tuple-element.9.left_ref, bf16[512,512]{1,0:T(8,128)(2,1)S(1)} %collective-permute-done.1.refs_0_, f32[8,2,512,2048]{3,2,1,0:T(8,128)} %correlate.4.refs_1_), custom_call_target="tpu_custom_call", output_to_operand_aliasing={{}: (3, {})} | custom-call | flops 1073741824 | bytes 16777216 | tf_op jit(solution)/shard_map/correlate/pallas_call | solution.py:234
  82.4 0.0 collective-permute-done.refs_0_
  82.4 0.2 collective-permute-start.2
  82.5 6.9 %correlate.6.refs_1_ = f32[8,2,512,2048]{3,2,1,0:T(8,128)} custom-call(s32[1]{0:T(128)} %bitcast.4.place_ref, bf16[512,1024]{1,0:T(8,128)(2,1)S(1)} %get-tuple-element.9.left_ref, bf16[512,512]{1,0:T(8,128)(2,1)S(1)} %collective-permute-done.refs_0_, f32[8,2,512,2048]{3,2,1,0:T(8,128)} %correlate.5.refs_1_), custom_call_target="tpu_custom_call", output_to_operand_aliasing={{}: (3, {})} | custom-call | flops 1073741824 | bytes 16777216 | tf_op jit(solution)/shard_map/correlate/pallas_call | solution.py:234
  89.4 0.0 collective-permute-done.2.refs_0_
  89.4 6.9 %correlate.7 = f32[8,2,512,2048]{3,2,1,0:T(8,128)} custom-call(s32[1]{0:T(128)} %bitcast.place_ref, bf16[512,1024]{1,0:T(8,128)(2,1)S(1)} %get-tuple-element.9.left_ref, bf16[512,512]{1,0:T(8,128)(2,1)S(1)} %collective-permute-done.2.refs_0_, f32[8,2,512,2048]{3,2,1,0:T(8,128)} %correlate.6.refs_1_), custom_call_target="tpu_custom_call", output_to_operand_aliasing={{}: (3, {})} | custom-call | flops 1073741824 | bytes 16777216 | tf_op jit(solution)/shard_map/correlate/pallas_call | solution.py:234
Async XLA Ops:
  66.9 8.6 %collective-permute-start.1 = (bf16[512,512]{1,0:T(8,128)(2,1)S(1)}, bf16[512,512]{1,0:T(8,128)(2,1)S(1)}, u32[]{:S(2)}, u32[]{:S(2)}) collective-permute-start(bf16[512,512]{1,0:T(8,128)(2,1)S(1)} %get-tuple-element.10.refs_0_), channel_id=1, source_target_pairs={{0,2},{2,0},{1,3},{3,1},{4,6},{6,4},{5,7},{7,5},{8,10},{10,8},{9,1... | collective-permute-start | bytes 1572872 | tf_op jit(solution)/shard_map/ppermute | solution.py:285
  67.0 15.4 %collective-permute-start = (bf16[512,512]{1,0:T(8,128)(2,1)S(1)}, bf16[512,512]{1,0:T(8,128)(2,1)S(1)}, u32[]{:S(2)}, u32[]{:S(2)}) collective-permute-start(bf16[512,512]{1,0:T(8,128)(2,1)S(1)} %get-tuple-element.10.refs_0_), channel_id=1, source_target_pairs={{0,1},{1,0},{2,3},{3,2},{4,5},{5,4},{6,7},{7,6},{8,9},{9,8},{10,11... | collective-permute-start | bytes 1572872 | tf_op jit(solution)/shard_map/ppermute | solution.py:285
  82.4 7.0 %collective-permute-start.2 = (bf16[512,512]{1,0:T(8,128)(2,1)S(1)}, bf16[512,512]{1,0:T(8,128)(2,1)S(1)}, u32[]{:S(2)}, u32[]{:S(2)}) collective-permute-start(bf16[512,512]{1,0:T(8,128)(2,1)S(1)} %collective-permute-done.refs_0_), channel_id=1, source_target_pairs={{0,2},{2,0},{1,3},{3,1},{4,6},{6,4},{5,7},{7,5},{8,10},{10,8},{9,1... | collective-permute-start | bytes 1572872 | tf_op jit(solution)/shard_map/ppermute | solution.py:285

commit v5 on v4

--- a/solution.py
+++ b/solution.py
@@ -49,64 +49,36 @@
     return me ^ step
 
 
-def filter_kernel(volt_ref, table_hbm, gain_ref, out_ref, sums, table, arrived):
-    frame, part = pl.program_id(0), pl.program_id(1)
-    width = sums.shape[3]
-    half = width // 2
-    pieces = arrived.shape[0]
-    depth = table.shape[0] // pieces
+def combine_kernel(*refs):
+    product_refs, gain_ref, out_ref = refs[:-2], refs[-2], refs[-1]
+    half = gain_ref.shape[1]
+    width = 2 * half
+    owners = out_ref.shape[0]
+    share = half // owners
     order, low_order = tap_order()
-
-    def fetch(piece):
-        rows = pl.ds(piece * depth, depth)
-        return pltpu.make_async_copy(table_hbm.at[rows, :], table.at[rows, :], arrived.at[piece])
-
-    def add(start, size):
-        product = jnp.dot(
-            volt_ref[0, :, start : start + size],
-            table[start : start + size, :],
-            preferred_element_type=jnp.float32,
-        )
-        for at, tap in enumerate(order):
-            value = product[:, at * width : (at + 1) * width]
-            if tap in low_order:
-                low = (len(order) + low_order.index(tap)) * width
-                value = value + product[:, low : low + width]
-            sums[frame + at, part] += value
-
-    first = (frame == 0) & (part == 0)
-
-    @pl.when(first)
-    def _():
-        for piece in range(pieces):
-            fetch(piece).start()
-        sums[...] = jnp.zeros_like(sums)
-        for piece in range(pieces):
-            fetch(piece).wait()
-            add(piece * depth, depth)
-
-    @pl.when(jnp.logical_not(first))
-    def _():
-        add(0, table.shape[0])
-
-    @pl.when((frame == pl.num_programs(0) - 1) & (part == 1))
-    def _():
-        owners = out_ref.shape[0]
-        share = half // owners
-        lane = lax.broadcasted_iota(jnp.int32, sums.shape[2:], 1)
-        for slot in range(sums.shape[0]):
-            first_part, second = sums[slot, 0], pltpu.roll(sums[slot, 1], half, 1)
-            raw = jnp.where(lane < half, second + first_part, second - first_part).T
-            real, imag = raw[:half], raw[half:]
-            out_real = gain_ref[0] * real - gain_ref[1] * imag
-            out_imag = gain_ref[0] * imag + gain_ref[1] * real
-            for owner in range(owners):
-                at = owner * share
-                pair = jnp.concatenate(
-                    [out_real[at : at + share], out_imag[at : at + share]], axis=0
-                )
-                at = 2 * share * slot
-                out_ref[owner, at : at + 2 * share, :] = pair.astype(jnp.bfloat16)
+    frames = len(product_refs)
+
+    def term(frame, at, part):
+        value = product_refs[frame][part, :, at * width : (at + 1) * width]
+        if order[at] in low_order:
+            low = (len(order) + low_order.index(order[at])) * width
+            value = value + product_refs[frame][part, :, low : low + width]
+        return value
+
+    lane = lax.broadcasted_iota(jnp.int32, (product_refs[0].shape[1], width), 1)
+    for slot in range(frames + TAPS - 1):
+        used = [f for f in range(frames) if 0 <= slot - f < TAPS]
+        first, second = (sum(term(f, slot - f, part) for f in used) for part in range(2))
+        second = pltpu.roll(second, half, 1)
+        raw = jnp.where(lane < half, second + first, second - first).T
+        real, imag = raw[:half], raw[half:]
+        out_real = gain_ref[0] * real - gain_ref[1] * imag
+        out_imag = gain_ref[0] * imag + gain_ref[1] * real
+        for owner in range(owners):
+            at = owner * share
+            pair = jnp.concatenate([out_real[at : at + share], out_imag[at : at + share]], axis=0)
+            at = 2 * share * slot
+            out_ref[owner, at : at + 2 * share, :] = pair.astype(jnp.bfloat16)
 
 
 def filter_all(voltages, table, gains, owners):
@@ -115,31 +87,22 @@
     half = gains.shape[1]
     slots = frames + TAPS - 1
     out_rows = slots * 2 * half // owners
-    columns = table.shape[1]
-    pieces = 4
-    return pl.pallas_call(
-        filter_kernel,
-        grid=(frames, 2),
-        in_specs=[
-            pl.BlockSpec((1, rows, NFFT), lambda f, c: (c, 0, f)),
-            pl.BlockSpec(memory_space=pl.ANY),
-            pl.BlockSpec((2, half, rows), lambda f, c: (0, 0, 0)),
-        ],
-        out_specs=pl.BlockSpec((owners, out_rows, rows), lambda f, c: (0, 0, 0)),
+    products = [
+        lax.dot_general(
+            voltages[:, :, frame * NFFT : (frame + 1) * NFFT],
+            table,
+            (((2,), (0,)), ((), ())),
+            preferred_element_type=jnp.float32,
+        )
+        for frame in range(frames)
+    ]
+    return pl.pallas_call(
+        combine_kernel,
+        in_specs=[pl.BlockSpec(memory_space=pltpu.VMEM)] * (frames + 1),
         out_shape=jax.ShapeDtypeStruct((owners, out_rows, rows), jnp.bfloat16),
-        scratch_shapes=[
-            pltpu.VMEM((slots, 2, rows, 2 * half), jnp.float32),
-            pltpu.VMEM((NFFT, columns), jnp.bfloat16),
-            pltpu.SemaphoreType.DMA((pieces,)),
-        ],
-        compiler_params=pltpu.CompilerParams(vmem_limit_bytes=VMEM),
-        cost_estimate=pl.CostEstimate(
-            flops=2 * 2 * rows * frames * NFFT * columns,
-            bytes_accessed=2 * (2 * rows * frames * NFFT + NFFT * columns),
-            transcendentals=0,
-        ),
-        name="filter_all",
-    )(voltages, table, gains)
+        compiler_params=pltpu.CompilerParams(vmem_limit_bytes=24 * 2**20),
+        name="combine",
+    )(*products, gains)
 
 
 def merge_kernel(frames, share, norm, in_ref, out_ref, left_ref, scratch):

time: 96.5 us -> 102 us (1.057)
  matrix products: 0 us -> 39.7 us
  Pallas kernels: 63.9 us -> 30.1 us
    dot_general x0 -> x4, matrix products: none -> 39.7 us  [filter_all(): lax.dot_general(voltages[:, :, frame * NFFT:(frame + 1) * NFFT], table, (...]
    pallas_call x1, Pallas kernels: 35.2 us -> 1.43 us  [filter_all(): pl.pallas_call(combine_kernel, in_specs=[pl.BlockSpec(memory_space=pltpu....]
  transfers between devices with their start and end apart: 3 -> 3, of which waited for: 0 -> 0; matrix products, arithmetic and copies ran while one was open for 0% -> 0% of each run, Pallas kernels for 21% -> 20%
where the time goes in v5:
time: 102 us; the launch traced here: 101 us
  matrix products  39.7 us (39%)
  Pallas kernels  30.1 us (30%)
  blocking collectives  29.7 us (29%)
  starting transfers between devices  1.84 us (2%)
    dot_general x4, matrix products, filter_all(): lax.dot_general(voltages[:, :, frame * NFFT:(frame + 1) * NFFT], table, (...  39.7 us
    all_to_all x1, blocking collectives, body(): lax.all_to_all(partial, 'fgrp', split_axis=0, concat_axis=0, tiled=True)  29.7 us
    pallas_call x4, Pallas kernels, correlate(): pl.pallas_call(functools.partial(block_kernel, blocks), grid_spec=pltpu.P...  27.5 us
  transfers between devices with their start and end apart: 3, of which 0 were waited for; matrix products, arithmetic and copies ran while one was open for 0% of the time, Pallas kernels for 20%

profile of v5, /device:TPU:0, one launch (start us, length us, event | category | flops | bytes accessed | tf_op | source)
XLA Modules:
  0.0 101.4 jit_solution(10933721112316202357)
XLA Ops:
  0.0 0.0 slice-start
  0.0 0.0 slice-start.1
  0.0 11.8 %fusion.11.refs_1_ = f32[2,512,768]{2,1,0:T(8,128)S(1)} fusion(bf16[4096,768,1]{0,1,2:T(8,128)(2,1)} %constant.13, bf16[2,512,16384]{2,1,0:T(8,128)(2,1)} %param.3), kind=kOutput, calls=%fused_computation.9 | convolution fusion | flops 6442450944 | bytes 17825792 | tf_op jit(solution)/shard_map/dot_general | solution.py:91
  11.9 0.0 slice-done
  11.9 0.0 slice-done.1
  11.9 9.2 %fusion.8.refs_0_ = f32[2,512,768]{2,1,0:T(8,128)S(1)} fusion(bf16[4096,768,1]{0,1,2:T(8,128)(2,1)S(1)} %bitcast.20, bf16[2,512,16384]{2,1,0:T(8,128)(2,1)} %param.3), kind=kOutput, calls=%fused_computation.8 | convolution fusion | flops 6442450944 | bytes 17825792 | tf_op jit(solution)/shard_map/dot_general | solution.py:91
  21.1 9.2 %fusion.17.refs_3_ = f32[2,512,768]{2,1,0:T(8,128)S(1)} fusion(bf16[4096,768,1]{0,1,2:T(8,128)(2,1)S(1)} %bitcast.20, bf16[2,512,16384]{2,1,0:T(8,128)(2,1)} %param.3), kind=kOutput, calls=%fused_computation.11 | convolution fusion | flops 6442450944 | bytes 17825792 | tf_op jit(solution)/shard_map/dot_general | solution.py:91
  30.3 0.0 copy-start
  30.3 9.4 %fusion.14.refs_2_ = f32[2,512,768]{2,1,0:T(8,128)S(1)} fusion(bf16[4096,768,1]{0,1,2:T(8,128)(2,1)S(1)} %bitcast.20, bf16[2,512,16384]{2,1,0:T(8,128)(2,1)} %param.3), kind=kOutput, calls=%fused_computation.10 | convolution fusion | flops 6442450944 | bytes 17825792 | tf_op jit(solution)/shard_map/dot_general | solution.py:91
  39.8 0.0 copy-done
  39.8 1.4 %combine.1 = bf16[8,112,512]{2,1,0:T(8,128)(2,1)S(1)} custom-call(f32[2,512,768]{2,1,0:T(8,128)S(1)} %fusion.8.refs_0_, f32[2,512,768]{2,1,0:T(8,128)S(1)} %fusion.11.refs_1_, f32[2,512,768]{2,1,0:T(8,128)S(1)} %fusion.14.refs_2_, f32[2,512,768]{2,1,0:T(8,128)S(1)} %fusion.17.refs_3_, f32[2,64,512]{2,1,0:T(8,128)S(1)} %bitcast.18), custom_call_target="tpu_custom_call" | custom-call | tf_op jit(solution)/shard_map/combine/pallas_call | solution.py:99
  41.2 29.7 %all_to_all.5.in_ref = bf16[8,112,512]{2,1,0:T(8,128)(2,1)S(1)} all-to-all(bf16[8,112,512]{2,1,0:T(8,128)(2,1)S(1)} %combine.1), channel_id=1, replica_groups=mesh['fgrp'=8,'tile'=2,'pol'=2] {'fgrp'}, dimensions={0} | all-to-all | bytes 1835008 | tf_op jit(solution)/shard_map/all_to_all | solution.py:260
  70.9 1.1 %merge.1 = (bf16[512,512]{1,0:T(8,128)(2,1)S(1)}, bf16[512,1024]{1,0:T(8,128)(2,1)S(1)}) custom-call(bf16[8,112,512]{2,1,0:T(8,128)(2,1)S(1)} %all_to_all.5.in_ref), custom_call_target="tpu_custom_call" | custom-call | tf_op jit(solution)/shard_map/merge/pallas_call | solution.py:145
  72.0 0.1 collective-permute-start.1
  72.1 1.6 %collective-permute-start = (bf16[512,512]{1,0:T(8,128)(2,1)S(1)}, bf16[512,512]{1,0:T(8,128)(2,1)S(1)}, u32[]{:S(2)}, u32[]{:S(2)}) collective-permute-start(bf16[512,512]{1,0:T(8,128)(2,1)S(1)} %get-tuple-element.10.refs_0_), channel_id=1, source_target_pairs={{0,1},{1,0},{2,3},{3,2},{4,5},{5,4},{6,7},{7,6},{8,9},{9,8},{10,11... | collective-permute-start | bytes 1572872 | tf_op jit(solution)/shard_map/ppermute | solution.py:248
  73.7 6.9 %correlate.4.refs_1_ = f32[8,2,512,2048]{3,2,1,0:T(8,128)} custom-call(s32[1]{0:T(128)} %bitcast.8.place_ref, bf16[512,1024]{1,0:T(8,128)(2,1)S(1)} %get-tuple-element.9.left_ref, bf16[512,512]{1,0:T(8,128)(2,1)S(1)} %get-tuple-element.10.refs_0_), custom_call_target="tpu_custom_call" | custom-call | flops 1073741824 | bytes 16777216 | tf_op jit(solution)/shard_map/correlate/pallas_call | solution.py:197
  80.6 0.0 collective-permute-done.1.refs_0_
  80.6 6.9 %correlate.5.refs_1_ = f32[8,2,512,2048]{3,2,1,0:T(8,128)} custom-call(s32[1]{0:T(128)} %bitcast.7.place_ref, bf16[512,1024]{1,0:T(8,128)(2,1)S(1)} %get-tuple-element.9.left_ref, bf16[512,512]{1,0:T(8,128)(2,1)S(1)} %collective-permute-done.1.refs_0_, f32[8,2,512,2048]{3,2,1,0:T(8,128)} %correlate.4.refs_1_), custom_call_target="tpu_custom_call", output_to_operand_aliasing={{}: (3, {})} | custom-call | flops 1073741824 | bytes 16777216 | tf_op jit(solution)/shard_map/correlate/pallas_call | solution.py:197
  87.5 0.0 collective-permute-done.refs_0_
  87.5 0.2 collective-permute-start.2
  87.6 6.9 %correlate.6.refs_1_ = f32[8,2,512,2048]{3,2,1,0:T(8,128)} custom-call(s32[1]{0:T(128)} %bitcast.9.place_ref, bf16[512,1024]{1,0:T(8,128)(2,1)S(1)} %get-tuple-element.9.left_ref, bf16[512,512]{1,0:T(8,128)(2,1)S(1)} %collective-permute-done.refs_0_, f32[8,2,512,2048]{3,2,1,0:T(8,128)} %correlate.5.refs_1_), custom_call_target="tpu_custom_call", output_to_operand_aliasing={{}: (3, {})} | custom-call | flops 1073741824 | bytes 16777216 | tf_op jit(solution)/shard_map/correlate/pallas_call | solution.py:197
  94.5 0.0 collective-permute-done.2.refs_0_
  94.5 6.9 %correlate.7 = f32[8,2,512,2048]{3,2,1,0:T(8,128)} custom-call(s32[1]{0:T(128)} %bitcast.place_ref, bf16[512,1024]{1,0:T(8,128)(2,1)S(1)} %get-tuple-element.9.left_ref, bf16[512,512]{1,0:T(8,128)(2,1)S(1)} %collective-permute-done.2.refs_0_, f32[8,2,512,2048]{3,2,1,0:T(8,128)} %correlate.6.refs_1_), custom_call_target="tpu_custom_call", output_to_operand_aliasing={{}: (3, {})} | custom-call | flops 1073741824 | bytes 16777216 | tf_op jit(solution)/shard_map/correlate/pallas_call | solution.py:197
  (1 shorter events, 0.0 us)
Async XLA Ops:
  0.0 11.9 %slice-start = ((s8[6291456]{0:T(1024)(128)(4,1)}), s8[4194304]{0:T(1024)(128)(4,1)S(1)}, s32[]{:S(2)}) async-start(s8[6291456]{0:T(1024)(128)(4,1)} %bitcast.19), calls=%async_computation.1 | async-start | bytes 8388608
  0.0 11.9 %slice-start.1 = ((s8[6291456]{0:T(1024)(128)(4,1)}), s8[2097152]{0:T(1024)(128)(4,1)S(1)}, s32[]{:S(2)}) async-start(s8[6291456]{0:T(1024)(128)(4,1)} %bitcast.19), calls=%async_computation.2 | async-start | bytes 4194304
  30.3 9.4 %copy-start = (f32[2,512,64]{1,2,0:T(8,128)S(1)}, f32[2,512,64]{1,2,0:T(8,128)}, u32[]{:S(2)}) copy-start(f32[2,512,64]{1,2,0:T(8,128)} %param.4) | copy-start | bytes 786436
  72.0 8.6 %collective-permute-start.1 = (bf16[512,512]{1,0:T(8,128)(2,1)S(1)}, bf16[512,512]{1,0:T(8,128)(2,1)S(1)}, u32[]{:S(2)}, u32[]{:S(2)}) collective-permute-start(bf16[512,512]{1,0:T(8,128)(2,1)S(1)} %get-tuple-element.10.refs_0_), channel_id=1, source_target_pairs={{0,2},{2,0},{1,3},{3,1},{4,6},{6,4},{5,7},{7,5},{8,10},{10,8},{9,1... | collective-permute-start | bytes 1572872 | tf_op jit(solution)/shard_map/ppermute | solution.py:248
  72.1 15.4 %collective-permute-start = (bf16[512,512]{1,0:T(8,128)(2,1)S(1)}, bf16[512,512]{1,0:T(8,128)(2,1)S(1)}, u32[]{:S(2)}, u32[]{:S(2)}) collective-permute-start(bf16[512,512]{1,0:T(8,128)(2,1)S(1)} %get-tuple-element.10.refs_0_), channel_id=1, source_target_pairs={{0,1},{1,0},{2,3},{3,2},{4,5},{5,4},{6,7},{7,6},{8,9},{9,8},{10,11... | collective-permute-start | bytes 1572872 | tf_op jit(solution)/shard_map/ppermute | solution.py:248
  87.5 7.1 %collective-permute-start.2 = (bf16[512,512]{1,0:T(8,128)(2,1)S(1)}, bf16[512,512]{1,0:T(8,128)(2,1)S(1)}, u32[]{:S(2)}, u32[]{:S(2)}) collective-permute-start(bf16[512,512]{1,0:T(8,128)(2,1)S(1)} %collective-permute-done.refs_0_), channel_id=1, source_target_pairs={{0,2},{2,0},{1,3},{3,1},{4,6},{6,4},{5,7},{7,5},{8,10},{10,8},{9,1... | collective-permute-start | bytes 1572872 | tf_op jit(solution)/shard_map/ppermute | solution.py:248

commit v6 on v3

--- a/solution.py
+++ b/solution.py
@@ -36,11 +36,11 @@
     transform = np.concatenate([np.cos(angles), np.sin(angles)], axis=1) / math.sqrt(NFFT)
     blocks = {t: filter_taps()[t][:, None] * transform for t in order}
     high = {t: b.astype(np.float32).astype(ml_dtypes.bfloat16) for t, b in blocks.items()}
-    low = [
-        (blocks[t] - high[t].astype(np.float64)).astype(np.float32).astype(ml_dtypes.bfloat16)
-        for t in low_order
-    ]
-    return np.ascontiguousarray(np.concatenate([high[t] for t in order] + low, axis=1).T)
+    low = np.concatenate([blocks[t] - high[t].astype(np.float64) for t in low_order], axis=1)
+    scale = 2.0 ** np.floor(np.log2(256.0 / np.abs(low).max()))
+    low = (low * scale).astype(np.float32).astype(ml_dtypes.float8_e4m3fn)
+    high = np.concatenate([high[t] for t in order], axis=1)
+    return np.ascontiguousarray(high.T), np.ascontiguousarray(low.T), float(1.0 / scale)
 
 
 def peer(me, step, length, way):
@@ -49,7 +49,9 @@
     return me ^ step
 
 
-def filter_kernel(volt_ref, table_hbm, gain_ref, out_ref, sums, low_sums, table, arrived):
+def filter_kernel(
+    low_scale, volt_ref, table_hbm, low_ref, gain_ref, out_ref, sums, low_sums, table, arrived
+):
     frame, part = pl.program_id(0), pl.program_id(1)
     rows = sums.shape[2]
     half = gain_ref.shape[1]
@@ -66,16 +68,17 @@
             table_hbm.at[:, columns], table.at[:, columns], arrived.at[piece]
         )
 
+    def product(left, right):
+        return lax.dot_general(
+            left, right, (((1,), (1,)), ((), ())), preferred_element_type=jnp.float32
+        )
+
     def add(start, size):
-        before = jnp.concatenate([sums[part, here, :], low_sums[part, low_here, :]], axis=0)
-        after = before + lax.dot_general(
-            table[:, start : start + size],
-            volt_ref[0, :, start : start + size],
-            (((1,), (1,)), ((), ())),
-            preferred_element_type=jnp.float32,
+        volts = volt_ref[0, :, start : start + size]
+        sums[part, here, :] += product(table[:, start : start + size], volts)
+        low_sums[part, low_here, :] += product(
+            low_ref[:, start : start + size], volts.astype(jnp.float8_e4m3fn)
         )
-        sums[part, here, :] = after[: len(order) * width]
-        low_sums[part, low_here, :] = after[len(order) * width :]
 
     first = (frame == 0) & (part == 0)
 
@@ -101,7 +104,7 @@
             both = [sums[c, slot * width : (slot + 1) * width, :] for c in range(2)]
             at = (slot - order.index(low_order[0])) * width
             if 0 <= at < low_sums.shape[1]:
-                both = [both[c] + low_sums[c, at : at + width, :] for c in range(2)]
+                both = [both[c] + low_scale * low_sums[c, at : at + width, :] for c in range(2)]
             real = both[0][:half] + both[1][half:]
             imag = both[1][:half] - both[0][half:]
             out_real = gain_ref[0] * real - gain_ref[1] * imag
@@ -115,21 +118,23 @@
                 out_ref[owner, at : at + 2 * share, :] = pair.astype(jnp.bfloat16)
 
 
-def filter_all(voltages, table, gains, owners):
+def filter_all(voltages, tables, gains, owners):
     rows = voltages.shape[1]
     frames = voltages.shape[2] // NFFT
     half = gains.shape[1]
     slots = frames + TAPS - 1
     low_slots = frames + len(tap_order()[1]) - 1
     out_rows = slots * 2 * half // owners
+    table, low_table, low_scale = tables
     columns = table.shape[0]
     pieces = 4
     return pl.pallas_call(
-        filter_kernel,
+        functools.partial(filter_kernel, low_scale),
         grid=(frames, 2),
         in_specs=[
             pl.BlockSpec((1, rows, NFFT), lambda f, c: (c, 0, f)),
             pl.BlockSpec(memory_space=pl.ANY),
+            pl.BlockSpec(low_table.shape, lambda f, c: (0, 0)),
             pl.BlockSpec((2, half, rows), lambda f, c: (0, 0, 0)),
         ],
         out_specs=pl.BlockSpec((owners, out_rows, rows), lambda f, c: (0, 0, 0)),
@@ -147,7 +152,7 @@
             transcendentals=0,
         ),
         name="filter_all",
-    )(voltages, table, gains)
+    )(voltages, jnp.asarray(table), jnp.asarray(low_table), gains)
 
 
 def merge_kernel(frames, share, norm, in_ref, out_ref, left_ref, scratch):
@@ -300,8 +305,7 @@
     owners = lax.axis_size("fgrp")
     share = channels // owners
     norm = 1.0 / math.sqrt(frames_here * owners)
-    table = jnp.asarray(filter_table(channels))
-    partial = filter_all(voltages, table, jnp.swapaxes(gains, 1, 2), owners)
+    partial = filter_all(voltages, filter_table(channels), jnp.swapaxes(gains, 1, 2), owners)
     turned = lax.all_to_all(partial, "fgrp", split_axis=0, concat_axis=0, tiled=True)
     own, left = merge(turned, frames_here, share, norm)
     tiles, pols = lax.axis_size("tile"), lax.axis_size("pol")

time: 94.8 us -> 90.9 us (0.959)
  Pallas kernels: 62.2 us -> 58.2 us
    pallas_call x1, Pallas kernels: 33.5 us -> 29.6 us  [filter_all(): pl.pallas_call(functools.partial(filter_kernel, low_scale), grid=(frames,...]
  transfers between devices with their start and end apart: 3 -> 3, of which waited for: 0 -> 0; matrix products, arithmetic and copies ran while one was open for 0% -> 0% of each run, Pallas kernels for 22% -> 23%
where the time goes in v6:
time: 90.9 us; the launch traced here: 90.7 us
  Pallas kernels  58.2 us (64%)
  blocking collectives  30.6 us (34%)
  starting transfers between devices  1.82 us (2%)
    all_to_all x1, blocking collectives, body(): lax.all_to_all(partial, 'fgrp', split_axis=0, concat_axis=0, tiled=True)  30.6 us
    pallas_call x1, Pallas kernels, filter_all(): pl.pallas_call(functools.partial(filter_kernel, low_scale), grid=(frames,...  29.6 us
    pallas_call x4, Pallas kernels, correlate(): pl.pallas_call(functools.partial(block_kernel, blocks), grid_spec=pltpu.P...  27.5 us
    ppermute x3, starting transfers between devices, swapped(): lax.ppermute(shard, axis, [(i, peer(i, step, length, 1)) for i in range(l...  1.82 us
  transfers between devices with their start and end apart: 3, of which 0 were waited for; matrix products, arithmetic and copies ran while one was open for 0% of the time, Pallas kernels for 23%

profile of v6, /device:TPU:0, one launch (start us, length us, event | category | flops | bytes accessed | tf_op | source)
XLA Modules:
  0.0 90.7 jit_solution(1755357562105493554)
XLA Ops:
  0.0 29.6 %filter_all.1 = bf16[8,112,512]{2,1,0:T(8,128)(2,1)} custom-call(bf16[2,512,16384]{2,1,0:T(8,128)(2,1)} %volt_ref.1, bf16[512,4096]{1,0:T(8,128)(2,1)} %constant.14.clone.table_hbm, f8e4m3fn[256,4096]{1,0:T(32,128)(4,1)} %constant.15.clone.low_ref, f32[2,64,512]{2,1,0:T(8,128)} %bitcast.5), custom_call_target="tpu_custom_call" | custom-call | flops 17179869184 | bytes 37748736 | tf_op jit(solution)/shard_map/filter_all/pallas_call | solution.py:131
  29.6 30.6 %all_to_all.5.in_ref = bf16[8,112,512]{2,1,0:T(8,128)(2,1)S(1)} all-to-all(bf16[8,112,512]{2,1,0:T(8,128)(2,1)} %filter_all.1), channel_id=1, replica_groups=mesh['fgrp'=8,'tile'=2,'pol'=2] {'fgrp'}, dimensions={0} | all-to-all | bytes 1835008 | tf_op jit(solution)/shard_map/all_to_all | solution.py:309
  60.2 1.1 %merge.1 = (bf16[512,512]{1,0:T(8,128)(2,1)S(1)}, bf16[512,1024]{1,0:T(8,128)(2,1)S(1)}) custom-call(bf16[8,112,512]{2,1,0:T(8,128)(2,1)S(1)} %all_to_all.5.in_ref), custom_call_target="tpu_custom_call" | custom-call | tf_op jit(solution)/shard_map/merge/pallas_call | solution.py:195
  61.3 0.1 collective-permute-start.1
  61.4 1.6 %collective-permute-start = (bf16[512,512]{1,0:T(8,128)(2,1)S(1)}, bf16[512,512]{1,0:T(8,128)(2,1)S(1)}, u32[]{:S(2)}, u32[]{:S(2)}) collective-permute-start(bf16[512,512]{1,0:T(8,128)(2,1)S(1)} %get-tuple-element.10.refs_0_), channel_id=1, source_target_pairs={{0,1},{1,0},{2,3},{3,2},{4,5},{5,4},{6,7},{7,6},{8,9},{9,8},{10,11... | collective-permute-start | bytes 1572872 | tf_op jit(solution)/shard_map/ppermute | solution.py:298
  63.0 6.9 %correlate.4.refs_1_ = f32[8,2,512,2048]{3,2,1,0:T(8,128)} custom-call(s32[1]{0:T(128)} %bitcast.3.place_ref, bf16[512,1024]{1,0:T(8,128)(2,1)S(1)} %get-tuple-element.9.left_ref, bf16[512,512]{1,0:T(8,128)(2,1)S(1)} %get-tuple-element.10.refs_0_), custom_call_target="tpu_custom_call" | custom-call | flops 1073741824 | bytes 16777216 | tf_op jit(solution)/shard_map/correlate/pallas_call | solution.py:247
  69.9 0.0 collective-permute-done.1.refs_0_
  69.9 6.9 %correlate.5.refs_1_ = f32[8,2,512,2048]{3,2,1,0:T(8,128)} custom-call(s32[1]{0:T(128)} %bitcast.2.place_ref, bf16[512,1024]{1,0:T(8,128)(2,1)S(1)} %get-tuple-element.9.left_ref, bf16[512,512]{1,0:T(8,128)(2,1)S(1)} %collective-permute-done.1.refs_0_, f32[8,2,512,2048]{3,2,1,0:T(8,128)} %correlate.4.refs_1_), custom_call_target="tpu_custom_call", output_to_operand_aliasing={{}: (3, {})} | custom-call | flops 1073741824 | bytes 16777216 | tf_op jit(solution)/shard_map/correlate/pallas_call | solution.py:247
  76.8 0.0 collective-permute-done.refs_0_
  76.8 0.2 collective-permute-start.2
  76.9 6.9 %correlate.6.refs_1_ = f32[8,2,512,2048]{3,2,1,0:T(8,128)} custom-call(s32[1]{0:T(128)} %bitcast.4.place_ref, bf16[512,1024]{1,0:T(8,128)(2,1)S(1)} %get-tuple-element.9.left_ref, bf16[512,512]{1,0:T(8,128)(2,1)S(1)} %collective-permute-done.refs_0_, f32[8,2,512,2048]{3,2,1,0:T(8,128)} %correlate.5.refs_1_), custom_call_target="tpu_custom_call", output_to_operand_aliasing={{}: (3, {})} | custom-call | flops 1073741824 | bytes 16777216 | tf_op jit(solution)/shard_map/correlate/pallas_call | solution.py:247
  83.8 0.0 collective-permute-done.2.refs_0_
  83.8 6.9 %correlate.7 = f32[8,2,512,2048]{3,2,1,0:T(8,128)} custom-call(s32[1]{0:T(128)} %bitcast.place_ref, bf16[512,1024]{1,0:T(8,128)(2,1)S(1)} %get-tuple-element.9.left_ref, bf16[512,512]{1,0:T(8,128)(2,1)S(1)} %collective-permute-done.2.refs_0_, f32[8,2,512,2048]{3,2,1,0:T(8,128)} %correlate.6.refs_1_), custom_call_target="tpu_custom_call", output_to_operand_aliasing={{}: (3, {})} | custom-call | flops 1073741824 | bytes 16777216 | tf_op jit(solution)/shard_map/correlate/pallas_call | solution.py:247
Async XLA Ops:
  61.3 8.6 %collective-permute-start.1 = (bf16[512,512]{1,0:T(8,128)(2,1)S(1)}, bf16[512,512]{1,0:T(8,128)(2,1)S(1)}, u32[]{:S(2)}, u32[]{:S(2)}) collective-permute-start(bf16[512,512]{1,0:T(8,128)(2,1)S(1)} %get-tuple-element.10.refs_0_), channel_id=1, source_target_pairs={{0,2},{2,0},{1,3},{3,1},{4,6},{6,4},{5,7},{7,5},{8,10},{10,8},{9,1... | collective-permute-start | bytes 1572872 | tf_op jit(solution)/shard_map/ppermute | solution.py:298
  61.4 15.4 %collective-permute-start = (bf16[512,512]{1,0:T(8,128)(2,1)S(1)}, bf16[512,512]{1,0:T(8,128)(2,1)S(1)}, u32[]{:S(2)}, u32[]{:S(2)}) collective-permute-start(bf16[512,512]{1,0:T(8,128)(2,1)S(1)} %get-tuple-element.10.refs_0_), channel_id=1, source_target_pairs={{0,1},{1,0},{2,3},{3,2},{4,5},{5,4},{6,7},{7,6},{8,9},{9,8},{10,11... | collective-permute-start | bytes 1572872 | tf_op jit(solution)/shard_map/ppermute | solution.py:298
  76.8 7.0 %collective-permute-start.2 = (bf16[512,512]{1,0:T(8,128)(2,1)S(1)}, bf16[512,512]{1,0:T(8,128)(2,1)S(1)}, u32[]{:S(2)}, u32[]{:S(2)}) collective-permute-start(bf16[512,512]{1,0:T(8,128)(2,1)S(1)} %collective-permute-done.refs_0_), channel_id=1, source_target_pairs={{0,2},{2,0},{1,3},{3,1},{4,6},{6,4},{5,7},{7,5},{8,10},{10,8},{9,1... | collective-permute-start | bytes 1572872 | tf_op jit(solution)/shard_map/ppermute | solution.py:298

commit v7 on v6

--- a/solution.py
+++ b/solution.py
@@ -59,7 +59,6 @@
     pieces = arrived.shape[0]
     depth = table.shape[1] // pieces
     order, low_order = tap_order()
-    here = pl.ds(pl.multiple_of(frame * width, width), len(order) * width)
     low_here = pl.ds(pl.multiple_of(frame * width, width), len(low_order) * width)
 
     def fetch(piece):
@@ -75,7 +74,9 @@
 
     def add(start, size):
         volts = volt_ref[0, :, start : start + size]
-        sums[part, here, :] += product(table[:, start : start + size], volts)
+        for at in range(0, table.shape[0], 2 * width):
+            to = pl.ds(pl.multiple_of(frame * width, width) + at, 2 * width)
+            sums[part, to, :] += product(table[at : at + 2 * width, start : start + size], volts)
         low_sums[part, low_here, :] += product(
             low_ref[:, start : start + size], volts.astype(jnp.float8_e4m3fn)
         )
@@ -235,7 +236,7 @@
     blocks = len(rights)
     out_rows, rows = rights[0].shape
     depth = out_rows // share
-    count = 2
+    count = 1
     operands = [places, left, *rights]
     specs = [pl.BlockSpec((rows, 2 * depth * count), lambda c, b, places: (0, c))]
     specs += [pl.BlockSpec((depth * count, rows), lambda c, b, places: (c, 0))] * blocks

time: 90.9 us -> 94.5 us (1.040)
  Pallas kernels: 58.2 us -> 61.8 us
    pallas_call x4, Pallas kernels: 27.5 us -> 31.2 us  [correlate(): pl.pallas_call(functools.partial(block_kernel, blocks), grid_spec=pltpu.P...]
  transfers between devices with their start and end apart: 3 -> 3, of which waited for: 0 -> 0; matrix products, arithmetic and copies ran while one was open for 0% -> 0% of each run, Pallas kernels for 23% -> 25%
where the time goes in v7:
time: 94.5 us; the launch traced here: 94.3 us
  Pallas kernels  61.8 us (65%)
  blocking collectives  30.6 us (32%)
  starting transfers between devices  1.82 us (2%)
    pallas_call x4, Pallas kernels, correlate(): pl.pallas_call(functools.partial(block_kernel, blocks), grid_spec=pltpu.P...  31.2 us
    all_to_all x1, blocking collectives, body(): lax.all_to_all(partial, 'fgrp', split_axis=0, concat_axis=0, tiled=True)  30.6 us
    pallas_call x1, Pallas kernels, filter_all(): pl.pallas_call(functools.partial(filter_kernel, low_scale), grid=(frames,...  29.5 us
  transfers between devices with their start and end apart: 3, of which 0 were waited for; matrix products, arithmetic and copies ran while one was open for 0% of the time, Pallas kernels for 25%

profile of v7, /device:TPU:0, one launch (start us, length us, event | category | flops | bytes accessed | tf_op | source)
XLA Modules:
  0.0 94.3 jit_solution(11027386447261063451)
XLA Ops:
  0.0 29.5 %filter_all.1 = bf16[8,112,512]{2,1,0:T(8,128)(2,1)} custom-call(bf16[2,512,16384]{2,1,0:T(8,128)(2,1)} %volt_ref.1, bf16[512,4096]{1,0:T(8,128)(2,1)} %constant.14.clone.table_hbm, f8e4m3fn[256,4096]{1,0:T(32,128)(4,1)} %constant.15.clone.low_ref, f32[2,64,512]{2,1,0:T(8,128)} %bitcast.5), custom_call_target="tpu_custom_call" | custom-call | flops 17179869184 | bytes 37748736 | tf_op jit(solution)/shard_map/filter_all/pallas_call | solution.py:132
  29.5 30.6 %all_to_all.5.in_ref = bf16[8,112,512]{2,1,0:T(8,128)(2,1)S(1)} all-to-all(bf16[8,112,512]{2,1,0:T(8,128)(2,1)} %filter_all.1), channel_id=1, replica_groups=mesh['fgrp'=8,'tile'=2,'pol'=2] {'fgrp'}, dimensions={0} | all-to-all | bytes 1835008 | tf_op jit(solution)/shard_map/all_to_all | solution.py:310
  60.1 1.1 %merge.1 = (bf16[512,512]{1,0:T(8,128)(2,1)S(1)}, bf16[512,1024]{1,0:T(8,128)(2,1)S(1)}) custom-call(bf16[8,112,512]{2,1,0:T(8,128)(2,1)S(1)} %all_to_all.5.in_ref), custom_call_target="tpu_custom_call" | custom-call | tf_op jit(solution)/shard_map/merge/pallas_call | solution.py:196
  61.2 0.1 collective-permute-start.1
  61.3 1.6 %collective-permute-start = (bf16[512,512]{1,0:T(8,128)(2,1)S(1)}, bf16[512,512]{1,0:T(8,128)(2,1)S(1)}, u32[]{:S(2)}, u32[]{:S(2)}) collective-permute-start(bf16[512,512]{1,0:T(8,128)(2,1)S(1)} %get-tuple-element.10.refs_0_), channel_id=1, source_target_pairs={{0,1},{1,0},{2,3},{3,2},{4,5},{5,4},{6,7},{7,6},{8,9},{9,8},{10,11... | collective-permute-start | bytes 1572872 | tf_op jit(solution)/shard_map/ppermute | solution.py:299
  62.9 7.8 %correlate.4.refs_1_ = f32[8,2,512,2048]{3,2,1,0:T(8,128)} custom-call(s32[1]{0:T(128)} %bitcast.3.place_ref, bf16[512,1024]{1,0:T(8,128)(2,1)S(1)} %get-tuple-element.9.left_ref, bf16[512,512]{1,0:T(8,128)(2,1)S(1)} %get-tuple-element.10.refs_0_), custom_call_target="tpu_custom_call" | custom-call | flops 1073741824 | bytes 16777216 | tf_op jit(solution)/shard_map/correlate/pallas_call | solution.py:248
  70.7 0.0 collective-permute-done.1.refs_0_
  70.7 7.8 %correlate.5.refs_1_ = f32[8,2,512,2048]{3,2,1,0:T(8,128)} custom-call(s32[1]{0:T(128)} %bitcast.2.place_ref, bf16[512,1024]{1,0:T(8,128)(2,1)S(1)} %get-tuple-element.9.left_ref, bf16[512,512]{1,0:T(8,128)(2,1)S(1)} %collective-permute-done.1.refs_0_, f32[8,2,512,2048]{3,2,1,0:T(8,128)} %correlate.4.refs_1_), custom_call_target="tpu_custom_call", output_to_operand_aliasing={{}: (3, {})} | custom-call | flops 1073741824 | bytes 16777216 | tf_op jit(solution)/shard_map/correlate/pallas_call | solution.py:248
  78.5 0.0 collective-permute-done.refs_0_
  78.5 0.2 collective-permute-start.2
  78.7 7.8 %correlate.6.refs_1_ = f32[8,2,512,2048]{3,2,1,0:T(8,128)} custom-call(s32[1]{0:T(128)} %bitcast.4.place_ref, bf16[512,1024]{1,0:T(8,128)(2,1)S(1)} %get-tuple-element.9.left_ref, bf16[512,512]{1,0:T(8,128)(2,1)S(1)} %collective-permute-done.refs_0_, f32[8,2,512,2048]{3,2,1,0:T(8,128)} %correlate.5.refs_1_), custom_call_target="tpu_custom_call", output_to_operand_aliasing={{}: (3, {})} | custom-call | flops 1073741824 | bytes 16777216 | tf_op jit(solution)/shard_map/correlate/pallas_call | solution.py:248
  86.5 0.0 collective-permute-done.2.refs_0_
  86.5 7.8 %correlate.7 = f32[8,2,512,2048]{3,2,1,0:T(8,128)} custom-call(s32[1]{0:T(128)} %bitcast.place_ref, bf16[512,1024]{1,0:T(8,128)(2,1)S(1)} %get-tuple-element.9.left_ref, bf16[512,512]{1,0:T(8,128)(2,1)S(1)} %collective-permute-done.2.refs_0_, f32[8,2,512,2048]{3,2,1,0:T(8,128)} %correlate.6.refs_1_), custom_call_target="tpu_custom_call", output_to_operand_aliasing={{}: (3, {})} | custom-call | flops 1073741824 | bytes 16777216 | tf_op jit(solution)/shard_map/correlate/pallas_call | solution.py:248
Async XLA Ops:
  61.2 9.5 %collective-permute-start.1 = (bf16[512,512]{1,0:T(8,128)(2,1)S(1)}, bf16[512,512]{1,0:T(8,128)(2,1)S(1)}, u32[]{:S(2)}, u32[]{:S(2)}) collective-permute-start(bf16[512,512]{1,0:T(8,128)(2,1)S(1)} %get-tuple-element.10.refs_0_), channel_id=1, source_target_pairs={{0,2},{2,0},{1,3},{3,1},{4,6},{6,4},{5,7},{7,5},{8,10},{10,8},{9,1... | collective-permute-start | bytes 1572872 | tf_op jit(solution)/shard_map/ppermute | solution.py:299
  61.3 17.2 %collective-permute-start = (bf16[512,512]{1,0:T(8,128)(2,1)S(1)}, bf16[512,512]{1,0:T(8,128)(2,1)S(1)}, u32[]{:S(2)}, u32[]{:S(2)}) collective-permute-start(bf16[512,512]{1,0:T(8,128)(2,1)S(1)} %get-tuple-element.10.refs_0_), channel_id=1, source_target_pairs={{0,1},{1,0},{2,3},{3,2},{4,5},{5,4},{6,7},{7,6},{8,9},{9,8},{10,11... | collective-permute-start | bytes 1572872 | tf_op jit(solution)/shard_map/ppermute | solution.py:299
  78.5 8.0 %collective-permute-start.2 = (bf16[512,512]{1,0:T(8,128)(2,1)S(1)}, bf16[512,512]{1,0:T(8,128)(2,1)S(1)}, u32[]{:S(2)}, u32[]{:S(2)}) collective-permute-start(bf16[512,512]{1,0:T(8,128)(2,1)S(1)} %collective-permute-done.refs_0_), channel_id=1, source_target_pairs={{0,2},{2,0},{1,3},{3,1},{4,6},{6,4},{5,7},{7,5},{8,10},{10,8},{9,1... | collective-permute-start | bytes 1572872 | tf_op jit(solution)/shard_map/ppermute | solution.py:299

commit v8 on v5

--- a/solution.py
+++ b/solution.py
@@ -12,7 +12,6 @@
 
 NFFT = 4096
 TAPS = 4
-VMEM = 56 * 2**20
 
 
 def filter_taps():
@@ -36,11 +35,11 @@
     transform = np.concatenate([np.cos(angles), np.sin(angles)], axis=1) / math.sqrt(NFFT)
     blocks = {t: filter_taps()[t][:, None] * transform for t in order}
     high = {t: b.astype(np.float32).astype(ml_dtypes.bfloat16) for t, b in blocks.items()}
-    low = [
-        (blocks[t] - high[t].astype(np.float64)).astype(np.float32).astype(ml_dtypes.bfloat16)
-        for t in low_order
-    ]
-    return np.concatenate([high[t] for t in order] + low, axis=1)
+    low = np.concatenate([blocks[t] - high[t].astype(np.float64) for t in low_order], axis=1)
+    scale = 2.0 ** np.floor(np.log2(256.0 / np.abs(low).max()))
+    low = (low * scale).astype(np.float32).astype(ml_dtypes.float8_e4m3fn)
+    high = np.concatenate([high[t] for t in order], axis=1)
+    return np.ascontiguousarray(high.T), np.ascontiguousarray(low.T), float(1.0 / scale)
 
 
 def peer(me, step, length, way):
@@ -49,29 +48,78 @@
     return me ^ step
 
 
-def combine_kernel(*refs):
-    product_refs, gain_ref, out_ref = refs[:-2], refs[-2], refs[-1]
+def filter_kernel(low_scale, volt_hbm, table_hbm, low_hbm, gain_ref, out_ref, *scratch):
+    sums, low_sums, volts, table, low_table, volt_here, first_here, table_here, low_here = scratch
     half = gain_ref.shape[1]
     width = 2 * half
+    order, low_order = tap_order()
+    steps = 2 * (volt_hbm.shape[2] // NFFT)
+    pieces = first_here.shape[0]
+    depth = NFFT // pieces
+
+    def block(step):
+        slot = lax.rem(step, 2)
+        samples = pl.ds(pl.multiple_of(lax.div(step, 2) * NFFT, NFFT), NFFT)
+        return pltpu.make_async_copy(
+            volt_hbm.at[slot, :, samples], volts.at[slot], volt_here.at[slot]
+        )
+
+    def fetch(piece):
+        part = pl.ds(piece * depth, depth)
+        return [
+            pltpu.make_async_copy(
+                volt_hbm.at[0, :, part], volts.at[0, :, part], first_here.at[piece]
+            ),
+            pltpu.make_async_copy(table_hbm.at[:, part], table.at[:, part], table_here.at[piece]),
+            pltpu.make_async_copy(low_hbm.at[:, part], low_table.at[:, part], low_here.at[piece]),
+        ]
+
+    def product(left, right):
+        return lax.dot_general(
+            left, right, (((1,), (1,)), ((), ())), preferred_element_type=jnp.float32
+        )
+
+    def add(step, start, size):
+        part = lax.rem(step, 2)
+        first = pl.multiple_of(lax.div(step, 2) * width, width)
+        here = pl.ds(first, len(order) * width)
+        low = pl.ds(first, len(low_order) * width)
+        values = volts[part, :, start : start + size]
+        sums[part, here, :] += product(table[:, start : start + size], values)
+        low_sums[part, low, :] += product(
+            low_table[:, start : start + size], values.astype(jnp.float8_e4m3fn)
+        )
+
+    for piece in range(pieces):
+        for copy in fetch(piece):
+            copy.start()
+    block(1).start()
+    sums[...] = jnp.zeros_like(sums)
+    low_sums[...] = jnp.zeros_like(low_sums)
+    for piece in range(pieces):
+        for copy in fetch(piece):
+            copy.wait()
+        add(0, piece * depth, depth)
+
+    @pl.loop(1, steps)
+    def _(step):
+        block(step).wait()
+
+        @pl.when(step + 1 < steps)
+        def _():
+            block(step + 1).start()
+
+        add(step, 0, NFFT)
+
     owners = out_ref.shape[0]
     share = half // owners
-    order, low_order = tap_order()
-    frames = len(product_refs)
-
-    def term(frame, at, part):
-        value = product_refs[frame][part, :, at * width : (at + 1) * width]
-        if order[at] in low_order:
-            low = (len(order) + low_order.index(order[at])) * width
-            value = value + product_refs[frame][part, :, low : low + width]
-        return value
-
-    lane = lax.broadcasted_iota(jnp.int32, (product_refs[0].shape[1], width), 1)
-    for slot in range(frames + TAPS - 1):
-        used = [f for f in range(frames) if 0 <= slot - f < TAPS]
-        first, second = (sum(term(f, slot - f, part) for f in used) for part in range(2))
-        second = pltpu.roll(second, half, 1)
-        raw = jnp.where(lane < half, second + first, second - first).T
-        real, imag = raw[:half], raw[half:]
+    for slot in range(sums.shape[1] // width):
+        both = [sums[c, slot * width : (slot + 1) * width, :] for c in range(2)]
+        at = (slot - order.index(low_order[0])) * width
+        if 0 <= at < low_sums.shape[1]:
+            both = [both[c] + low_scale * low_sums[c, at : at + width, :] for c in range(2)]
+        real = both[0][:half] + both[1][half:]
+        imag = both[1][:half] - both[0][half:]
         out_real = gain_ref[0] * real - gain_ref[1] * imag
         out_imag = gain_ref[0] * imag + gain_ref[1] * real
         for owner in range(owners):
@@ -81,28 +129,38 @@
             out_ref[owner, at : at + 2 * share, :] = pair.astype(jnp.bfloat16)
 
 
-def filter_all(voltages, table, gains, owners):
+def filter_all(voltages, tables, gains, owners):
     rows = voltages.shape[1]
     frames = voltages.shape[2] // NFFT
     half = gains.shape[1]
     slots = frames + TAPS - 1
+    low_slots = frames + len(tap_order()[1]) - 1
     out_rows = slots * 2 * half // owners
-    products = [
-        lax.dot_general(
-            voltages[:, :, frame * NFFT : (frame + 1) * NFFT],
-            table,
-            (((2,), (0,)), ((), ())),
-            preferred_element_type=jnp.float32,
-        )
-        for frame in range(frames)
-    ]
+    table, low_table, low_scale = tables
+    pieces = 4
     return pl.pallas_call(
-        combine_kernel,
-        in_specs=[pl.BlockSpec(memory_space=pltpu.VMEM)] * (frames + 1),
+        functools.partial(filter_kernel, low_scale),
+        in_specs=[pl.BlockSpec(memory_space=pl.ANY)] * 3 + [pl.BlockSpec(memory_space=pltpu.VMEM)],
         out_shape=jax.ShapeDtypeStruct((owners, out_rows, rows), jnp.bfloat16),
-        compiler_params=pltpu.CompilerParams(vmem_limit_bytes=24 * 2**20),
-        name="combine",
-    )(*products, gains)
+        scratch_shapes=[
+            pltpu.VMEM((2, slots * 2 * half, rows), jnp.float32),
+            pltpu.VMEM((2, low_slots * 2 * half, rows), jnp.float32),
+            pltpu.VMEM((2, rows, NFFT), jnp.bfloat16),
+            pltpu.VMEM(table.shape, jnp.bfloat16),
+            pltpu.VMEM(low_table.shape, jnp.float8_e4m3fn),
+            pltpu.SemaphoreType.DMA((2,)),
+            pltpu.SemaphoreType.DMA((pieces,)),
+            pltpu.SemaphoreType.DMA((pieces,)),
+            pltpu.SemaphoreType.DMA((pieces,)),
+        ],
+        compiler_params=pltpu.CompilerParams(vmem_limit_bytes=40 * 2**20),
+        cost_estimate=pl.CostEstimate(
+            flops=2 * 2 * rows * frames * NFFT * (table.shape[0] + low_table.shape[0]),
+            bytes_accessed=2 * (2 * rows * frames * NFFT + NFFT * table.shape[0]),
+            transcendentals=0,
+        ),
+        name="filter_all",
+    )(voltages, jnp.asarray(table), jnp.asarray(low_table), gains)
 
 
 def merge_kernel(frames, share, norm, in_ref, out_ref, left_ref, scratch):
@@ -166,50 +224,57 @@
     ]
 
 
-def block_kernel(blocks, place_ref, left_ref, *refs):
-    right_refs, out_ref = refs[:blocks], refs[-1]
-    count = out_ref.shape[0]
-    depth = right_refs[0].shape[0] // count
-    for block in range(blocks):
-
-        @pl.when(pl.program_id(1) == block)
-        def _():
-            for channel in range(count):
-                out_ref[channel, 0], out_ref[channel, 1] = visibility(
-                    left_ref[:, 2 * depth * channel : 2 * depth * (channel + 1)],
-                    right_refs[block][depth * channel : depth * (channel + 1), :],
-                )
-
-
-def correlate(left, rights, places, total, result, share):
-    blocks = len(rights)
-    out_rows, rows = rights[0].shape
+def block_kernel(share, place_ref, left_ref, right_ref, *refs):
+    out_hbm, (values, written) = refs[-3], refs[-2:]
+    depth = right_ref.shape[0] // share
+    rows = right_ref.shape[1]
+    slots = values.shape[0]
+    columns = pl.ds(pl.multiple_of(place_ref[0] * rows, rows), rows)
+
+    def write(channel):
+        slot = channel % slots
+        return pltpu.make_async_copy(
+            values.at[slot], out_hbm.at[channel, :, :, columns], written.at[slot]
+        )
+
+    for channel in range(share):
+        slot = channel % slots
+        if channel >= slots:
+            write(channel - slots).wait()
+        values[slot, 0], values[slot, 1] = visibility(
+            left_ref[:, 2 * depth * channel : 2 * depth * (channel + 1)],
+            right_ref[depth * channel : depth * (channel + 1), :],
+        )
+        write(channel).start()
+    for channel in range(max(share - slots, 0), share):
+        write(channel).wait()
+
+
+def correlate(left, right, place, total, result, share):
+    out_rows, rows = right.shape
     depth = out_rows // share
-    count = 2
-    operands = [places, left, *rights]
-    specs = [pl.BlockSpec((rows, 2 * depth * count), lambda c, b, places: (0, c))]
-    specs += [pl.BlockSpec((depth * count, rows), lambda c, b, places: (c, 0))] * blocks
+    slots = 4
+    operands = [place, left, right]
+    specs = [pl.BlockSpec(memory_space=pltpu.SMEM)] + [pl.BlockSpec(memory_space=pltpu.VMEM)] * 2
     aliases = {}
     if result is not None:
         aliases = {len(operands): 0}
         operands.append(result)
         specs.append(pl.BlockSpec(memory_space=pl.ANY))
     return pl.pallas_call(
-        functools.partial(block_kernel, blocks),
-        grid_spec=pltpu.PrefetchScalarGridSpec(
-            num_scalar_prefetch=1,
-            grid=(share // count, blocks),
-            in_specs=specs,
-            out_specs=pl.BlockSpec(
-                (count, 2, rows, rows), lambda c, b, places: (c, 0, 0, places[b])
-            ),
-        ),
+        functools.partial(block_kernel, share),
+        in_specs=specs,
+        out_specs=pl.BlockSpec(memory_space=pl.ANY),
         out_shape=jax.ShapeDtypeStruct((share, 2, rows, total), jnp.float32),
+        scratch_shapes=[
+            pltpu.VMEM((slots, 2, rows, rows), jnp.float32),
+            pltpu.SemaphoreType.DMA((slots,)),
+        ],
         input_output_aliases=aliases,
         compiler_params=pltpu.CompilerParams(vmem_limit_bytes=24 * 2**20),
         cost_estimate=pl.CostEstimate(
-            flops=8 * share * blocks * rows * rows * depth,
-            bytes_accessed=4 * share * 2 * blocks * rows * rows,
+            flops=8 * share * rows * rows * depth,
+            bytes_accessed=4 * share * 2 * rows * rows,
             transcendentals=0,
         ),
         name="correlate",
@@ -255,8 +320,7 @@
     owners = lax.axis_size("fgrp")
     share = channels // owners
     norm = 1.0 / math.sqrt(frames_here * owners)
-    table = jnp.asarray(filter_table(channels))
-    partial = filter_all(voltages, table, jnp.swapaxes(gains, 1, 2), owners)
+    partial = filter_all(voltages, filter_table(channels), jnp.swapaxes(gains, 1, 2), owners)
     turned = lax.all_to_all(partial, "fgrp", split_axis=0, concat_axis=0, tiled=True)
     own, left = merge(turned, frames_here, share, norm)
     tiles, pols = lax.axis_size("tile"), lax.axis_size("pol")
@@ -277,7 +341,7 @@
         for by_tile in range(tiles):
             right = swapped(near, "tile", by_tile)
             where = place(by_tile, by_pol).reshape(1)
-            result = correlate(left, [right], where, total, result, share)
+            result = correlate(left, right, where, total, result, share)
     return result
 
 

time: 102 us -> 89.2 us (0.87)
  matrix products: 39.7 us -> 0 us
  Pallas kernels: 30.1 us -> 52.1 us
  local copies, waits for them, and re-layouts: 0.01 us -> 4.36 us
    dot_general x4 -> x0, matrix products: 39.7 us -> none  [filter_all(): lax.dot_general(voltages[:, :, frame * NFFT:(frame + 1) * NFFT], table, (...]
    pallas_call x5, Pallas kernels: 29 us -> 51 us  [the longest x1 25.8 us: filter_all(): pl.pallas_call(functools.partial(filter_kernel, low_scale), in_specs=[pl....]
    unnamed x6, local copies, waits for them, and re-layouts: 0.01 us -> 4.36 us
  transfers between devices with their start and end apart: 3 -> 3, of which waited for: 0 -> 1; matrix products, arithmetic and copies ran while one was open for 0% -> 0% of each run, Pallas kernels for 20% -> 21%
where the time goes in v8:
time: 89.2 us; the launch traced here: 89 us
  Pallas kernels  52.1 us (58%)
  blocking collectives  30.4 us (34%)
  local copies, waits for them, and re-layouts  4.36 us (5%)
  starting transfers between devices  1.77 us (2%)
    all_to_all x1, blocking collectives, body(): lax.all_to_all(partial, 'fgrp', split_axis=0, concat_axis=0, tiled=True)  30.4 us
    pallas_call x1, Pallas kernels, filter_all(): pl.pallas_call(functools.partial(filter_kernel, low_scale), in_specs=[pl....  25.8 us
    pallas_call x4, Pallas kernels, correlate(): pl.pallas_call(functools.partial(block_kernel, share), in_specs=specs, ou...  25.2 us
    unnamed x6, local copies, waits for them, and re-layouts  4.36 us
  transfers between devices with their start and end apart: 3, of which 1 were waited for; matrix products, arithmetic and copies ran while one was open for 0% of the time, Pallas kernels for 21%

profile of v8, /device:TPU:0, one launch (start us, length us, event | category | flops | bytes accessed | tf_op | source)
XLA Modules:
  0.0 89.0 jit_solution(13879827431034184842)
XLA Ops:
  0.0 0.0 copy-start
  0.0 0.9 %copy-done = f32[2,512,64]{1,2,0:T(8,128)S(1)} copy-done((f32[2,512,64]{1,2,0:T(8,128)S(1)}, f32[2,512,64]{1,2,0:T(8,128)}, u32[]{:S(2)}) %copy-start) | copy-done | bytes 262168
  1.0 0.0 copy-start.1
  1.0 2.2 %copy-done.1 = bf16[512,4096]{1,0:T(8,128)(2,1)S(1)} copy-done((bf16[512,4096]{1,0:T(8,128)(2,1)S(1)}, bf16[512,4096]{1,0:T(8,128)(2,1)}, u32[]{:S(2)}) %copy-start.1) | copy-done | bytes 4194328
  3.1 0.0 copy-start.2
  3.1 1.2 %copy-done.2 = f8e4m3fn[256,4096]{1,0:T(32,128)(4,1)S(1)} copy-done((f8e4m3fn[256,4096]{1,0:T(32,128)(4,1)S(1)}, f8e4m3fn[256,4096]{1,0:T(32,128)(4,1)}, u32[]{:S(2)}) %copy-start.2) | copy-done | bytes 1048600
  4.4 25.8 %filter_all.1 = bf16[8,112,512]{2,1,0:T(8,128)(2,1)S(1)} custom-call(bf16[2,512,16384]{2,1,0:T(8,128)(2,1)} %volt_hbm.1, bf16[512,4096]{1,0:T(8,128)(2,1)S(1)} %copy-done.1, f8e4m3fn[256,4096]{1,0:T(32,128)(4,1)S(1)} %copy-done.2, f32[2,64,512]{2,1,0:T(8,128)S(1)} %bitcast.5), custom_call_target="tpu_custom_call" | custom-call | flops 25769803776 | bytes 37748736 | tf_op jit(solution)/shard_map/filter_all/pallas_call | solution.py:141
  30.1 30.4 %all_to_all.5.in_ref = bf16[8,112,512]{2,1,0:T(8,128)(2,1)S(1)} all-to-all(bf16[8,112,512]{2,1,0:T(8,128)(2,1)S(1)} %filter_all.1), channel_id=1, replica_groups=mesh['fgrp'=8,'tile'=2,'pol'=2] {'fgrp'}, dimensions={0} | all-to-all | bytes 1835008 | tf_op jit(solution)/shard_map/all_to_all | solution.py:324
  60.5 1.1 %merge.1 = (bf16[512,512]{1,0:T(8,128)(2,1)S(1)}, bf16[512,1024]{1,0:T(8,128)(2,1)S(1)}) custom-call(bf16[8,112,512]{2,1,0:T(8,128)(2,1)S(1)} %all_to_all.5.in_ref), custom_call_target="tpu_custom_call" | custom-call | tf_op jit(solution)/shard_map/merge/pallas_call | solution.py:203
  61.6 0.1 collective-permute-start.1
  61.7 1.6 %collective-permute-start = (bf16[512,512]{1,0:T(8,128)(2,1)S(1)}, bf16[512,512]{1,0:T(8,128)(2,1)S(1)}, u32[]{:S(2)}, u32[]{:S(2)}) collective-permute-start(bf16[512,512]{1,0:T(8,128)(2,1)S(1)} %get-tuple-element.10.right_ref), channel_id=1, source_target_pairs={{0,1},{1,0},{2,3},{3,2},{4,5},{5,4},{6,7},{7,6},{8,9},{9,8},{10,11... | collective-permute-start | bytes 1572872 | tf_op jit(solution)/shard_map/ppermute | solution.py:313
  63.3 6.3 %correlate.4.refs_0_ = f32[8,2,512,2048]{3,2,1,0:T(8,128)} custom-call(s32[1]{0:T(128)} %bitcast.3.place_ref, bf16[512,1024]{1,0:T(8,128)(2,1)S(1)} %get-tuple-element.9.left_ref, bf16[512,512]{1,0:T(8,128)(2,1)S(1)} %get-tuple-element.10.right_ref), custom_call_target="tpu_custom_call" | custom-call | flops 1073741824 | bytes 16777216 | tf_op jit(solution)/shard_map/correlate/pallas_call | solution.py:264
  69.6 0.0 collective-permute-done.1.right_ref
  69.6 6.3 %correlate.5.refs_0_ = f32[8,2,512,2048]{3,2,1,0:T(8,128)} custom-call(s32[1]{0:T(128)} %bitcast.2.place_ref, bf16[512,1024]{1,0:T(8,128)(2,1)S(1)} %get-tuple-element.9.left_ref, bf16[512,512]{1,0:T(8,128)(2,1)S(1)} %collective-permute-done.1.right_ref, f32[8,2,512,2048]{3,2,1,0:T(8,128)} %correlate.4.refs_0_), custom_call_target="tpu_custom_call", output_to_operand_aliasing={{}: (3, {})} | custom-call | flops 1073741824 | bytes 16777216 | tf_op jit(solution)/shard_map/correlate/pallas_call | solution.py:264
  75.9 0.1 collective-permute-done.right_ref
  76.0 0.1 collective-permute-start.2
  76.2 6.3 %correlate.6.refs_0_ = f32[8,2,512,2048]{3,2,1,0:T(8,128)} custom-call(s32[1]{0:T(128)} %bitcast.4.place_ref, bf16[512,1024]{1,0:T(8,128)(2,1)S(1)} %get-tuple-element.9.left_ref, bf16[512,512]{1,0:T(8,128)(2,1)S(1)} %collective-permute-done.right_ref, f32[8,2,512,2048]{3,2,1,0:T(8,128)} %correlate.5.refs_0_), custom_call_target="tpu_custom_call", output_to_operand_aliasing={{}: (3, {})} | custom-call | flops 1073741824 | bytes 16777216 | tf_op jit(solution)/shard_map/correlate/pallas_call | solution.py:264
  82.5 0.0 collective-permute-done.2.right_ref
  82.5 6.3 %correlate.7 = f32[8,2,512,2048]{3,2,1,0:T(8,128)} custom-call(s32[1]{0:T(128)} %bitcast.place_ref, bf16[512,1024]{1,0:T(8,128)(2,1)S(1)} %get-tuple-element.9.left_ref, bf16[512,512]{1,0:T(8,128)(2,1)S(1)} %collective-permute-done.2.right_ref, f32[8,2,512,2048]{3,2,1,0:T(8,128)} %correlate.6.refs_0_), custom_call_target="tpu_custom_call", output_to_operand_aliasing={{}: (3, {})} | custom-call | flops 1073741824 | bytes 16777216 | tf_op jit(solution)/shard_map/correlate/pallas_call | solution.py:264
Async XLA Ops:
  0.0 0.9 %copy-start = (f32[2,512,64]{1,2,0:T(8,128)S(1)}, f32[2,512,64]{1,2,0:T(8,128)}, u32[]{:S(2)}) copy-start(f32[2,512,64]{1,2,0:T(8,128)} %param.5) | copy-start | bytes 786436
  1.0 2.2 %copy-start.1 = (bf16[512,4096]{1,0:T(8,128)(2,1)S(1)}, bf16[512,4096]{1,0:T(8,128)(2,1)}, u32[]{:S(2)}) copy-start(bf16[512,4096]{1,0:T(8,128)(2,1)} %constant.14.clone.table_hbm) | copy-start | bytes 12582916
  3.1 1.2 %copy-start.2 = (f8e4m3fn[256,4096]{1,0:T(32,128)(4,1)S(1)}, f8e4m3fn[256,4096]{1,0:T(32,128)(4,1)}, u32[]{:S(2)}) copy-start(f8e4m3fn[256,4096]{1,0:T(32,128)(4,1)} %constant.15.clone.low_hbm) | copy-start | bytes 3145732
  61.6 8.0 %collective-permute-start.1 = (bf16[512,512]{1,0:T(8,128)(2,1)S(1)}, bf16[512,512]{1,0:T(8,128)(2,1)S(1)}, u32[]{:S(2)}, u32[]{:S(2)}) collective-permute-start(bf16[512,512]{1,0:T(8,128)(2,1)S(1)} %get-tuple-element.10.right_ref), channel_id=1, source_target_pairs={{0,2},{2,0},{1,3},{3,1},{4,6},{6,4},{5,7},{7,5},{8,10},{10,8},{9,1... | collective-permute-start | bytes 1572872 | tf_op jit(solution)/shard_map/ppermute | solution.py:313
  61.7 14.3 %collective-permute-start = (bf16[512,512]{1,0:T(8,128)(2,1)S(1)}, bf16[512,512]{1,0:T(8,128)(2,1)S(1)}, u32[]{:S(2)}, u32[]{:S(2)}) collective-permute-start(bf16[512,512]{1,0:T(8,128)(2,1)S(1)} %get-tuple-element.10.right_ref), channel_id=1, source_target_pairs={{0,1},{1,0},{2,3},{3,2},{4,5},{5,4},{6,7},{7,6},{8,9},{9,8},{10,11... | collective-permute-start | bytes 1572872 | tf_op jit(solution)/shard_map/ppermute | solution.py:313
  76.0 6.4 %collective-permute-start.2 = (bf16[512,512]{1,0:T(8,128)(2,1)S(1)}, bf16[512,512]{1,0:T(8,128)(2,1)S(1)}, u32[]{:S(2)}, u32[]{:S(2)}) collective-permute-start(bf16[512,512]{1,0:T(8,128)(2,1)S(1)} %collective-permute-done.right_ref), channel_id=1, source_target_pairs={{0,2},{2,0},{1,3},{3,1},{4,6},{6,4},{5,7},{7,5},{8,10},{10,8},{9,1... | collective-permute-start | bytes 1572872 | tf_op jit(solution)/shard_map/ppermute | solution.py:313

commit v9 on v8

--- a/solution.py
+++ b/solution.py
@@ -48,27 +48,30 @@
     return me ^ step
 
 
-def filter_kernel(low_scale, volt_hbm, table_hbm, low_hbm, gain_ref, out_ref, *scratch):
+def filter_kernel(frame, low_scale, volt_hbm, table_hbm, low_hbm, *refs):
+    out_refs, scratch = refs[:-9], refs[-9:]
     sums, low_sums, volts, table, low_table, volt_here, first_here, table_here, low_here = scratch
-    half = gain_ref.shape[1]
-    width = 2 * half
     order, low_order = tap_order()
-    steps = 2 * (volt_hbm.shape[2] // NFFT)
+    width = table.shape[0] // len(order)
+    half = width // 2
+    count = sums.shape[1] // width - (TAPS - 1)
+    steps = 2 * count
     pieces = first_here.shape[0]
     depth = NFFT // pieces
 
     def block(step):
         slot = lax.rem(step, 2)
-        samples = pl.ds(pl.multiple_of(lax.div(step, 2) * NFFT, NFFT), NFFT)
+        samples = pl.ds(pl.multiple_of((lax.div(step, 2) + frame) * NFFT, NFFT), NFFT)
         return pltpu.make_async_copy(
             volt_hbm.at[slot, :, samples], volts.at[slot], volt_here.at[slot]
         )
 
     def fetch(piece):
         part = pl.ds(piece * depth, depth)
+        samples = pl.ds(frame * NFFT + piece * depth, depth)
         return [
             pltpu.make_async_copy(
-                volt_hbm.at[0, :, part], volts.at[0, :, part], first_here.at[piece]
+                volt_hbm.at[0, :, samples], volts.at[0, :, part], first_here.at[piece]
             ),
             pltpu.make_async_copy(table_hbm.at[:, part], table.at[:, part], table_here.at[piece]),
             pltpu.make_async_copy(low_hbm.at[:, part], low_table.at[:, part], low_here.at[piece]),
@@ -111,40 +114,40 @@
 
         add(step, 0, NFFT)
 
-    owners = out_ref.shape[0]
-    share = half // owners
+    kept = out_refs[0].shape[0] // width
     for slot in range(sums.shape[1] // width):
         both = [sums[c, slot * width : (slot + 1) * width, :] for c in range(2)]
         at = (slot - order.index(low_order[0])) * width
         if 0 <= at < low_sums.shape[1]:
             both = [both[c] + low_scale * low_sums[c, at : at + width, :] for c in range(2)]
-        real = both[0][:half] + both[1][half:]
-        imag = both[1][:half] - both[0][half:]
-        out_real = gain_ref[0] * real - gain_ref[1] * imag
-        out_imag = gain_ref[0] * imag + gain_ref[1] * real
-        for owner in range(owners):
-            at = owner * share
-            pair = jnp.concatenate([out_real[at : at + share], out_imag[at : at + share]], axis=0)
-            at = 2 * share * slot
-            out_ref[owner, at : at + 2 * share, :] = pair.astype(jnp.bfloat16)
-
-
-def filter_all(voltages, tables, gains, owners):
+        raw = jnp.concatenate(
+            [both[0][:half] + both[1][half:], both[1][:half] - both[0][half:]], axis=0
+        )
+        if slot < kept:
+            out_refs[0][slot * width : (slot + 1) * width, :] = raw
+        else:
+            at = (slot - kept) * width
+            out_refs[1][at : at + width, :] = raw.astype(jnp.bfloat16)
+
+
+def filter_part(voltages, tables, frame, count, kept):
     rows = voltages.shape[1]
-    frames = voltages.shape[2] // NFFT
-    half = gains.shape[1]
-    slots = frames + TAPS - 1
-    low_slots = frames + len(tap_order()[1]) - 1
-    out_rows = slots * 2 * half // owners
     table, low_table, low_scale = tables
+    width = table.shape[0] // TAPS
+    slots = count + TAPS - 1
+    low_slots = count + len(tap_order()[1]) - 1
+    shapes = [jax.ShapeDtypeStruct((kept * width, rows), jnp.float32)]
+    if slots > kept:
+        shapes.append(jax.ShapeDtypeStruct(((slots - kept) * width, rows), jnp.bfloat16))
     pieces = 4
     return pl.pallas_call(
-        functools.partial(filter_kernel, low_scale),
-        in_specs=[pl.BlockSpec(memory_space=pl.ANY)] * 3 + [pl.BlockSpec(memory_space=pltpu.VMEM)],
-        out_shape=jax.ShapeDtypeStruct((owners, out_rows, rows), jnp.bfloat16),
+        functools.partial(filter_kernel, frame, low_scale),
+        in_specs=[pl.BlockSpec(memory_space=pl.ANY)] * 3,
+        out_specs=[pl.BlockSpec(memory_space=pltpu.VMEM)] * len(shapes),
+        out_shape=shapes,
         scratch_shapes=[
-            pltpu.VMEM((2, slots * 2 * half, rows), jnp.float32),
-            pltpu.VMEM((2, low_slots * 2 * half, rows), jnp.float32),
+            pltpu.VMEM((2, slots * width, rows), jnp.float32),
+            pltpu.VMEM((2, low_slots * width, rows), jnp.float32),
             pltpu.VMEM((2, rows, NFFT), jnp.bfloat16),
             pltpu.VMEM(table.shape, jnp.bfloat16),
             pltpu.VMEM(low_table.shape, jnp.float8_e4m3fn),
@@ -153,14 +156,47 @@
             pltpu.SemaphoreType.DMA((pieces,)),
             pltpu.SemaphoreType.DMA((pieces,)),
         ],
-        compiler_params=pltpu.CompilerParams(vmem_limit_bytes=40 * 2**20),
+        compiler_params=pltpu.CompilerParams(vmem_limit_bytes=52 * 2**20),
         cost_estimate=pl.CostEstimate(
-            flops=2 * 2 * rows * frames * NFFT * (table.shape[0] + low_table.shape[0]),
-            bytes_accessed=2 * (2 * rows * frames * NFFT + NFFT * table.shape[0]),
+            flops=2 * 2 * rows * count * NFFT * (table.shape[0] + low_table.shape[0]),
+            bytes_accessed=2 * (2 * rows * count * NFFT + NFFT * table.shape[0]),
             transcendentals=0,
         ),
-        name="filter_all",
-    )(voltages, jnp.asarray(table), jnp.asarray(low_table), gains)
+        name="filter_part",
+    )(voltages, jnp.asarray(table), jnp.asarray(low_table))
+
+
+def combine_kernel(early_ref, late_ref, handed_ref, gain_ref, out_ref):
+    half = gain_ref.shape[1]
+    width = 2 * half
+    owners = out_ref.shape[0]
+    share = half // owners
+    for slot in range(out_ref.shape[1] // (2 * share)):
+        raw = early_ref[slot * width : (slot + 1) * width, :] if slot < TAPS else 0.0
+        if slot:
+            raw = raw + late_ref[(slot - 1) * width : slot * width, :]
+        if slot < TAPS - 1:
+            raw = raw + handed_ref[slot * width : (slot + 1) * width, :].astype(jnp.float32)
+        real, imag = raw[:half], raw[half:]
+        out_real = gain_ref[0] * real - gain_ref[1] * imag
+        out_imag = gain_ref[0] * imag + gain_ref[1] * real
+        for owner in range(owners):
+            at = owner * share
+            pair = jnp.concatenate([out_real[at : at + share], out_imag[at : at + share]], axis=0)
+            at = 2 * share * slot
+            out_ref[owner, at : at + 2 * share, :] = pair.astype(jnp.bfloat16)
+
+
+def combine(early, late, handed, gains, frames, owners):
+    _, half, rows = gains.shape
+    return pl.pallas_call(
+        combine_kernel,
+        in_specs=[pl.BlockSpec(memory_space=pltpu.VMEM)] * 4,
+        out_specs=pl.BlockSpec(memory_space=pltpu.VMEM),
+        out_shape=jax.ShapeDtypeStruct((owners, frames * 2 * half // owners, rows), jnp.bfloat16),
+        compiler_params=pltpu.CompilerParams(vmem_limit_bytes=16 * 2**20),
+        name="combine",
+    )(early, late, handed, gains)
 
 
 def merge_kernel(frames, share, norm, in_ref, out_ref, left_ref, scratch):
@@ -171,9 +207,6 @@
         for frame in range(frames):
             at = 2 * share * frame
             value = in_ref[group, at : at + 2 * share, :].astype(jnp.float32)
-            if group > 0 and frame < TAPS - 1:
-                at = 2 * share * (frame + frames)
-                value = value + in_ref[group - 1, at : at + 2 * share, :].astype(jnp.float32)
             if value.shape[1] < 128 * blocks:
                 spare = jnp.zeros((2 * share, 128 * blocks - value.shape[1]), jnp.float32)
                 value = jnp.concatenate([value, spare], axis=1)
@@ -320,7 +353,13 @@
     owners = lax.axis_size("fgrp")
     share = channels // owners
     norm = 1.0 / math.sqrt(frames_here * owners)
-    partial = filter_all(voltages, filter_table(channels), jnp.swapaxes(gains, 1, 2), owners)
+    tables = filter_table(channels)
+    late, ending = filter_part(voltages, tables, 1, frames_here - 1, frames_here - 1)
+    voltages, ending = lax.optimization_barrier((voltages, ending))
+    handed = lax.ppermute(ending, "fgrp", [(i, i + 1) for i in range(owners - 1)])
+    (early,) = filter_part(voltages, tables, 0, 1, TAPS)
+    handed, early = lax.optimization_barrier((handed, early))
+    partial = combine(early, late, handed, jnp.swapaxes(gains, 1, 2), frames_here, owners)
     turned = lax.all_to_all(partial, "fgrp", split_axis=0, concat_axis=0, tiled=True)
     own, left = merge(turned, frames_here, share, norm)
     tiles, pols = lax.axis_size("tile"), lax.axis_size("pol")

time: 89.2 us -> 82.3 us (0.923)
  blocking collectives: 30.4 us -> 20.2 us
  starting transfers between devices: 1.77 us -> 6.65 us
  local copies, waits for them, and re-layouts: 4.36 us -> 0.01 us
  Pallas kernels: 52.1 us -> 54.6 us
    all_to_all x1, blocking collectives: 30.4 us -> 20.2 us  [body(): lax.all_to_all(partial, 'fgrp', split_axis=0, concat_axis=0, tiled=True)]
    ppermute x0 -> x1, starting transfers between devices: none -> 4.87 us  [body(): lax.ppermute(ending, 'fgrp', [(i, i + 1) for i in range(owners - 1)])]
    unnamed x6 -> x2, local copies, waits for them, and re-layouts: 4.36 us -> 0.01 us
    pallas_call x1 -> x3, Pallas kernels: 25.8 us -> 28.3 us  [the longest x2 28.1 us: filter_part(): pl.pallas_call(functools.partial(filter_kernel, frame, low_scale), in_spe...]
  transfers between devices with their start and end apart: 3 -> 4, of which waited for: 1 -> 2; matrix products, arithmetic and copies ran while one was open for 0% -> 0% of each run, Pallas kernels for 21% -> 33%
where the time goes in v9:
time: 82.3 us; the launch traced here: 82.1 us
  Pallas kernels  54.6 us (66%)
  blocking collectives  20.2 us (25%)
  starting transfers between devices  6.65 us (8%)
    pallas_call x2, Pallas kernels, filter_part(): pl.pallas_call(functools.partial(filter_kernel, frame, low_scale), in_spe...  28.1 us
    pallas_call x4, Pallas kernels, correlate(): pl.pallas_call(functools.partial(block_kernel, share), in_specs=specs, ou...  25.2 us
    all_to_all x1, blocking collectives, body(): lax.all_to_all(partial, 'fgrp', split_axis=0, concat_axis=0, tiled=True)  20.2 us
    ppermute x1, starting transfers between devices, body(): lax.ppermute(ending, 'fgrp', [(i, i + 1) for i in range(owners - 1)])  4.87 us
    ppermute x3, starting transfers between devices, swapped(): lax.ppermute(shard, axis, [(i, peer(i, step, length, 1)) for i in range(l...  1.77 us
  transfers between devices with their start and end apart: 4, of which 2 were waited for; matrix products, arithmetic and copies ran while one was open for 0% of the time, Pallas kernels for 33%

profile of v9, /device:TPU:0, one launch (start us, length us, event | category | flops | bytes accessed | tf_op | source)
XLA Modules:
  0.0 82.1 jit_solution(370459396130246262)
XLA Ops:
  0.0 0.0 copy-start
  0.0 20.0 %filter_part.2 = (f32[384,512]{1,0:T(8,128)S(1)}, bf16[384,512]{1,0:T(8,128)(2,1)S(1)}) custom-call(bf16[2,512,16384]{2,1,0:T(8,128)(2,1)} %volt_hbm.2, bf16[512,4096]{1,0:T(8,128)(2,1)} %constant.14.clone.table_hbm, f8e4m3fn[256,4096]{1,0:T(32,128)(4,1)} %constant.15.clone.low_hbm), custom_call_target="tpu_custom_call" | custom-call | flops 19327352832 | bytes 29360128 | tf_op jit(solution)/shard_map/filter_part/pallas_call | solution.py:143
  20.0 4.9 %collective-permute-start = (bf16[384,512]{1,0:T(8,128)(2,1)S(1)}, bf16[384,512]{1,0:T(8,128)(2,1)S(1)}, u32[]{:S(2)}, u32[]{:S(2)}) collective-permute-start(bf16[384,512]{1,0:T(8,128)(2,1)S(1)} %get-tuple-element.16), channel_id=1, source_target_pairs={{0,4},{4,8},{8,12},{12,16},{16,20},{20,24},{24,28},{1,5},{5,9},{9,... | collective-permute-start | bytes 1179656 | tf_op jit(solution)/shard_map/ppermute | solution.py:359
  24.9 8.1 %filter_part.3.early_ref = f32[512,512]{1,0:T(8,128)S(1)} custom-call(bf16[2,512,16384]{2,1,0:T(8,128)(2,1)} %volt_hbm.2, bf16[512,4096]{1,0:T(8,128)(2,1)} %constant.14.clone.table_hbm, f8e4m3fn[256,4096]{1,0:T(32,128)(4,1)} %constant.15.clone.low_hbm), custom_call_target="tpu_custom_call" | custom-call | flops 6442450944 | bytes 12582912 | tf_op jit(solution)/shard_map/filter_part/pallas_call | solution.py:143
  33.0 0.2 collective-permute-done.handed_ref
  33.2 0.0 copy-done
  33.2 0.2 combine.1
  33.4 20.2 %all_to_all.5.in_ref = bf16[8,64,512]{2,1,0:T(8,128)(2,1)S(1)} all-to-all(bf16[8,64,512]{2,1,0:T(8,128)(2,1)S(1)} %combine.1), channel_id=1, replica_groups=mesh['fgrp'=8,'tile'=2,'pol'=2] {'fgrp'}, dimensions={0} | all-to-all | bytes 1048576 | tf_op jit(solution)/shard_map/all_to_all | solution.py:363
  53.6 1.1 %merge.1 = (bf16[512,512]{1,0:T(8,128)(2,1)S(1)}, bf16[512,1024]{1,0:T(8,128)(2,1)S(1)}) custom-call(bf16[8,64,512]{2,1,0:T(8,128)(2,1)S(1)} %all_to_all.5.in_ref), custom_call_target="tpu_custom_call" | custom-call | tf_op jit(solution)/shard_map/merge/pallas_call | solution.py:236
  54.8 0.1 collective-permute-start.2
  54.9 1.6 %collective-permute-start.1 = (bf16[512,512]{1,0:T(8,128)(2,1)S(1)}, bf16[512,512]{1,0:T(8,128)(2,1)S(1)}, u32[]{:S(2)}, u32[]{:S(2)}) collective-permute-start(bf16[512,512]{1,0:T(8,128)(2,1)S(1)} %get-tuple-element.22.right_ref), channel_id=1, source_target_pairs={{0,1},{1,0},{2,3},{3,2},{4,5},{5,4},{6,7},{7,6},{8,9},{9,8},{10,11... | collective-permute-start | bytes 1572872 | tf_op jit(solution)/shard_map/ppermute | solution.py:346
  56.4 6.3 %correlate.4.refs_0_ = f32[8,2,512,2048]{3,2,1,0:T(8,128)} custom-call(s32[1]{0:T(128)} %bitcast.3.place_ref, bf16[512,1024]{1,0:T(8,128)(2,1)S(1)} %get-tuple-element.21.left_ref, bf16[512,512]{1,0:T(8,128)(2,1)S(1)} %get-tuple-element.22.right_ref), custom_call_target="tpu_custom_call" | custom-call | flops 1073741824 | bytes 16777216 | tf_op jit(solution)/shard_map/correlate/pallas_call | solution.py:297
  62.7 0.0 collective-permute-done.2.right_ref
  62.8 6.3 %correlate.5.refs_0_ = f32[8,2,512,2048]{3,2,1,0:T(8,128)} custom-call(s32[1]{0:T(128)} %bitcast.2.place_ref, bf16[512,1024]{1,0:T(8,128)(2,1)S(1)} %get-tuple-element.21.left_ref, bf16[512,512]{1,0:T(8,128)(2,1)S(1)} %collective-permute-done.2.right_ref, f32[8,2,512,2048]{3,2,1,0:T(8,128)} %correlate.4.refs_0_), custom_call_target="tpu_custom_call", output_to_operand_aliasing={{}: (3, {})} | custom-call | flops 1073741824 | bytes 16777216 | tf_op jit(solution)/shard_map/correlate/pallas_call | solution.py:297
  69.1 0.1 collective-permute-done.1.right_ref
  69.2 0.1 collective-permute-start.3
  69.3 6.3 %correlate.6.refs_0_ = f32[8,2,512,2048]{3,2,1,0:T(8,128)} custom-call(s32[1]{0:T(128)} %bitcast.4.place_ref, bf16[512,1024]{1,0:T(8,128)(2,1)S(1)} %get-tuple-element.21.left_ref, bf16[512,512]{1,0:T(8,128)(2,1)S(1)} %collective-permute-done.1.right_ref, f32[8,2,512,2048]{3,2,1,0:T(8,128)} %correlate.5.refs_0_), custom_call_target="tpu_custom_call", output_to_operand_aliasing={{}: (3, {})} | custom-call | flops 1073741824 | bytes 16777216 | tf_op jit(solution)/shard_map/correlate/pallas_call | solution.py:297
  75.6 0.0 collective-permute-done.3.right_ref
  75.6 6.3 %correlate.7 = f32[8,2,512,2048]{3,2,1,0:T(8,128)} custom-call(s32[1]{0:T(128)} %bitcast.place_ref, bf16[512,1024]{1,0:T(8,128)(2,1)S(1)} %get-tuple-element.21.left_ref, bf16[512,512]{1,0:T(8,128)(2,1)S(1)} %collective-permute-done.3.right_ref, f32[8,2,512,2048]{3,2,1,0:T(8,128)} %correlate.6.refs_0_), custom_call_target="tpu_custom_call", output_to_operand_aliasing={{}: (3, {})} | custom-call | flops 1073741824 | bytes 16777216 | tf_op jit(solution)/shard_map/correlate/pallas_call | solution.py:297
Async XLA Ops:
  0.0 33.2 %copy-start = (f32[2,512,64]{1,2,0:T(8,128)S(1)}, f32[2,512,64]{1,2,0:T(8,128)}, u32[]{:S(2)}) copy-start(f32[2,512,64]{1,2,0:T(8,128)} %param.5) | copy-start | bytes 786436
  20.0 13.2 %collective-permute-start = (bf16[384,512]{1,0:T(8,128)(2,1)S(1)}, bf16[384,512]{1,0:T(8,128)(2,1)S(1)}, u32[]{:S(2)}, u32[]{:S(2)}) collective-permute-start(bf16[384,512]{1,0:T(8,128)(2,1)S(1)} %get-tuple-element.16), channel_id=1, source_target_pairs={{0,4},{4,8},{8,12},{12,16},{16,20},{20,24},{24,28},{1,5},{5,9},{9,... | collective-permute-start | bytes 1179656 | tf_op jit(solution)/shard_map/ppermute | solution.py:359
  54.8 8.0 %collective-permute-start.2 = (bf16[512,512]{1,0:T(8,128)(2,1)S(1)}, bf16[512,512]{1,0:T(8,128)(2,1)S(1)}, u32[]{:S(2)}, u32[]{:S(2)}) collective-permute-start(bf16[512,512]{1,0:T(8,128)(2,1)S(1)} %get-tuple-element.22.right_ref), channel_id=1, source_target_pairs={{0,2},{2,0},{1,3},{3,1},{4,6},{6,4},{5,7},{7,5},{8,10},{10,8},{9,1... | collective-permute-start | bytes 1572872 | tf_op jit(solution)/shard_map/ppermute | solution.py:346
  54.9 14.3 %collective-permute-start.1 = (bf16[512,512]{1,0:T(8,128)(2,1)S(1)}, bf16[512,512]{1,0:T(8,128)(2,1)S(1)}, u32[]{:S(2)}, u32[]{:S(2)}) collective-permute-start(bf16[512,512]{1,0:T(8,128)(2,1)S(1)} %get-tuple-element.22.right_ref), channel_id=1, source_target_pairs={{0,1},{1,0},{2,3},{3,2},{4,5},{5,4},{6,7},{7,6},{8,9},{9,8},{10,11... | collective-permute-start | bytes 1572872 | tf_op jit(solution)/shard_map/ppermute | solution.py:346
  69.2 6.4 %collective-permute-start.3 = (bf16[512,512]{1,0:T(8,128)(2,1)S(1)}, bf16[512,512]{1,0:T(8,128)(2,1)S(1)}, u32[]{:S(2)}, u32[]{:S(2)}) collective-permute-start(bf16[512,512]{1,0:T(8,128)(2,1)S(1)} %collective-permute-done.1.right_ref), channel_id=1, source_target_pairs={{0,2},{2,0},{1,3},{3,1},{4,6},{6,4},{5,7},{7,5},{8,10},{10,8},{9,1... | collective-permute-start | bytes 1572872 | tf_op jit(solution)/shard_map/ppermute | solution.py:346

commit v10 on v9

--- a/solution.py
+++ b/solution.py
@@ -166,7 +166,7 @@
     )(voltages, jnp.asarray(table), jnp.asarray(low_table))
 
 
-def combine_kernel(early_ref, late_ref, handed_ref, gain_ref, out_ref):
+def combine_kernel(early_ref, late_ref, odd_ref, even_ref, gain_ref, out_ref):
     half = gain_ref.shape[1]
     width = 2 * half
     owners = out_ref.shape[0]
@@ -176,7 +176,8 @@
         if slot:
             raw = raw + late_ref[(slot - 1) * width : slot * width, :]
         if slot < TAPS - 1:
-            raw = raw + handed_ref[slot * width : (slot + 1) * width, :].astype(jnp.float32)
+            for handed_ref in (odd_ref, even_ref):
+                raw = raw + handed_ref[slot * width : (slot + 1) * width, :].astype(jnp.float32)
         real, imag = raw[:half], raw[half:]
         out_real = gain_ref[0] * real - gain_ref[1] * imag
         out_imag = gain_ref[0] * imag + gain_ref[1] * real
@@ -187,16 +188,16 @@
             out_ref[owner, at : at + 2 * share, :] = pair.astype(jnp.bfloat16)
 
 
-def combine(early, late, handed, gains, frames, owners):
+def combine(early, late, to_odd, to_even, gains, frames, owners):
     _, half, rows = gains.shape
     return pl.pallas_call(
         combine_kernel,
-        in_specs=[pl.BlockSpec(memory_space=pltpu.VMEM)] * 4,
+        in_specs=[pl.BlockSpec(memory_space=pltpu.VMEM)] * 5,
         out_specs=pl.BlockSpec(memory_space=pltpu.VMEM),
         out_shape=jax.ShapeDtypeStruct((owners, frames * 2 * half // owners, rows), jnp.bfloat16),
         compiler_params=pltpu.CompilerParams(vmem_limit_bytes=16 * 2**20),
         name="combine",
-    )(early, late, handed, gains)
+    )(early, late, to_odd, to_even, gains)
 
 
 def merge_kernel(frames, share, norm, in_ref, out_ref, left_ref, scratch):
@@ -246,15 +247,12 @@
     )(turned)
 
 
-def visibility(left, right):
-    half = right.shape[0] // 2
-    crossed = jnp.concatenate([-right[half:], right[:half]], axis=0)
-    return [
-        jnp.dot(
-            left, jnp.concatenate([value, value], axis=0), preferred_element_type=jnp.float32
-        )
-        for value in (right, crossed)
-    ]
+def visibility(left, right, kind):
+    if kind:
+        half = right.shape[0] // 2
+        right = jnp.concatenate([-right[half:], right[:half]], axis=0)
+    both = jnp.concatenate([right, right], axis=0)
+    return jnp.dot(left, both, preferred_element_type=jnp.float32)
 
 
 def block_kernel(share, place_ref, left_ref, right_ref, *refs):
@@ -264,23 +262,25 @@
     slots = values.shape[0]
     columns = pl.ds(pl.multiple_of(place_ref[0] * rows, rows), rows)
 
-    def write(channel):
+    def write(channel, kind):
         slot = channel % slots
         return pltpu.make_async_copy(
-            values.at[slot], out_hbm.at[channel, :, :, columns], written.at[slot]
+            values.at[slot, kind], out_hbm.at[channel, kind, :, columns], written.at[slot, kind]
         )
 
     for channel in range(share):
         slot = channel % slots
-        if channel >= slots:
-            write(channel - slots).wait()
-        values[slot, 0], values[slot, 1] = visibility(
-            left_ref[:, 2 * depth * channel : 2 * depth * (channel + 1)],
-            right_ref[depth * channel : depth * (channel + 1), :],
-        )
-        write(channel).start()
+        right = right_ref[depth * channel : depth * (channel + 1), :]
+        for kind in range(2):
+            if channel >= slots:
+                write(channel - slots, kind).wait()
+            values[slot, kind] = visibility(
+                left_ref[:, 2 * depth * channel : 2 * depth * (channel + 1)], right, kind
+            )
+            write(channel, kind).start()
     for channel in range(max(share - slots, 0), share):
-        write(channel).wait()
+        for kind in range(2):
+            write(channel, kind).wait()
 
 
 def correlate(left, right, place, total, result, share):
@@ -301,7 +301,7 @@
         out_shape=jax.ShapeDtypeStruct((share, 2, rows, total), jnp.float32),
         scratch_shapes=[
             pltpu.VMEM((slots, 2, rows, rows), jnp.float32),
-            pltpu.SemaphoreType.DMA((slots,)),
+            pltpu.SemaphoreType.DMA((slots, 2)),
         ],
         input_output_aliases=aliases,
         compiler_params=pltpu.CompilerParams(vmem_limit_bytes=24 * 2**20),
@@ -317,9 +317,10 @@
 def whole_kernel(left_ref, all_ref, out_ref):
     rows = left_ref.shape[0]
     for group in range(all_ref.shape[0]):
-        values = visibility(left_ref[...], all_ref[group])
         for kind in range(2):
-            out_ref[0, kind, :, group * rows : (group + 1) * rows] = values[kind]
+            out_ref[0, kind, :, group * rows : (group + 1) * rows] = visibility(
+                left_ref[...], all_ref[group], kind
+            )
 
 
 def correlate_whole(left, gathered, share):
@@ -356,10 +357,13 @@
     tables = filter_table(channels)
     late, ending = filter_part(voltages, tables, 1, frames_here - 1, frames_here - 1)
     voltages, ending = lax.optimization_barrier((voltages, ending))
-    handed = lax.ppermute(ending, "fgrp", [(i, i + 1) for i in range(owners - 1)])
+    handed = [
+        lax.ppermute(ending, "fgrp", [(i, i + 1) for i in range(first, owners - 1, 2)])
+        for first in range(2)
+    ]
     (early,) = filter_part(voltages, tables, 0, 1, TAPS)
     handed, early = lax.optimization_barrier((handed, early))
-    partial = combine(early, late, handed, jnp.swapaxes(gains, 1, 2), frames_here, owners)
+    partial = combine(early, late, *handed, jnp.swapaxes(gains, 1, 2), frames_here, owners)
     turned = lax.all_to_all(partial, "fgrp", split_axis=0, concat_axis=0, tiled=True)
     own, left = merge(turned, frames_here, share, norm)
     tiles, pols = lax.axis_size("tile"), lax.axis_size("pol")

time: 82.3 us -> 83.9 us (1.019)
  starting transfers between devices: 6.65 us -> 10 us
  blocking collectives: 20.2 us -> 18.8 us
    ppermute x1 -> x2, starting transfers between devices: 4.87 us -> 8.35 us  [body(): lax.ppermute(ending, 'fgrp', [(i, i + 1) for i in range(first, owners - 1...]
    all_to_all x1, blocking collectives: 20.2 us -> 18.8 us  [body(): lax.all_to_all(partial, 'fgrp', split_axis=0, concat_axis=0, tiled=True)]
  transfers between devices with their start and end apart: 4 -> 5, of which waited for: 2 -> 1; matrix products, arithmetic and copies ran while one was open for 0% -> 0% of each run, Pallas kernels for 33% -> 32%
where the time goes in v10:
time: 83.9 us; the launch traced here: 83.6 us
  Pallas kernels  54.1 us (64%)
  blocking collectives  18.8 us (22%)
  starting transfers between devices  10 us (12%)
    pallas_call x2, Pallas kernels, filter_part(): pl.pallas_call(functools.partial(filter_kernel, frame, low_scale), in_spe...  28.1 us
    pallas_call x4, Pallas kernels, correlate(): pl.pallas_call(functools.partial(block_kernel, share), in_specs=specs, ou...  24.7 us
    all_to_all x1, blocking collectives, body(): lax.all_to_all(partial, 'fgrp', split_axis=0, concat_axis=0, tiled=True)  18.8 us
    ppermute x2, starting transfers between devices, body(): lax.ppermute(ending, 'fgrp', [(i, i + 1) for i in range(first, owners - 1...  8.35 us
  transfers between devices with their start and end apart: 5, of which 1 were waited for; matrix products, arithmetic and copies ran while one was open for 0% of the time, Pallas kernels for 32%

profile of v10, /device:TPU:0, one launch (start us, length us, event | category | flops | bytes accessed | tf_op | source)
XLA Modules:
  0.0 83.6 jit_solution(2953660269600530620)
XLA Ops:
  0.0 0.0 copy-start
  0.0 20.0 %filter_part.2 = (f32[384,512]{1,0:T(8,128)S(1)}, bf16[384,512]{1,0:T(8,128)(2,1)S(1)}) custom-call(bf16[2,512,16384]{2,1,0:T(8,128)(2,1)} %volt_hbm.2, bf16[512,4096]{1,0:T(8,128)(2,1)} %constant.14.clone.table_hbm, f8e4m3fn[256,4096]{1,0:T(32,128)(4,1)} %constant.15.clone.low_hbm), custom_call_target="tpu_custom_call" | custom-call | flops 19327352832 | bytes 29360128 | tf_op jit(solution)/shard_map/filter_part/pallas_call | solution.py:143
  20.0 0.7 collective-permute-start.1
  20.7 7.7 %collective-permute-start = (bf16[384,512]{1,0:T(8,128)(2,1)S(1)}, bf16[384,512]{1,0:T(8,128)(2,1)S(1)}, u32[]{:S(2)}, u32[]{:S(2)}) collective-permute-start(bf16[384,512]{1,0:T(8,128)(2,1)S(1)} %get-tuple-element.17), channel_id=1, source_target_pairs={{0,4},{8,12},{16,20},{24,28},{1,5},{9,13},{17,21},{25,29},{2,6},{1... | collective-permute-start | bytes 1179656 | tf_op jit(solution)/shard_map/ppermute | solution.py:361
  28.4 8.1 %filter_part.3.early_ref = f32[512,512]{1,0:T(8,128)S(1)} custom-call(bf16[2,512,16384]{2,1,0:T(8,128)(2,1)} %volt_hbm.2, bf16[512,4096]{1,0:T(8,128)(2,1)} %constant.14.clone.table_hbm, f8e4m3fn[256,4096]{1,0:T(32,128)(4,1)} %constant.15.clone.low_hbm), custom_call_target="tpu_custom_call" | custom-call | flops 6442450944 | bytes 12582912 | tf_op jit(solution)/shard_map/filter_part/pallas_call | solution.py:143
  36.5 0.0 collective-permute-done.1.even_ref
  36.5 0.0 collective-permute-done.odd_ref
  36.5 0.0 copy-done
  36.5 0.3 combine.1
  36.7 18.8 %all_to_all.5.in_ref = bf16[8,64,512]{2,1,0:T(8,128)(2,1)S(1)} all-to-all(bf16[8,64,512]{2,1,0:T(8,128)(2,1)S(1)} %combine.1), channel_id=1, replica_groups=mesh['fgrp'=8,'tile'=2,'pol'=2] {'fgrp'}, dimensions={0} | all-to-all | bytes 1048576 | tf_op jit(solution)/shard_map/all_to_all | solution.py:367
  55.6 1.1 %merge.1 = (bf16[512,512]{1,0:T(8,128)(2,1)S(1)}, bf16[512,1024]{1,0:T(8,128)(2,1)S(1)}) custom-call(bf16[8,64,512]{2,1,0:T(8,128)(2,1)S(1)} %all_to_all.5.in_ref), custom_call_target="tpu_custom_call" | custom-call | tf_op jit(solution)/shard_map/merge/pallas_call | solution.py:237
  56.7 0.1 collective-permute-start.3
  56.8 1.6 %collective-permute-start.2 = (bf16[512,512]{1,0:T(8,128)(2,1)S(1)}, bf16[512,512]{1,0:T(8,128)(2,1)S(1)}, u32[]{:S(2)}, u32[]{:S(2)}) collective-permute-start(bf16[512,512]{1,0:T(8,128)(2,1)S(1)} %get-tuple-element.24.right_ref), channel_id=1, source_target_pairs={{0,1},{1,0},{2,3},{3,2},{4,5},{5,4},{6,7},{7,6},{8,9},{9,8},{10,11... | collective-permute-start | bytes 1572872 | tf_op jit(solution)/shard_map/ppermute | solution.py:347
  58.4 6.2 %correlate.4.refs_0_ = f32[8,2,512,2048]{3,2,1,0:T(8,128)} custom-call(s32[1]{0:T(128)} %bitcast.3.place_ref, bf16[512,1024]{1,0:T(8,128)(2,1)S(1)} %get-tuple-element.23.left_ref, bf16[512,512]{1,0:T(8,128)(2,1)S(1)} %get-tuple-element.24.right_ref), custom_call_target="tpu_custom_call" | custom-call | flops 1073741824 | bytes 16777216 | tf_op jit(solution)/shard_map/correlate/pallas_call | solution.py:297
  64.5 0.0 collective-permute-done.3.right_ref
  64.6 6.2 %correlate.5.refs_0_ = f32[8,2,512,2048]{3,2,1,0:T(8,128)} custom-call(s32[1]{0:T(128)} %bitcast.2.place_ref, bf16[512,1024]{1,0:T(8,128)(2,1)S(1)} %get-tuple-element.23.left_ref, bf16[512,512]{1,0:T(8,128)(2,1)S(1)} %collective-permute-done.3.right_ref, f32[8,2,512,2048]{3,2,1,0:T(8,128)} %correlate.4.refs_0_), custom_call_target="tpu_custom_call", output_to_operand_aliasing={{}: (3, {})} | custom-call | flops 1073741824 | bytes 16777216 | tf_op jit(solution)/shard_map/correlate/pallas_call | solution.py:297
  70.7 0.4 collective-permute-done.2.right_ref
  71.1 0.0 collective-permute-start.4
  71.1 6.2 %correlate.6.refs_0_ = f32[8,2,512,2048]{3,2,1,0:T(8,128)} custom-call(s32[1]{0:T(128)} %bitcast.4.place_ref, bf16[512,1024]{1,0:T(8,128)(2,1)S(1)} %get-tuple-element.23.left_ref, bf16[512,512]{1,0:T(8,128)(2,1)S(1)} %collective-permute-done.2.right_ref, f32[8,2,512,2048]{3,2,1,0:T(8,128)} %correlate.5.refs_0_), custom_call_target="tpu_custom_call", output_to_operand_aliasing={{}: (3, {})} | custom-call | flops 1073741824 | bytes 16777216 | tf_op jit(solution)/shard_map/correlate/pallas_call | solution.py:297
  77.3 0.0 collective-permute-done.4.right_ref
  77.3 6.2 %correlate.7 = f32[8,2,512,2048]{3,2,1,0:T(8,128)} custom-call(s32[1]{0:T(128)} %bitcast.place_ref, bf16[512,1024]{1,0:T(8,128)(2,1)S(1)} %get-tuple-element.23.left_ref, bf16[512,512]{1,0:T(8,128)(2,1)S(1)} %collective-permute-done.4.right_ref, f32[8,2,512,2048]{3,2,1,0:T(8,128)} %correlate.6.refs_0_), custom_call_target="tpu_custom_call", output_to_operand_aliasing={{}: (3, {})} | custom-call | flops 1073741824 | bytes 16777216 | tf_op jit(solution)/shard_map/correlate/pallas_call | solution.py:297
Async XLA Ops:
  0.0 36.5 %copy-start = (f32[2,512,64]{1,2,0:T(8,128)S(1)}, f32[2,512,64]{1,2,0:T(8,128)}, u32[]{:S(2)}) copy-start(f32[2,512,64]{1,2,0:T(8,128)} %param.5) | copy-start | bytes 786436
  20.0 16.4 %collective-permute-start.1 = (bf16[384,512]{1,0:T(8,128)(2,1)S(1)}, bf16[384,512]{1,0:T(8,128)(2,1)S(1)}, u32[]{:S(2)}, u32[]{:S(2)}) collective-permute-start(bf16[384,512]{1,0:T(8,128)(2,1)S(1)} %get-tuple-element.17), channel_id=1, source_target_pairs={{4,8},{12,16},{20,24},{5,9},{13,17},{21,25},{6,10},{14,18},{22,26}... | collective-permute-start | bytes 1179656 | tf_op jit(solution)/shard_map/ppermute | solution.py:361
  20.7 15.8 %collective-permute-start = (bf16[384,512]{1,0:T(8,128)(2,1)S(1)}, bf16[384,512]{1,0:T(8,128)(2,1)S(1)}, u32[]{:S(2)}, u32[]{:S(2)}) collective-permute-start(bf16[384,512]{1,0:T(8,128)(2,1)S(1)} %get-tuple-element.17), channel_id=1, source_target_pairs={{0,4},{8,12},{16,20},{24,28},{1,5},{9,13},{17,21},{25,29},{2,6},{1... | collective-permute-start | bytes 1179656 | tf_op jit(solution)/shard_map/ppermute | solution.py:361
  56.7 7.8 %collective-permute-start.3 = (bf16[512,512]{1,0:T(8,128)(2,1)S(1)}, bf16[512,512]{1,0:T(8,128)(2,1)S(1)}, u32[]{:S(2)}, u32[]{:S(2)}) collective-permute-start(bf16[512,512]{1,0:T(8,128)(2,1)S(1)} %get-tuple-element.24.right_ref), channel_id=1, source_target_pairs={{0,2},{2,0},{1,3},{3,1},{4,6},{6,4},{5,7},{7,5},{8,10},{10,8},{9,1... | collective-permute-start | bytes 1572872 | tf_op jit(solution)/shard_map/ppermute | solution.py:347
  56.8 14.3 %collective-permute-start.2 = (bf16[512,512]{1,0:T(8,128)(2,1)S(1)}, bf16[512,512]{1,0:T(8,128)(2,1)S(1)}, u32[]{:S(2)}, u32[]{:S(2)}) collective-permute-start(bf16[512,512]{1,0:T(8,128)(2,1)S(1)} %get-tuple-element.24.right_ref), channel_id=1, source_target_pairs={{0,1},{1,0},{2,3},{3,2},{4,5},{5,4},{6,7},{7,6},{8,9},{9,8},{10,11... | collective-permute-start | bytes 1572872 | tf_op jit(solution)/shard_map/ppermute | solution.py:347
  71.1 6.2 %collective-permute-start.4 = (bf16[512,512]{1,0:T(8,128)(2,1)S(1)}, bf16[512,512]{1,0:T(8,128)(2,1)S(1)}, u32[]{:S(2)}, u32[]{:S(2)}) collective-permute-start(bf16[512,512]{1,0:T(8,128)(2,1)S(1)} %collective-permute-done.2.right_ref), channel_id=1, source_target_pairs={{0,2},{2,0},{1,3},{3,1},{4,6},{6,4},{5,7},{7,5},{8,10},{10,8},{9,1... | collective-permute-start | bytes 1572872 | tf_op jit(solution)/shard_map/ppermute | solution.py:347

commit v11 on v10

--- a/solution.py
+++ b/solution.py
@@ -48,14 +48,14 @@
     return me ^ step
 
 
-def filter_kernel(frame, low_scale, volt_hbm, table_hbm, low_hbm, *refs):
+def filter_kernel(frame, low_from, low_scale, volt_hbm, table_hbm, low_hbm, *refs):
     out_refs, scratch = refs[:-9], refs[-9:]
     sums, low_sums, volts, table, low_table, volt_here, first_here, table_here, low_here = scratch
     order, low_order = tap_order()
     width = table.shape[0] // len(order)
     half = width // 2
     count = sums.shape[1] // width - (TAPS - 1)
-    steps = 2 * count
+    steps = 2 * (low_sums.shape[1] // width - (len(low_order) - 1))
     pieces = first_here.shape[0]
     depth = NFFT // pieces
 
@@ -86,10 +86,15 @@
         part = lax.rem(step, 2)
         first = pl.multiple_of(lax.div(step, 2) * width, width)
         here = pl.ds(first, len(order) * width)
-        low = pl.ds(first, len(low_order) * width)
         values = volts[part, :, start : start + size]
         sums[part, here, :] += product(table[:, start : start + size], values)
-        low_sums[part, low, :] += product(
+
+    def add_low(step, start, size):
+        part = lax.rem(step, 2)
+        first = pl.multiple_of(lax.div(step, 2) * width, width)
+        here = pl.ds(first, len(low_order) * width)
+        values = volts[part, :, start : start + size]
+        low_sums[part, here, :] += product(
             low_table[:, start : start + size], values.astype(jnp.float8_e4m3fn)
         )
 
@@ -103,6 +108,8 @@
         for copy in fetch(piece):
             copy.wait()
         add(0, piece * depth, depth)
+        if low_from == 0:
+            add_low(0, piece * depth, depth)
 
     @pl.loop(1, steps)
     def _(step):
@@ -112,7 +119,24 @@
         def _():
             block(step + 1).start()
 
-        add(step, 0, NFFT)
+        whole = (step < 2 * count) & (step >= 2 * low_from)
+
+        @pl.when(whole)
+        def _():
+            add(step, 0, NFFT)
+            add_low(step, 0, NFFT)
+
+        if low_from > 0:
+
+            @pl.when(step < 2 * low_from)
+            def _():
+                add(step, 0, NFFT)
+
+        if 2 * count < steps:
+
+            @pl.when(step >= 2 * count)
+            def _():
+                add_low(step, 0, NFFT)
 
     kept = out_refs[0].shape[0] // width
     for slot in range(sums.shape[1] // width):
@@ -130,18 +154,18 @@
             out_refs[1][at : at + width, :] = raw.astype(jnp.bfloat16)
 
 
-def filter_part(voltages, tables, frame, count, kept):
+def filter_part(voltages, tables, frame, count, low_from, low_to, kept):
     rows = voltages.shape[1]
     table, low_table, low_scale = tables
     width = table.shape[0] // TAPS
     slots = count + TAPS - 1
-    low_slots = count + len(tap_order()[1]) - 1
+    low_slots = low_to + len(tap_order()[1]) - 1
     shapes = [jax.ShapeDtypeStruct((kept * width, rows), jnp.float32)]
     if slots > kept:
         shapes.append(jax.ShapeDtypeStruct(((slots - kept) * width, rows), jnp.bfloat16))
     pieces = 4
     return pl.pallas_call(
-        functools.partial(filter_kernel, frame, low_scale),
+        functools.partial(filter_kernel, frame, low_from, low_scale),
         in_specs=[pl.BlockSpec(memory_space=pl.ANY)] * 3,
         out_specs=[pl.BlockSpec(memory_space=pltpu.VMEM)] * len(shapes),
         out_shape=shapes,
@@ -166,7 +190,7 @@
     )(voltages, jnp.asarray(table), jnp.asarray(low_table))
 
 
-def combine_kernel(early_ref, late_ref, odd_ref, even_ref, gain_ref, out_ref):
+def combine_kernel(early_ref, late_ref, handed_ref, gain_ref, out_ref):
     half = gain_ref.shape[1]
     width = 2 * half
     owners = out_ref.shape[0]
@@ -176,8 +200,7 @@
         if slot:
             raw = raw + late_ref[(slot - 1) * width : slot * width, :]
         if slot < TAPS - 1:
-            for handed_ref in (odd_ref, even_ref):
-                raw = raw + handed_ref[slot * width : (slot + 1) * width, :].astype(jnp.float32)
+            raw = raw + handed_ref[slot * width : (slot + 1) * width, :].astype(jnp.float32)
         real, imag = raw[:half], raw[half:]
         out_real = gain_ref[0] * real - gain_ref[1] * imag
         out_imag = gain_ref[0] * imag + gain_ref[1] * real
@@ -188,16 +211,16 @@
             out_ref[owner, at : at + 2 * share, :] = pair.astype(jnp.bfloat16)
 
 
-def combine(early, late, to_odd, to_even, gains, frames, owners):
+def combine(early, late, handed, gains, frames, owners):
     _, half, rows = gains.shape
     return pl.pallas_call(
         combine_kernel,
-        in_specs=[pl.BlockSpec(memory_space=pltpu.VMEM)] * 5,
+        in_specs=[pl.BlockSpec(memory_space=pltpu.VMEM)] * 4,
         out_specs=pl.BlockSpec(memory_space=pltpu.VMEM),
         out_shape=jax.ShapeDtypeStruct((owners, frames * 2 * half // owners, rows), jnp.bfloat16),
         compiler_params=pltpu.CompilerParams(vmem_limit_bytes=16 * 2**20),
         name="combine",
-    )(early, late, to_odd, to_even, gains)
+    )(early, late, handed, gains)
 
 
 def merge_kernel(frames, share, norm, in_ref, out_ref, left_ref, scratch):
@@ -355,15 +378,14 @@
     share = channels // owners
     norm = 1.0 / math.sqrt(frames_here * owners)
     tables = filter_table(channels)
-    late, ending = filter_part(voltages, tables, 1, frames_here - 1, frames_here - 1)
+    late, ending = filter_part(
+        voltages, tables, 1, frames_here - 1, 1, frames_here - 1, frames_here - 1
+    )
     voltages, ending = lax.optimization_barrier((voltages, ending))
-    handed = [
-        lax.ppermute(ending, "fgrp", [(i, i + 1) for i in range(first, owners - 1, 2)])
-        for first in range(2)
-    ]
-    (early,) = filter_part(voltages, tables, 0, 1, TAPS)
+    handed = lax.ppermute(ending, "fgrp", [(i, i + 1) for i in range(owners - 1)])
+    (early,) = filter_part(voltages, tables, 0, 1, 0, 2, TAPS)
     handed, early = lax.optimization_barrier((handed, early))
-    partial = combine(early, late, *handed, jnp.swapaxes(gains, 1, 2), frames_here, owners)
+    partial = combine(early, late, handed, jnp.swapaxes(gains, 1, 2), frames_here, owners)
     turned = lax.all_to_all(partial, "fgrp", split_axis=0, concat_axis=0, tiled=True)
     own, left = merge(turned, frames_here, share, norm)
     tiles, pols = lax.axis_size("tile"), lax.axis_size("pol")

time: 83.9 us -> 83.1 us (level)
  starting transfers between devices: 10 us -> 6.69 us
  Pallas kernels: 54.1 us -> 56.6 us
    ppermute x2 -> x1, starting transfers between devices: 8.35 us -> 5.05 us  [body(): lax.ppermute(ending, 'fgrp', [(i, i + 1) for i in range(owners - 1)])]
    pallas_call x2, Pallas kernels: 28.1 us -> 30.6 us  [filter_part(): pl.pallas_call(functools.partial(filter_kernel, frame, low_from, low_scal...]
  transfers between devices with their start and end apart: 5 -> 4, of which waited for: 1 -> 1; matrix products, arithmetic and copies ran while one was open for 0% -> 0% of each run, Pallas kernels for 32% -> 36%
where the time goes in v11:
time: 83.1 us; the launch traced here: 82.9 us
  Pallas kernels  56.6 us (68%)
  blocking collectives  18.9 us (23%)
  starting transfers between devices  6.69 us (8%)
    pallas_call x2, Pallas kernels, filter_part(): pl.pallas_call(functools.partial(filter_kernel, frame, low_from, low_scal...  30.6 us
    pallas_call x4, Pallas kernels, correlate(): pl.pallas_call(functools.partial(block_kernel, share), in_specs=specs, ou...  24.7 us
    all_to_all x1, blocking collectives, body(): lax.all_to_all(partial, 'fgrp', split_axis=0, concat_axis=0, tiled=True)  18.9 us
    ppermute x1, starting transfers between devices, body(): lax.ppermute(ending, 'fgrp', [(i, i + 1) for i in range(owners - 1)])  5.05 us
  transfers between devices with their start and end apart: 4, of which 1 were waited for; matrix products, arithmetic and copies ran while one was open for 0% of the time, Pallas kernels for 36%

profile of v11, /device:TPU:0, one launch (start us, length us, event | category | flops | bytes accessed | tf_op | source)
XLA Modules:
  0.0 82.9 jit_solution(11869358507088902336)
XLA Ops:
  0.0 0.0 copy-start
  0.0 19.5 %filter_part.2 = (f32[384,512]{1,0:T(8,128)S(1)}, bf16[384,512]{1,0:T(8,128)(2,1)S(1)}) custom-call(bf16[2,512,16384]{2,1,0:T(8,128)(2,1)} %volt_hbm.2, bf16[512,4096]{1,0:T(8,128)(2,1)} %constant.14.clone.table_hbm, f8e4m3fn[256,4096]{1,0:T(32,128)(4,1)} %constant.15.clone.low_hbm), custom_call_target="tpu_custom_call" | custom-call | flops 19327352832 | bytes 29360128 | tf_op jit(solution)/shard_map/filter_part/pallas_call | solution.py:167
  19.5 5.0 %collective-permute-start = (bf16[384,512]{1,0:T(8,128)(2,1)S(1)}, bf16[384,512]{1,0:T(8,128)(2,1)S(1)}, u32[]{:S(2)}, u32[]{:S(2)}) collective-permute-start(bf16[384,512]{1,0:T(8,128)(2,1)S(1)} %get-tuple-element.16), channel_id=1, source_target_pairs={{0,4},{4,8},{8,12},{12,16},{16,20},{20,24},{24,28},{1,5},{5,9},{9,... | collective-permute-start | bytes 1179656 | tf_op jit(solution)/shard_map/ppermute | solution.py:385
  24.6 11.1 %filter_part.3.early_ref = f32[512,512]{1,0:T(8,128)S(1)} custom-call(bf16[2,512,16384]{2,1,0:T(8,128)(2,1)} %volt_hbm.2, bf16[512,4096]{1,0:T(8,128)(2,1)} %constant.14.clone.table_hbm, f8e4m3fn[256,4096]{1,0:T(32,128)(4,1)} %constant.15.clone.low_hbm), custom_call_target="tpu_custom_call" | custom-call | flops 6442450944 | bytes 12582912 | tf_op jit(solution)/shard_map/filter_part/pallas_call | solution.py:167
  35.7 0.0 collective-permute-done.handed_ref
  35.7 0.0 copy-done
  35.7 0.2 combine.1
  35.9 18.9 %all_to_all.5.in_ref = bf16[8,64,512]{2,1,0:T(8,128)(2,1)S(1)} all-to-all(bf16[8,64,512]{2,1,0:T(8,128)(2,1)S(1)} %combine.1), channel_id=1, replica_groups=mesh['fgrp'=8,'tile'=2,'pol'=2] {'fgrp'}, dimensions={0} | all-to-all | bytes 1048576 | tf_op jit(solution)/shard_map/all_to_all | solution.py:389
  54.8 1.1 %merge.1 = (bf16[512,512]{1,0:T(8,128)(2,1)S(1)}, bf16[512,1024]{1,0:T(8,128)(2,1)S(1)}) custom-call(bf16[8,64,512]{2,1,0:T(8,128)(2,1)S(1)} %all_to_all.5.in_ref), custom_call_target="tpu_custom_call" | custom-call | tf_op jit(solution)/shard_map/merge/pallas_call | solution.py:260
  55.9 0.1 collective-permute-start.2
  56.0 1.6 %collective-permute-start.1 = (bf16[512,512]{1,0:T(8,128)(2,1)S(1)}, bf16[512,512]{1,0:T(8,128)(2,1)S(1)}, u32[]{:S(2)}, u32[]{:S(2)}) collective-permute-start(bf16[512,512]{1,0:T(8,128)(2,1)S(1)} %get-tuple-element.22.right_ref), channel_id=1, source_target_pairs={{0,1},{1,0},{2,3},{3,2},{4,5},{5,4},{6,7},{7,6},{8,9},{9,8},{10,11... | collective-permute-start | bytes 1572872 | tf_op jit(solution)/shard_map/ppermute | solution.py:370
  57.6 6.2 %correlate.4.refs_0_ = f32[8,2,512,2048]{3,2,1,0:T(8,128)} custom-call(s32[1]{0:T(128)} %bitcast.3.place_ref, bf16[512,1024]{1,0:T(8,128)(2,1)S(1)} %get-tuple-element.21.left_ref, bf16[512,512]{1,0:T(8,128)(2,1)S(1)} %get-tuple-element.22.right_ref), custom_call_target="tpu_custom_call" | custom-call | flops 1073741824 | bytes 16777216 | tf_op jit(solution)/shard_map/correlate/pallas_call | solution.py:320
  63.7 0.0 collective-permute-done.2.right_ref
  63.7 6.2 %correlate.5.refs_0_ = f32[8,2,512,2048]{3,2,1,0:T(8,128)} custom-call(s32[1]{0:T(128)} %bitcast.2.place_ref, bf16[512,1024]{1,0:T(8,128)(2,1)S(1)} %get-tuple-element.21.left_ref, bf16[512,512]{1,0:T(8,128)(2,1)S(1)} %collective-permute-done.2.right_ref, f32[8,2,512,2048]{3,2,1,0:T(8,128)} %correlate.4.refs_0_), custom_call_target="tpu_custom_call", output_to_operand_aliasing={{}: (3, {})} | custom-call | flops 1073741824 | bytes 16777216 | tf_op jit(solution)/shard_map/correlate/pallas_call | solution.py:320
  69.9 0.4 collective-permute-done.1.right_ref
  70.3 0.0 collective-permute-start.3
  70.3 6.2 %correlate.6.refs_0_ = f32[8,2,512,2048]{3,2,1,0:T(8,128)} custom-call(s32[1]{0:T(128)} %bitcast.4.place_ref, bf16[512,1024]{1,0:T(8,128)(2,1)S(1)} %get-tuple-element.21.left_ref, bf16[512,512]{1,0:T(8,128)(2,1)S(1)} %collective-permute-done.1.right_ref, f32[8,2,512,2048]{3,2,1,0:T(8,128)} %correlate.5.refs_0_), custom_call_target="tpu_custom_call", output_to_operand_aliasing={{}: (3, {})} | custom-call | flops 1073741824 | bytes 16777216 | tf_op jit(solution)/shard_map/correlate/pallas_call | solution.py:320
  76.5 0.0 collective-permute-done.3.right_ref
  76.5 6.2 %correlate.7 = f32[8,2,512,2048]{3,2,1,0:T(8,128)} custom-call(s32[1]{0:T(128)} %bitcast.place_ref, bf16[512,1024]{1,0:T(8,128)(2,1)S(1)} %get-tuple-element.21.left_ref, bf16[512,512]{1,0:T(8,128)(2,1)S(1)} %collective-permute-done.3.right_ref, f32[8,2,512,2048]{3,2,1,0:T(8,128)} %correlate.6.refs_0_), custom_call_target="tpu_custom_call", output_to_operand_aliasing={{}: (3, {})} | custom-call | flops 1073741824 | bytes 16777216 | tf_op jit(solution)/shard_map/correlate/pallas_call | solution.py:320
Async XLA Ops:
  0.0 35.7 %copy-start = (f32[2,512,64]{1,2,0:T(8,128)S(1)}, f32[2,512,64]{1,2,0:T(8,128)}, u32[]{:S(2)}) copy-start(f32[2,512,64]{1,2,0:T(8,128)} %param.5) | copy-start | bytes 786436
  19.5 16.2 %collective-permute-start = (bf16[384,512]{1,0:T(8,128)(2,1)S(1)}, bf16[384,512]{1,0:T(8,128)(2,1)S(1)}, u32[]{:S(2)}, u32[]{:S(2)}) collective-permute-start(bf16[384,512]{1,0:T(8,128)(2,1)S(1)} %get-tuple-element.16), channel_id=1, source_target_pairs={{0,4},{4,8},{8,12},{12,16},{16,20},{20,24},{24,28},{1,5},{5,9},{9,... | collective-permute-start | bytes 1179656 | tf_op jit(solution)/shard_map/ppermute | solution.py:385
  55.9 7.8 %collective-permute-start.2 = (bf16[512,512]{1,0:T(8,128)(2,1)S(1)}, bf16[512,512]{1,0:T(8,128)(2,1)S(1)}, u32[]{:S(2)}, u32[]{:S(2)}) collective-permute-start(bf16[512,512]{1,0:T(8,128)(2,1)S(1)} %get-tuple-element.22.right_ref), channel_id=1, source_target_pairs={{0,2},{2,0},{1,3},{3,1},{4,6},{6,4},{5,7},{7,5},{8,10},{10,8},{9,1... | collective-permute-start | bytes 1572872 | tf_op jit(solution)/shard_map/ppermute | solution.py:370
  56.0 14.3 %collective-permute-start.1 = (bf16[512,512]{1,0:T(8,128)(2,1)S(1)}, bf16[512,512]{1,0:T(8,128)(2,1)S(1)}, u32[]{:S(2)}, u32[]{:S(2)}) collective-permute-start(bf16[512,512]{1,0:T(8,128)(2,1)S(1)} %get-tuple-element.22.right_ref), channel_id=1, source_target_pairs={{0,1},{1,0},{2,3},{3,2},{4,5},{5,4},{6,7},{7,6},{8,9},{9,8},{10,11... | collective-permute-start | bytes 1572872 | tf_op jit(solution)/shard_map/ppermute | solution.py:370
  70.3 6.2 %collective-permute-start.3 = (bf16[512,512]{1,0:T(8,128)(2,1)S(1)}, bf16[512,512]{1,0:T(8,128)(2,1)S(1)}, u32[]{:S(2)}, u32[]{:S(2)}) collective-permute-start(bf16[512,512]{1,0:T(8,128)(2,1)S(1)} %collective-permute-done.1.right_ref), channel_id=1, source_target_pairs={{0,2},{2,0},{1,3},{3,1},{4,6},{6,4},{5,7},{7,5},{8,10},{10,8},{9,1... | collective-permute-start | bytes 1572872 | tf_op jit(solution)/shard_map/ppermute | solution.py:370

commit v12 on v10

--- a/solution.py
+++ b/solution.py
@@ -55,15 +55,14 @@
     width = table.shape[0] // len(order)
     half = width // 2
     count = sums.shape[1] // width - (TAPS - 1)
-    steps = 2 * count
     pieces = first_here.shape[0]
     depth = NFFT // pieces
 
-    def block(step):
-        slot = lax.rem(step, 2)
-        samples = pl.ds(pl.multiple_of((lax.div(step, 2) + frame) * NFFT, NFFT), NFFT)
+    def block(at, part):
+        slot = 2 * lax.rem(at, 2) + part
+        samples = pl.ds(pl.multiple_of((at + frame) * NFFT, NFFT), NFFT)
         return pltpu.make_async_copy(
-            volt_hbm.at[slot, :, samples], volts.at[slot], volt_here.at[slot]
+            volt_hbm.at[part, :, samples], volts.at[slot], volt_here.at[slot]
         )
 
     def fetch(piece):
@@ -82,12 +81,11 @@
             left, right, (((1,), (1,)), ((), ())), preferred_element_type=jnp.float32
         )
 
-    def add(step, start, size):
-        part = lax.rem(step, 2)
-        first = pl.multiple_of(lax.div(step, 2) * width, width)
+    def add(at, part, start, size):
+        first = pl.multiple_of(at * width, width)
         here = pl.ds(first, len(order) * width)
         low = pl.ds(first, len(low_order) * width)
-        values = volts[part, :, start : start + size]
+        values = volts[2 * lax.rem(at, 2) + part, :, start : start + size]
         sums[part, here, :] += product(table[:, start : start + size], values)
         low_sums[part, low, :] += product(
             low_table[:, start : start + size], values.astype(jnp.float8_e4m3fn)
@@ -96,23 +94,31 @@
     for piece in range(pieces):
         for copy in fetch(piece):
             copy.start()
-    block(1).start()
+    block(0, 1).start()
     sums[...] = jnp.zeros_like(sums)
     low_sums[...] = jnp.zeros_like(low_sums)
     for piece in range(pieces):
         for copy in fetch(piece):
             copy.wait()
-        add(0, piece * depth, depth)
-
-    @pl.loop(1, steps)
-    def _(step):
-        block(step).wait()
-
-        @pl.when(step + 1 < steps)
+        add(0, 0, piece * depth, depth)
+    if count > 1:
+        for part in range(2):
+            block(1, part).start()
+    block(0, 1).wait()
+    add(0, 1, 0, NFFT)
+
+    @pl.loop(1, count)
+    def _(at):
+        for part in range(2):
+            block(at, part).wait()
+
+        @pl.when(at + 1 < count)
         def _():
-            block(step + 1).start()
-
-        add(step, 0, NFFT)
+            for part in range(2):
+                block(at + 1, part).start()
+
+        for part in range(2):
+            add(at, part, 0, NFFT)
 
     kept = out_refs[0].shape[0] // width
     for slot in range(sums.shape[1] // width):
@@ -148,10 +154,10 @@
         scratch_shapes=[
             pltpu.VMEM((2, slots * width, rows), jnp.float32),
             pltpu.VMEM((2, low_slots * width, rows), jnp.float32),
-            pltpu.VMEM((2, rows, NFFT), jnp.bfloat16),
+            pltpu.VMEM((4, rows, NFFT), jnp.bfloat16),
             pltpu.VMEM(table.shape, jnp.bfloat16),
             pltpu.VMEM(low_table.shape, jnp.float8_e4m3fn),
-            pltpu.SemaphoreType.DMA((2,)),
+            pltpu.SemaphoreType.DMA((4,)),
             pltpu.SemaphoreType.DMA((pieces,)),
             pltpu.SemaphoreType.DMA((pieces,)),
             pltpu.SemaphoreType.DMA((pieces,)),
@@ -166,7 +172,7 @@
     )(voltages, jnp.asarray(table), jnp.asarray(low_table))
 
 
-def combine_kernel(early_ref, late_ref, odd_ref, even_ref, gain_ref, out_ref):
+def combine_kernel(early_ref, late_ref, handed_ref, gain_ref, out_ref):
     half = gain_ref.shape[1]
     width = 2 * half
     owners = out_ref.shape[0]
@@ -176,8 +182,7 @@
         if slot:
             raw = raw + late_ref[(slot - 1) * width : slot * width, :]
         if slot < TAPS - 1:
-            for handed_ref in (odd_ref, even_ref):
-                raw = raw + handed_ref[slot * width : (slot + 1) * width, :].astype(jnp.float32)
+            raw = raw + handed_ref[slot * width : (slot + 1) * width, :].astype(jnp.float32)
         real, imag = raw[:half], raw[half:]
         out_real = gain_ref[0] * real - gain_ref[1] * imag
         out_imag = gain_ref[0] * imag + gain_ref[1] * real
@@ -188,16 +193,16 @@
             out_ref[owner, at : at + 2 * share, :] = pair.astype(jnp.bfloat16)
 
 
-def combine(early, late, to_odd, to_even, gains, frames, owners):
+def combine(early, late, handed, gains, frames, owners):
     _, half, rows = gains.shape
     return pl.pallas_call(
         combine_kernel,
-        in_specs=[pl.BlockSpec(memory_space=pltpu.VMEM)] * 5,
+        in_specs=[pl.BlockSpec(memory_space=pltpu.VMEM)] * 4,
         out_specs=pl.BlockSpec(memory_space=pltpu.VMEM),
         out_shape=jax.ShapeDtypeStruct((owners, frames * 2 * half // owners, rows), jnp.bfloat16),
         compiler_params=pltpu.CompilerParams(vmem_limit_bytes=16 * 2**20),
         name="combine",
-    )(early, late, to_odd, to_even, gains)
+    )(early, late, handed, gains)
 
 
 def merge_kernel(frames, share, norm, in_ref, out_ref, left_ref, scratch):
@@ -357,13 +362,10 @@
     tables = filter_table(channels)
     late, ending = filter_part(voltages, tables, 1, frames_here - 1, frames_here - 1)
     voltages, ending = lax.optimization_barrier((voltages, ending))
-    handed = [
-        lax.ppermute(ending, "fgrp", [(i, i + 1) for i in range(first, owners - 1, 2)])
-        for first in range(2)
-    ]
+    handed = lax.ppermute(ending, "fgrp", [(i, i + 1) for i in range(owners - 1)])
     (early,) = filter_part(voltages, tables, 0, 1, TAPS)
     handed, early = lax.optimization_barrier((handed, early))
-    partial = combine(early, late, *handed, jnp.swapaxes(gains, 1, 2), frames_here, owners)
+    partial = combine(early, late, handed, jnp.swapaxes(gains, 1, 2), frames_here, owners)
     turned = lax.all_to_all(partial, "fgrp", split_axis=0, concat_axis=0, tiled=True)
     own, left = merge(turned, frames_here, share, norm)
     tiles, pols = lax.axis_size("tile"), lax.axis_size("pol")

time: 83.9 us -> 81.7 us (0.974)
  starting transfers between devices: 10 us -> 6.7 us
  blocking collectives: 18.8 us -> 20.2 us
    ppermute x2 -> x1, starting transfers between devices: 8.35 us -> 5.05 us  [body(): lax.ppermute(ending, 'fgrp', [(i, i + 1) for i in range(owners - 1)])]
    all_to_all x1, blocking collectives: 18.8 us -> 20.2 us  [body(): lax.all_to_all(partial, 'fgrp', split_axis=0, concat_axis=0, tiled=True)]
  transfers between devices with their start and end apart: 5 -> 4, of which waited for: 1 -> 2; matrix products, arithmetic and copies ran while one was open for 0% -> 0% of each run, Pallas kernels for 32% -> 33%
where the time goes in v12:
time: 81.7 us; the launch traced here: 81.4 us
  Pallas kernels  53.8 us (66%)
  blocking collectives  20.2 us (25%)
  starting transfers between devices  6.7 us (8%)
    pallas_call x2, Pallas kernels, filter_part(): pl.pallas_call(functools.partial(filter_kernel, frame, low_scale), in_spe...  27.8 us
    pallas_call x4, Pallas kernels, correlate(): pl.pallas_call(functools.partial(block_kernel, share), in_specs=specs, ou...  24.7 us
    all_to_all x1, blocking collectives, body(): lax.all_to_all(partial, 'fgrp', split_axis=0, concat_axis=0, tiled=True)  20.2 us
    ppermute x1, starting transfers between devices, body(): lax.ppermute(ending, 'fgrp', [(i, i + 1) for i in range(owners - 1)])  5.05 us
    ppermute x3, starting transfers between devices, swapped(): lax.ppermute(shard, axis, [(i, peer(i, step, length, 1)) for i in range(l...  1.65 us
  transfers between devices with their start and end apart: 4, of which 2 were waited for; matrix products, arithmetic and copies ran while one was open for 0% of the time, Pallas kernels for 33%

profile of v12, /device:TPU:0, one launch (start us, length us, event | category | flops | bytes accessed | tf_op | source)
XLA Modules:
  0.0 81.4 jit_solution(16154433376099702853)
XLA Ops:
  0.0 0.0 copy-start
  0.0 19.7 %filter_part.2 = (f32[384,512]{1,0:T(8,128)S(1)}, bf16[384,512]{1,0:T(8,128)(2,1)S(1)}) custom-call(bf16[2,512,16384]{2,1,0:T(8,128)(2,1)} %volt_hbm.2, bf16[512,4096]{1,0:T(8,128)(2,1)} %constant.14.clone.table_hbm, f8e4m3fn[256,4096]{1,0:T(32,128)(4,1)} %constant.15.clone.low_hbm), custom_call_target="tpu_custom_call" | custom-call | flops 19327352832 | bytes 29360128 | tf_op jit(solution)/shard_map/filter_part/pallas_call | solution.py:149
  19.7 5.1 %collective-permute-start = (bf16[384,512]{1,0:T(8,128)(2,1)S(1)}, bf16[384,512]{1,0:T(8,128)(2,1)S(1)}, u32[]{:S(2)}, u32[]{:S(2)}) collective-permute-start(bf16[384,512]{1,0:T(8,128)(2,1)S(1)} %get-tuple-element.16), channel_id=1, source_target_pairs={{0,4},{4,8},{8,12},{12,16},{16,20},{20,24},{24,28},{1,5},{5,9},{9,... | collective-permute-start | bytes 1179656 | tf_op jit(solution)/shard_map/ppermute | solution.py:365
  24.8 8.1 %filter_part.3.early_ref = f32[512,512]{1,0:T(8,128)S(1)} custom-call(bf16[2,512,16384]{2,1,0:T(8,128)(2,1)} %volt_hbm.2, bf16[512,4096]{1,0:T(8,128)(2,1)} %constant.14.clone.table_hbm, f8e4m3fn[256,4096]{1,0:T(32,128)(4,1)} %constant.15.clone.low_hbm), custom_call_target="tpu_custom_call" | custom-call | flops 6442450944 | bytes 12582912 | tf_op jit(solution)/shard_map/filter_part/pallas_call | solution.py:149
  32.9 0.1 collective-permute-done.handed_ref
  32.9 0.0 copy-done
  32.9 0.2 combine.1
  33.1 20.2 %all_to_all.5.in_ref = bf16[8,64,512]{2,1,0:T(8,128)(2,1)S(1)} all-to-all(bf16[8,64,512]{2,1,0:T(8,128)(2,1)S(1)} %combine.1), channel_id=1, replica_groups=mesh['fgrp'=8,'tile'=2,'pol'=2] {'fgrp'}, dimensions={0} | all-to-all | bytes 1048576 | tf_op jit(solution)/shard_map/all_to_all | solution.py:369
  53.4 1.1 %merge.1 = (bf16[512,512]{1,0:T(8,128)(2,1)S(1)}, bf16[512,1024]{1,0:T(8,128)(2,1)S(1)}) custom-call(bf16[8,64,512]{2,1,0:T(8,128)(2,1)S(1)} %all_to_all.5.in_ref), custom_call_target="tpu_custom_call" | custom-call | tf_op jit(solution)/shard_map/merge/pallas_call | solution.py:242
  54.5 0.1 collective-permute-start.2
  54.6 1.6 %collective-permute-start.1 = (bf16[512,512]{1,0:T(8,128)(2,1)S(1)}, bf16[512,512]{1,0:T(8,128)(2,1)S(1)}, u32[]{:S(2)}, u32[]{:S(2)}) collective-permute-start(bf16[512,512]{1,0:T(8,128)(2,1)S(1)} %get-tuple-element.22.right_ref), channel_id=1, source_target_pairs={{0,1},{1,0},{2,3},{3,2},{4,5},{5,4},{6,7},{7,6},{8,9},{9,8},{10,11... | collective-permute-start | bytes 1572872 | tf_op jit(solution)/shard_map/ppermute | solution.py:352
  56.1 6.2 %correlate.4.refs_0_ = f32[8,2,512,2048]{3,2,1,0:T(8,128)} custom-call(s32[1]{0:T(128)} %bitcast.3.place_ref, bf16[512,1024]{1,0:T(8,128)(2,1)S(1)} %get-tuple-element.21.left_ref, bf16[512,512]{1,0:T(8,128)(2,1)S(1)} %get-tuple-element.22.right_ref), custom_call_target="tpu_custom_call" | custom-call | flops 1073741824 | bytes 16777216 | tf_op jit(solution)/shard_map/correlate/pallas_call | solution.py:302
  62.3 0.0 collective-permute-done.2.right_ref
  62.3 6.2 %correlate.5.refs_0_ = f32[8,2,512,2048]{3,2,1,0:T(8,128)} custom-call(s32[1]{0:T(128)} %bitcast.2.place_ref, bf16[512,1024]{1,0:T(8,128)(2,1)S(1)} %get-tuple-element.21.left_ref, bf16[512,512]{1,0:T(8,128)(2,1)S(1)} %collective-permute-done.2.right_ref, f32[8,2,512,2048]{3,2,1,0:T(8,128)} %correlate.4.refs_0_), custom_call_target="tpu_custom_call", output_to_operand_aliasing={{}: (3, {})} | custom-call | flops 1073741824 | bytes 16777216 | tf_op jit(solution)/shard_map/correlate/pallas_call | solution.py:302
  68.5 0.4 collective-permute-done.1.right_ref
  68.9 0.0 collective-permute-start.3
  68.9 6.2 %correlate.6.refs_0_ = f32[8,2,512,2048]{3,2,1,0:T(8,128)} custom-call(s32[1]{0:T(128)} %bitcast.4.place_ref, bf16[512,1024]{1,0:T(8,128)(2,1)S(1)} %get-tuple-element.21.left_ref, bf16[512,512]{1,0:T(8,128)(2,1)S(1)} %collective-permute-done.1.right_ref, f32[8,2,512,2048]{3,2,1,0:T(8,128)} %correlate.5.refs_0_), custom_call_target="tpu_custom_call", output_to_operand_aliasing={{}: (3, {})} | custom-call | flops 1073741824 | bytes 16777216 | tf_op jit(solution)/shard_map/correlate/pallas_call | solution.py:302
  75.1 0.0 collective-permute-done.3.right_ref
  75.1 6.2 %correlate.7 = f32[8,2,512,2048]{3,2,1,0:T(8,128)} custom-call(s32[1]{0:T(128)} %bitcast.place_ref, bf16[512,1024]{1,0:T(8,128)(2,1)S(1)} %get-tuple-element.21.left_ref, bf16[512,512]{1,0:T(8,128)(2,1)S(1)} %collective-permute-done.3.right_ref, f32[8,2,512,2048]{3,2,1,0:T(8,128)} %correlate.6.refs_0_), custom_call_target="tpu_custom_call", output_to_operand_aliasing={{}: (3, {})} | custom-call | flops 1073741824 | bytes 16777216 | tf_op jit(solution)/shard_map/correlate/pallas_call | solution.py:302
Async XLA Ops:
  0.0 32.9 %copy-start = (f32[2,512,64]{1,2,0:T(8,128)S(1)}, f32[2,512,64]{1,2,0:T(8,128)}, u32[]{:S(2)}) copy-start(f32[2,512,64]{1,2,0:T(8,128)} %param.5) | copy-start | bytes 786436
  19.7 13.2 %collective-permute-start = (bf16[384,512]{1,0:T(8,128)(2,1)S(1)}, bf16[384,512]{1,0:T(8,128)(2,1)S(1)}, u32[]{:S(2)}, u32[]{:S(2)}) collective-permute-start(bf16[384,512]{1,0:T(8,128)(2,1)S(1)} %get-tuple-element.16), channel_id=1, source_target_pairs={{0,4},{4,8},{8,12},{12,16},{16,20},{20,24},{24,28},{1,5},{5,9},{9,... | collective-permute-start | bytes 1179656 | tf_op jit(solution)/shard_map/ppermute | solution.py:365
  54.5 7.8 %collective-permute-start.2 = (bf16[512,512]{1,0:T(8,128)(2,1)S(1)}, bf16[512,512]{1,0:T(8,128)(2,1)S(1)}, u32[]{:S(2)}, u32[]{:S(2)}) collective-permute-start(bf16[512,512]{1,0:T(8,128)(2,1)S(1)} %get-tuple-element.22.right_ref), channel_id=1, source_target_pairs={{0,2},{2,0},{1,3},{3,1},{4,6},{6,4},{5,7},{7,5},{8,10},{10,8},{9,1... | collective-permute-start | bytes 1572872 | tf_op jit(solution)/shard_map/ppermute | solution.py:352
  54.6 14.3 %collective-permute-start.1 = (bf16[512,512]{1,0:T(8,128)(2,1)S(1)}, bf16[512,512]{1,0:T(8,128)(2,1)S(1)}, u32[]{:S(2)}, u32[]{:S(2)}) collective-permute-start(bf16[512,512]{1,0:T(8,128)(2,1)S(1)} %get-tuple-element.22.right_ref), channel_id=1, source_target_pairs={{0,1},{1,0},{2,3},{3,2},{4,5},{5,4},{6,7},{7,6},{8,9},{9,8},{10,11... | collective-permute-start | bytes 1572872 | tf_op jit(solution)/shard_map/ppermute | solution.py:352
  68.9 6.2 %collective-permute-start.3 = (bf16[512,512]{1,0:T(8,128)(2,1)S(1)}, bf16[512,512]{1,0:T(8,128)(2,1)S(1)}, u32[]{:S(2)}, u32[]{:S(2)}) collective-permute-start(bf16[512,512]{1,0:T(8,128)(2,1)S(1)} %collective-permute-done.1.right_ref), channel_id=1, source_target_pairs={{0,2},{2,0},{1,3},{3,1},{4,6},{6,4},{5,7},{7,5},{8,10},{10,8},{9,1... | collective-permute-start | bytes 1572872 | tf_op jit(solution)/shard_map/ppermute | solution.py:352

commit v13 on v12

--- a/solution.py
+++ b/solution.py
@@ -76,6 +76,13 @@
             pltpu.make_async_copy(low_hbm.at[:, part], low_table.at[:, part], low_here.at[piece]),
         ]
 
+    def half_block(at):
+        part = pl.ds(at * NFFT // 2, NFFT // 2)
+        samples = pl.ds(frame * NFFT + at * NFFT // 2, NFFT // 2)
+        return pltpu.make_async_copy(
+            volt_hbm.at[1, :, samples], volts.at[1, :, part], volt_here.at[at]
+        )
+
     def product(left, right):
         return lax.dot_general(
             left, right, (((1,), (1,)), ((), ())), preferred_element_type=jnp.float32
@@ -94,7 +101,9 @@
     for piece in range(pieces):
         for copy in fetch(piece):
             copy.start()
-    block(0, 1).start()
+    halves = [half_block(0), half_block(1)]
+    for copy in halves:
+        copy.start()
     sums[...] = jnp.zeros_like(sums)
     low_sums[...] = jnp.zeros_like(low_sums)
     for piece in range(pieces):
@@ -104,8 +113,9 @@
     if count > 1:
         for part in range(2):
             block(1, part).start()
-    block(0, 1).wait()
-    add(0, 1, 0, NFFT)
+    for at, copy in enumerate(halves):
+        copy.wait()
+        add(0, 1, at * NFFT // 2, NFFT // 2)
 
     @pl.loop(1, count)
     def _(at):
@@ -379,8 +389,9 @@
 
     total = tiles * pols * inputs_here
     result = None
+    far = [swapped(own, "pol", by_pol) for by_pol in range(pols)]
     for by_pol in range(pols):
-        near = swapped(own, "pol", by_pol)
+        near = far[by_pol]
         if by_pol:
             near, result = lax.optimization_barrier((near, result))
         for by_tile in range(tiles):

time: 81.7 us -> 81.9 us (level)
  transfers between devices with their start and end apart: 4 -> 4, of which waited for: 2 -> 1; matrix products, arithmetic and copies ran while one was open for 0% -> 0% of each run, Pallas kernels for 33% -> 33%
where the time goes in v13:
time: 81.9 us; the launch traced here: 81.7 us
  Pallas kernels  54.4 us (66%)
  blocking collectives  20 us (24%)
  starting transfers between devices  6.72 us (8%)
    pallas_call x2, Pallas kernels, filter_part(): pl.pallas_call(functools.partial(filter_kernel, frame, low_scale), in_spe...  28.4 us
    pallas_call x4, Pallas kernels, correlate(): pl.pallas_call(functools.partial(block_kernel, share), in_specs=specs, ou...  24.7 us
    all_to_all x1, blocking collectives, body(): lax.all_to_all(partial, 'fgrp', split_axis=0, concat_axis=0, tiled=True)  20 us
    ppermute x1, starting transfers between devices, body(): lax.ppermute(ending, 'fgrp', [(i, i + 1) for i in range(owners - 1)])  5.05 us
    ppermute x3, starting transfers between devices, swapped(): lax.ppermute(shard, axis, [(i, peer(i, step, length, 1)) for i in range(l...  1.68 us
  transfers between devices with their start and end apart: 4, of which 1 were waited for; matrix products, arithmetic and copies ran while one was open for 0% of the time, Pallas kernels for 33%

profile of v13, /device:TPU:0, one launch (start us, length us, event | category | flops | bytes accessed | tf_op | source)
XLA Modules:
  0.0 81.7 jit_solution(5893606033175386820)
XLA Ops:
  0.0 0.0 copy-start
  0.0 20.0 %filter_part.2 = (f32[384,512]{1,0:T(8,128)S(1)}, bf16[384,512]{1,0:T(8,128)(2,1)S(1)}) custom-call(bf16[2,512,16384]{2,1,0:T(8,128)(2,1)} %volt_hbm.2, bf16[512,4096]{1,0:T(8,128)(2,1)} %constant.14.clone.table_hbm, f8e4m3fn[256,4096]{1,0:T(32,128)(4,1)} %constant.15.clone.low_hbm), custom_call_target="tpu_custom_call" | custom-call | flops 19327352832 | bytes 29360128 | tf_op jit(solution)/shard_map/filter_part/pallas_call | solution.py:159
  20.0 5.0 %collective-permute-start = (bf16[384,512]{1,0:T(8,128)(2,1)S(1)}, bf16[384,512]{1,0:T(8,128)(2,1)S(1)}, u32[]{:S(2)}, u32[]{:S(2)}) collective-permute-start(bf16[384,512]{1,0:T(8,128)(2,1)S(1)} %get-tuple-element.16), channel_id=1, source_target_pairs={{0,4},{4,8},{8,12},{12,16},{16,20},{20,24},{24,28},{1,5},{5,9},{9,... | collective-permute-start | bytes 1179656 | tf_op jit(solution)/shard_map/ppermute | solution.py:375
  25.1 8.3 %filter_part.3.early_ref = f32[512,512]{1,0:T(8,128)S(1)} custom-call(bf16[2,512,16384]{2,1,0:T(8,128)(2,1)} %volt_hbm.2, bf16[512,4096]{1,0:T(8,128)(2,1)} %constant.14.clone.table_hbm, f8e4m3fn[256,4096]{1,0:T(32,128)(4,1)} %constant.15.clone.low_hbm), custom_call_target="tpu_custom_call" | custom-call | flops 6442450944 | bytes 12582912 | tf_op jit(solution)/shard_map/filter_part/pallas_call | solution.py:159
  33.4 0.0 collective-permute-done.handed_ref
  33.4 0.0 copy-done
  33.4 0.2 combine.1
  33.7 20.0 %all_to_all.5.in_ref = bf16[8,64,512]{2,1,0:T(8,128)(2,1)S(1)} all-to-all(bf16[8,64,512]{2,1,0:T(8,128)(2,1)S(1)} %combine.1), channel_id=1, replica_groups=mesh['fgrp'=8,'tile'=2,'pol'=2] {'fgrp'}, dimensions={0} | all-to-all | bytes 1048576 | tf_op jit(solution)/shard_map/all_to_all | solution.py:379
  53.6 1.1 %merge.1 = (bf16[512,512]{1,0:T(8,128)(2,1)S(1)}, bf16[512,1024]{1,0:T(8,128)(2,1)S(1)}) custom-call(bf16[8,64,512]{2,1,0:T(8,128)(2,1)S(1)} %all_to_all.5.in_ref), custom_call_target="tpu_custom_call" | custom-call | tf_op jit(solution)/shard_map/merge/pallas_call | solution.py:252
  54.8 0.1 collective-permute-start.2
  54.8 1.6 %collective-permute-start.1 = (bf16[512,512]{1,0:T(8,128)(2,1)S(1)}, bf16[512,512]{1,0:T(8,128)(2,1)S(1)}, u32[]{:S(2)}, u32[]{:S(2)}) collective-permute-start(bf16[512,512]{1,0:T(8,128)(2,1)S(1)} %get-tuple-element.22.right_ref), channel_id=1, source_target_pairs={{0,1},{1,0},{2,3},{3,2},{4,5},{5,4},{6,7},{7,6},{8,9},{9,8},{10,11... | collective-permute-start | bytes 1572872 | tf_op jit(solution)/shard_map/ppermute | solution.py:362
  56.4 6.2 %correlate.4.refs_0_ = f32[8,2,512,2048]{3,2,1,0:T(8,128)} custom-call(s32[1]{0:T(128)} %bitcast.3.place_ref, bf16[512,1024]{1,0:T(8,128)(2,1)S(1)} %get-tuple-element.21.left_ref, bf16[512,512]{1,0:T(8,128)(2,1)S(1)} %get-tuple-element.22.right_ref), custom_call_target="tpu_custom_call" | custom-call | flops 1073741824 | bytes 16777216 | tf_op jit(solution)/shard_map/correlate/pallas_call | solution.py:312
  62.6 0.0 collective-permute-done.2.right_ref
  62.6 6.2 %correlate.5.refs_0_ = f32[8,2,512,2048]{3,2,1,0:T(8,128)} custom-call(s32[1]{0:T(128)} %bitcast.2.place_ref, bf16[512,1024]{1,0:T(8,128)(2,1)S(1)} %get-tuple-element.21.left_ref, bf16[512,512]{1,0:T(8,128)(2,1)S(1)} %collective-permute-done.2.right_ref, f32[8,2,512,2048]{3,2,1,0:T(8,128)} %correlate.4.refs_0_), custom_call_target="tpu_custom_call", output_to_operand_aliasing={{}: (3, {})} | custom-call | flops 1073741824 | bytes 16777216 | tf_op jit(solution)/shard_map/correlate/pallas_call | solution.py:312
  68.8 0.4 collective-permute-done.1.right_ref
  69.2 0.0 collective-permute-start.3
  69.2 6.2 %correlate.6.refs_0_ = f32[8,2,512,2048]{3,2,1,0:T(8,128)} custom-call(s32[1]{0:T(128)} %bitcast.4.place_ref, bf16[512,1024]{1,0:T(8,128)(2,1)S(1)} %get-tuple-element.21.left_ref, bf16[512,512]{1,0:T(8,128)(2,1)S(1)} %collective-permute-done.1.right_ref, f32[8,2,512,2048]{3,2,1,0:T(8,128)} %correlate.5.refs_0_), custom_call_target="tpu_custom_call", output_to_operand_aliasing={{}: (3, {})} | custom-call | flops 1073741824 | bytes 16777216 | tf_op jit(solution)/shard_map/correlate/pallas_call | solution.py:312
  75.4 0.0 collective-permute-done.3.right_ref
  75.4 6.2 %correlate.7 = f32[8,2,512,2048]{3,2,1,0:T(8,128)} custom-call(s32[1]{0:T(128)} %bitcast.place_ref, bf16[512,1024]{1,0:T(8,128)(2,1)S(1)} %get-tuple-element.21.left_ref, bf16[512,512]{1,0:T(8,128)(2,1)S(1)} %collective-permute-done.3.right_ref, f32[8,2,512,2048]{3,2,1,0:T(8,128)} %correlate.6.refs_0_), custom_call_target="tpu_custom_call", output_to_operand_aliasing={{}: (3, {})} | custom-call | flops 1073741824 | bytes 16777216 | tf_op jit(solution)/shard_map/correlate/pallas_call | solution.py:312
Async XLA Ops:
  0.0 33.4 %copy-start = (f32[2,512,64]{1,2,0:T(8,128)S(1)}, f32[2,512,64]{1,2,0:T(8,128)}, u32[]{:S(2)}) copy-start(f32[2,512,64]{1,2,0:T(8,128)} %param.5) | copy-start | bytes 786436
  20.0 13.4 %collective-permute-start = (bf16[384,512]{1,0:T(8,128)(2,1)S(1)}, bf16[384,512]{1,0:T(8,128)(2,1)S(1)}, u32[]{:S(2)}, u32[]{:S(2)}) collective-permute-start(bf16[384,512]{1,0:T(8,128)(2,1)S(1)} %get-tuple-element.16), channel_id=1, source_target_pairs={{0,4},{4,8},{8,12},{12,16},{16,20},{20,24},{24,28},{1,5},{5,9},{9,... | collective-permute-start | bytes 1179656 | tf_op jit(solution)/shard_map/ppermute | solution.py:375
  54.8 7.9 %collective-permute-start.2 = (bf16[512,512]{1,0:T(8,128)(2,1)S(1)}, bf16[512,512]{1,0:T(8,128)(2,1)S(1)}, u32[]{:S(2)}, u32[]{:S(2)}) collective-permute-start(bf16[512,512]{1,0:T(8,128)(2,1)S(1)} %get-tuple-element.22.right_ref), channel_id=1, source_target_pairs={{0,2},{2,0},{1,3},{3,1},{4,6},{6,4},{5,7},{7,5},{8,10},{10,8},{9,1... | collective-permute-start | bytes 1572872 | tf_op jit(solution)/shard_map/ppermute | solution.py:362
  54.8 14.3 %collective-permute-start.1 = (bf16[512,512]{1,0:T(8,128)(2,1)S(1)}, bf16[512,512]{1,0:T(8,128)(2,1)S(1)}, u32[]{:S(2)}, u32[]{:S(2)}) collective-permute-start(bf16[512,512]{1,0:T(8,128)(2,1)S(1)} %get-tuple-element.22.right_ref), channel_id=1, source_target_pairs={{0,1},{1,0},{2,3},{3,2},{4,5},{5,4},{6,7},{7,6},{8,9},{9,8},{10,11... | collective-permute-start | bytes 1572872 | tf_op jit(solution)/shard_map/ppermute | solution.py:362
  69.2 6.2 %collective-permute-start.3 = (bf16[512,512]{1,0:T(8,128)(2,1)S(1)}, bf16[512,512]{1,0:T(8,128)(2,1)S(1)}, u32[]{:S(2)}, u32[]{:S(2)}) collective-permute-start(bf16[512,512]{1,0:T(8,128)(2,1)S(1)} %collective-permute-done.1.right_ref), channel_id=1, source_target_pairs={{0,2},{2,0},{1,3},{3,1},{4,6},{6,4},{5,7},{7,5},{8,10},{10,8},{9,1... | collective-permute-start | bytes 1572872 | tf_op jit(solution)/shard_map/ppermute | solution.py:362

commit v14 on v12

--- a/solution.py
+++ b/solution.py
@@ -81,15 +81,17 @@
             left, right, (((1,), (1,)), ((), ())), preferred_element_type=jnp.float32
         )
 
-    def add(at, part, start, size):
+    def add(at, part, start, size, kinds=(0, 1)):
         first = pl.multiple_of(at * width, width)
         here = pl.ds(first, len(order) * width)
         low = pl.ds(first, len(low_order) * width)
         values = volts[2 * lax.rem(at, 2) + part, :, start : start + size]
-        sums[part, here, :] += product(table[:, start : start + size], values)
-        low_sums[part, low, :] += product(
-            low_table[:, start : start + size], values.astype(jnp.float8_e4m3fn)
-        )
+        if 0 in kinds:
+            sums[part, here, :] += product(table[:, start : start + size], values)
+        if 1 in kinds:
+            low_sums[part, low, :] += product(
+                low_table[:, start : start + size], values.astype(jnp.float8_e4m3fn)
+            )
 
     for piece in range(pieces):
         for copy in fetch(piece):
@@ -117,8 +119,9 @@
             for part in range(2):
                 block(at + 1, part).start()
 
-        for part in range(2):
-            add(at, part, 0, NFFT)
+        for kind in range(2):
+            for part in range(2):
+                add(at, part, 0, NFFT, (kind,))
 
     kept = out_refs[0].shape[0] // width
     for slot in range(sums.shape[1] // width):

time: 81.7 us -> 81.5 us (level)
  no operation moved by 1% of the time
where the time goes in v14:
time: 81.5 us; the launch traced here: 81.3 us
  Pallas kernels  53.7 us (66%)
  blocking collectives  20.2 us (25%)
  starting transfers between devices  6.69 us (8%)
    pallas_call x2, Pallas kernels, filter_part(): pl.pallas_call(functools.partial(filter_kernel, frame, low_scale), in_spe...  27.7 us
    pallas_call x4, Pallas kernels, correlate(): pl.pallas_call(functools.partial(block_kernel, share), in_specs=specs, ou...  24.7 us
    all_to_all x1, blocking collectives, body(): lax.all_to_all(partial, 'fgrp', split_axis=0, concat_axis=0, tiled=True)  20.2 us
    ppermute x1, starting transfers between devices, body(): lax.ppermute(ending, 'fgrp', [(i, i + 1) for i in range(owners - 1)])  5.05 us
    ppermute x3, starting transfers between devices, swapped(): lax.ppermute(shard, axis, [(i, peer(i, step, length, 1)) for i in range(l...  1.65 us
  transfers between devices with their start and end apart: 4, of which 2 were waited for; matrix products, arithmetic and copies ran while one was open for 0% of the time, Pallas kernels for 33%

profile of v14, /device:TPU:0, one launch (start us, length us, event | category | flops | bytes accessed | tf_op | source)
XLA Modules:
  0.0 81.3 jit_solution(13789067415027980923)
XLA Ops:
  0.0 0.0 copy-start
  0.0 19.6 %filter_part.2 = (f32[384,512]{1,0:T(8,128)S(1)}, bf16[384,512]{1,0:T(8,128)(2,1)S(1)}) custom-call(bf16[2,512,16384]{2,1,0:T(8,128)(2,1)} %volt_hbm.2, bf16[512,4096]{1,0:T(8,128)(2,1)} %constant.14.clone.table_hbm, f8e4m3fn[256,4096]{1,0:T(32,128)(4,1)} %constant.15.clone.low_hbm), custom_call_target="tpu_custom_call" | custom-call | flops 19327352832 | bytes 29360128 | tf_op jit(solution)/shard_map/filter_part/pallas_call | solution.py:152
  19.6 5.0 %collective-permute-start = (bf16[384,512]{1,0:T(8,128)(2,1)S(1)}, bf16[384,512]{1,0:T(8,128)(2,1)S(1)}, u32[]{:S(2)}, u32[]{:S(2)}) collective-permute-start(bf16[384,512]{1,0:T(8,128)(2,1)S(1)} %get-tuple-element.16), channel_id=1, source_target_pairs={{0,4},{4,8},{8,12},{12,16},{16,20},{20,24},{24,28},{1,5},{5,9},{9,... | collective-permute-start | bytes 1179656 | tf_op jit(solution)/shard_map/ppermute | solution.py:368
  24.7 8.1 %filter_part.3.early_ref = f32[512,512]{1,0:T(8,128)S(1)} custom-call(bf16[2,512,16384]{2,1,0:T(8,128)(2,1)} %volt_hbm.2, bf16[512,4096]{1,0:T(8,128)(2,1)} %constant.14.clone.table_hbm, f8e4m3fn[256,4096]{1,0:T(32,128)(4,1)} %constant.15.clone.low_hbm), custom_call_target="tpu_custom_call" | custom-call | flops 6442450944 | bytes 12582912 | tf_op jit(solution)/shard_map/filter_part/pallas_call | solution.py:152
  32.7 0.1 collective-permute-done.handed_ref
  32.8 0.0 copy-done
  32.8 0.2 combine.1
  33.0 20.2 %all_to_all.5.in_ref = bf16[8,64,512]{2,1,0:T(8,128)(2,1)S(1)} all-to-all(bf16[8,64,512]{2,1,0:T(8,128)(2,1)S(1)} %combine.1), channel_id=1, replica_groups=mesh['fgrp'=8,'tile'=2,'pol'=2] {'fgrp'}, dimensions={0} | all-to-all | bytes 1048576 | tf_op jit(solution)/shard_map/all_to_all | solution.py:372
  53.2 1.1 %merge.1 = (bf16[512,512]{1,0:T(8,128)(2,1)S(1)}, bf16[512,1024]{1,0:T(8,128)(2,1)S(1)}) custom-call(bf16[8,64,512]{2,1,0:T(8,128)(2,1)S(1)} %all_to_all.5.in_ref), custom_call_target="tpu_custom_call" | custom-call | tf_op jit(solution)/shard_map/merge/pallas_call | solution.py:245
  54.3 0.1 collective-permute-start.2
  54.4 1.6 %collective-permute-start.1 = (bf16[512,512]{1,0:T(8,128)(2,1)S(1)}, bf16[512,512]{1,0:T(8,128)(2,1)S(1)}, u32[]{:S(2)}, u32[]{:S(2)}) collective-permute-start(bf16[512,512]{1,0:T(8,128)(2,1)S(1)} %get-tuple-element.22.right_ref), channel_id=1, source_target_pairs={{0,1},{1,0},{2,3},{3,2},{4,5},{5,4},{6,7},{7,6},{8,9},{9,8},{10,11... | collective-permute-start | bytes 1572872 | tf_op jit(solution)/shard_map/ppermute | solution.py:355
  56.0 6.2 %correlate.4.refs_0_ = f32[8,2,512,2048]{3,2,1,0:T(8,128)} custom-call(s32[1]{0:T(128)} %bitcast.3.place_ref, bf16[512,1024]{1,0:T(8,128)(2,1)S(1)} %get-tuple-element.21.left_ref, bf16[512,512]{1,0:T(8,128)(2,1)S(1)} %get-tuple-element.22.right_ref), custom_call_target="tpu_custom_call" | custom-call | flops 1073741824 | bytes 16777216 | tf_op jit(solution)/shard_map/correlate/pallas_call | solution.py:305
  62.2 0.0 collective-permute-done.2.right_ref
  62.2 6.2 %correlate.5.refs_0_ = f32[8,2,512,2048]{3,2,1,0:T(8,128)} custom-call(s32[1]{0:T(128)} %bitcast.2.place_ref, bf16[512,1024]{1,0:T(8,128)(2,1)S(1)} %get-tuple-element.21.left_ref, bf16[512,512]{1,0:T(8,128)(2,1)S(1)} %collective-permute-done.2.right_ref, f32[8,2,512,2048]{3,2,1,0:T(8,128)} %correlate.4.refs_0_), custom_call_target="tpu_custom_call", output_to_operand_aliasing={{}: (3, {})} | custom-call | flops 1073741824 | bytes 16777216 | tf_op jit(solution)/shard_map/correlate/pallas_call | solution.py:305
  68.4 0.4 collective-permute-done.1.right_ref
  68.8 0.0 collective-permute-start.3
  68.8 6.2 %correlate.6.refs_0_ = f32[8,2,512,2048]{3,2,1,0:T(8,128)} custom-call(s32[1]{0:T(128)} %bitcast.4.place_ref, bf16[512,1024]{1,0:T(8,128)(2,1)S(1)} %get-tuple-element.21.left_ref, bf16[512,512]{1,0:T(8,128)(2,1)S(1)} %collective-permute-done.1.right_ref, f32[8,2,512,2048]{3,2,1,0:T(8,128)} %correlate.5.refs_0_), custom_call_target="tpu_custom_call", output_to_operand_aliasing={{}: (3, {})} | custom-call | flops 1073741824 | bytes 16777216 | tf_op jit(solution)/shard_map/correlate/pallas_call | solution.py:305
  74.9 0.0 collective-permute-done.3.right_ref
  75.0 6.2 %correlate.7 = f32[8,2,512,2048]{3,2,1,0:T(8,128)} custom-call(s32[1]{0:T(128)} %bitcast.place_ref, bf16[512,1024]{1,0:T(8,128)(2,1)S(1)} %get-tuple-element.21.left_ref, bf16[512,512]{1,0:T(8,128)(2,1)S(1)} %collective-permute-done.3.right_ref, f32[8,2,512,2048]{3,2,1,0:T(8,128)} %correlate.6.refs_0_), custom_call_target="tpu_custom_call", output_to_operand_aliasing={{}: (3, {})} | custom-call | flops 1073741824 | bytes 16777216 | tf_op jit(solution)/shard_map/correlate/pallas_call | solution.py:305
Async XLA Ops:
  0.0 32.8 %copy-start = (f32[2,512,64]{1,2,0:T(8,128)S(1)}, f32[2,512,64]{1,2,0:T(8,128)}, u32[]{:S(2)}) copy-start(f32[2,512,64]{1,2,0:T(8,128)} %param.5) | copy-start | bytes 786436
  19.6 13.2 %collective-permute-start = (bf16[384,512]{1,0:T(8,128)(2,1)S(1)}, bf16[384,512]{1,0:T(8,128)(2,1)S(1)}, u32[]{:S(2)}, u32[]{:S(2)}) collective-permute-start(bf16[384,512]{1,0:T(8,128)(2,1)S(1)} %get-tuple-element.16), channel_id=1, source_target_pairs={{0,4},{4,8},{8,12},{12,16},{16,20},{20,24},{24,28},{1,5},{5,9},{9,... | collective-permute-start | bytes 1179656 | tf_op jit(solution)/shard_map/ppermute | solution.py:368
  54.3 7.8 %collective-permute-start.2 = (bf16[512,512]{1,0:T(8,128)(2,1)S(1)}, bf16[512,512]{1,0:T(8,128)(2,1)S(1)}, u32[]{:S(2)}, u32[]{:S(2)}) collective-permute-start(bf16[512,512]{1,0:T(8,128)(2,1)S(1)} %get-tuple-element.22.right_ref), channel_id=1, source_target_pairs={{0,2},{2,0},{1,3},{3,1},{4,6},{6,4},{5,7},{7,5},{8,10},{10,8},{9,1... | collective-permute-start | bytes 1572872 | tf_op jit(solution)/shard_map/ppermute | solution.py:355
  54.4 14.3 %collective-permute-start.1 = (bf16[512,512]{1,0:T(8,128)(2,1)S(1)}, bf16[512,512]{1,0:T(8,128)(2,1)S(1)}, u32[]{:S(2)}, u32[]{:S(2)}) collective-permute-start(bf16[512,512]{1,0:T(8,128)(2,1)S(1)} %get-tuple-element.22.right_ref), channel_id=1, source_target_pairs={{0,1},{1,0},{2,3},{3,2},{4,5},{5,4},{6,7},{7,6},{8,9},{9,8},{10,11... | collective-permute-start | bytes 1572872 | tf_op jit(solution)/shard_map/ppermute | solution.py:355
  68.8 6.2 %collective-permute-start.3 = (bf16[512,512]{1,0:T(8,128)(2,1)S(1)}, bf16[512,512]{1,0:T(8,128)(2,1)S(1)}, u32[]{:S(2)}, u32[]{:S(2)}) collective-permute-start(bf16[512,512]{1,0:T(8,128)(2,1)S(1)} %collective-permute-done.1.right_ref), channel_id=1, source_target_pairs={{0,2},{2,0},{1,3},{3,1},{4,6},{6,4},{5,7},{7,5},{8,10},{10,8},{9,1... | collective-permute-start | bytes 1572872 | tf_op jit(solution)/shard_map/ppermute | solution.py:355
